TPU v7x, 32 devices: a whole 2x2x4 slice. The times are simulated.
32 devices in a mesh: dp: 8 (over z, x), mp: 4 (over y, core).
Axes of the slice: x: 2, y: 2, z: 4, core: 2. Of those that a mesh axis runs over, the one named last changes fastest.
Arguments:
- inputs: bfloat16 [16, 512, 768], P('dp', 'mp'), may hold values from -6 to 6
- w_qkv: bfloat16 [3, 768, 768], P(None, 'dp', 'mp'), may hold values from -0.21875 to 0.21875
- w_out: bfloat16 [768, 768], P('mp', 'dp'), may hold values from -1.75 to 1.75
- w_up: bfloat16 [768, 3072], P('dp', 'mp'), may hold values from -0.21875 to 0.21875
- w_down: bfloat16 [3072, 768], P('mp', 'dp'), may hold values from -0.109375 to 0.109375
- unit_bias: bfloat16 [4, 1152], P('mp', 'dp'), may hold values from -3 to 3
- norm_gain: bfloat16 [2, 768], P(None, ('dp', 'mp')), may hold values from 0.25 to 1.75
- norm_bias: bfloat16 [4, 768], P(None, ('dp', 'mp')), may hold values from -3 to 3
- seq_lengths: int32 [16, 4], P('dp'), may hold values from 0 to 512, as said below
- cotangent: bfloat16 [16, 512, 768], P('dp', 'mp'), may hold values from -6 to 6
Outputs:
- outputs: bfloat16 [16, 512, 768], P('dp', 'mp')
- grad_inputs: float32 [16, 512, 768], P('dp', 'mp')
- grad_qkv: float32 [3, 768, 768], P(None, 'dp', 'mp')
- grad_out: float32 [768, 768], P('mp', 'dp')
- grad_up: float32 [768, 3072], P('dp', 'mp')
- grad_down: float32 [3072, 768], P('mp', 'dp')
- grad_unit_bias: float32 [4, 1152], P('mp', 'dp')
- grad_gain: float32 [2, 768], P(None, ('dp', 'mp'))
- grad_bias: float32 [4, 768], P(None, ('dp', 'mp'))
Inputs may be any that keep to these rules, and one draw needn't show every extreme that they name: `seq_lengths`: each row lists the lengths of 4 sequences packed from the first row of a micro-batch of 512 rows, zero for an unused slot; a row's lengths sum to at most 512, and the rows after that sum are padding.
All inputs are finite; a program needn't handle non-finite values.
Results may differ from a plain program's by a relative error of at most 0.02.
Values may be sent and summed in bfloat16 or wider, within the bound.
No kernel may reach another device: no remote copies, remote signals or barrier semaphores. Data moves between devices by JAX's collectives and lax.ppermute only.
A program may use at most 128 MiB of HBM per device.

v0:
```python
import jax
import jax.numpy as jnp
from jax import lax
from jax.sharding import PartitionSpec as P

HD = 64


def segment_ids(lengths, total_rows):
    bounds = jnp.cumsum(lengths, dtype=jnp.int32)
    places = jnp.arange(total_rows, dtype=jnp.int32)
    return jnp.sum((places[:, None] >= bounds[None, :]).astype(jnp.int32), axis=1, dtype=jnp.int32)


def layer_norm(values, scales, offsets):
    average = jnp.mean(values, axis=-1, keepdims=True)
    centred = values - average
    spread = jnp.mean(centred * centred, axis=-1, keepdims=True)
    return centred * lax.rsqrt(spread + 1e-06) * scales + offsets


def gelu_exact(values):
    return jax.nn.gelu(values, approximate=False)


def collect_weights(shards, vectors):
    full_weights = (
        lax.all_gather(shards[0], "dp", axis=1, tiled=True),
        lax.all_gather(shards[1], "dp", axis=1, tiled=True),
        lax.all_gather(shards[2], "dp", axis=0, tiled=True),
        lax.all_gather(shards[3], "dp", axis=1, tiled=True),
        lax.all_gather(shards[4], "dp", axis=1, tiled=True),
    )
    vector_full = (
        lax.all_gather(vectors[0], ("dp", "mp"), axis=1, tiled=True),
        lax.all_gather(vectors[1], ("dp", "mp"), axis=1, tiled=True),
    )
    return (full_weights, vector_full)


def reduce_grads(big_terms, small_terms):
    big_owned = (
        lax.psum_scatter(big_terms[0], "dp", scatter_dimension=1, tiled=True),
        lax.psum_scatter(big_terms[1], "dp", scatter_dimension=1, tiled=True),
        lax.psum_scatter(big_terms[2], "dp", scatter_dimension=0, tiled=True),
        lax.psum_scatter(big_terms[3], "dp", scatter_dimension=1, tiled=True),
        lax.psum_scatter(big_terms[4], "dp", scatter_dimension=1, tiled=True),
    )
    small_owned = (
        lax.psum_scatter(small_terms[0], ("dp", "mp"), scatter_dimension=1, tiled=True),
        lax.psum_scatter(small_terms[1], ("dp", "mp"), scatter_dimension=1, tiled=True),
    )
    return (big_owned, small_owned)


def forward_pass(full_weights, vector_full, rows_in, lengths):
    w_qkv, w_out, w_up, w_down, unit_row = full_weights
    gains = vector_full[0].astype(jnp.float32)
    offsets = vector_full[1].astype(jnp.float32)
    head_cols = w_qkv.shape[2]
    head_count = head_cols // HD
    unit_values = unit_row[0].astype(jnp.float32)
    q_bias = unit_values[:head_cols]
    v_bias = unit_values[head_cols : 2 * head_cols]
    up_bias = unit_values[2 * head_cols :]
    score_scale = HD ** (-0.5)
    whole_rows = lax.all_gather(rows_in, "mp", axis=0, tiled=True)
    group_rows = whole_rows.shape[0]
    labels = segment_ids(lengths, group_rows)
    allowed = labels[:, None] == labels[None, :]
    projected = jnp.einsum("rd,tde->tre", whole_rows, w_qkv, preferred_element_type=jnp.float32)
    bias_stack = jnp.stack([q_bias, jnp.zeros_like(q_bias), v_bias])[:, None, :]
    heads_qkv = (projected + bias_stack).astype(jnp.bfloat16).reshape(3, group_rows, head_count, HD)
    scores = (
        jnp.einsum("qhe,khe->hqk", heads_qkv[0], heads_qkv[1], preferred_element_type=jnp.float32)
        * score_scale
    )
    scores = jnp.where(allowed[None], scores, -1000000000.0)
    row_peak = jnp.max(scores, axis=-1, keepdims=True)
    exponent = jnp.exp(scores - row_peak)
    row_total = jnp.sum(exponent, axis=-1, keepdims=True)
    probabilities = exponent / row_total
    log_total = row_peak + jnp.log(row_total)
    probs_low = probabilities.astype(jnp.bfloat16)
    context = jnp.einsum(
        "hqk,khe->qhe", probs_low, heads_qkv[2], preferred_element_type=jnp.float32
    )
    context = context.reshape(group_rows, head_cols).astype(jnp.bfloat16)
    selected = context
    attended = lax.psum_scatter(
        jnp.dot(selected, w_out, preferred_element_type=jnp.float32).astype(jnp.bfloat16),
        "mp",
        scatter_dimension=0,
        tiled=True,
    ).astype(jnp.float32)
    first_in = rows_in.astype(jnp.float32) + attended + offsets[0]
    normed_first = layer_norm(first_in, gains[0], offsets[1])
    whole_first = lax.all_gather(normed_first.astype(jnp.bfloat16), "mp", axis=0, tiled=True)
    hidden = jnp.dot(whole_first, w_up, preferred_element_type=jnp.float32) + up_bias
    activated = gelu_exact(hidden).astype(jnp.bfloat16)
    selected = activated
    mlp_rows = lax.psum_scatter(
        jnp.dot(selected, w_down, preferred_element_type=jnp.float32).astype(jnp.bfloat16),
        "mp",
        scatter_dimension=0,
        tiled=True,
    ).astype(jnp.float32)
    second_in = normed_first + mlp_rows + offsets[2]
    result = layer_norm(second_in, gains[1], offsets[3]).astype(jnp.bfloat16)
    stored = (
        whole_rows,
        allowed,
        heads_qkv,
        log_total,
        context,
        first_in,
        whole_first,
        hidden,
        activated,
        second_in,
    )
    return (result, stored)


def backward_pass(full_weights, vector_full, stored, grad_rows):
    w_qkv, w_out, w_up, w_down, unit_row = full_weights
    gains = vector_full[0].astype(jnp.float32)
    offsets = vector_full[1].astype(jnp.float32)
    (
        whole_rows,
        allowed,
        heads_qkv,
        log_total,
        context,
        first_in,
        whole_first,
        hidden,
        activated,
        second_in,
    ) = stored
    group_rows = whole_rows.shape[0]
    head_cols = w_qkv.shape[2]
    head_count = head_cols // HD
    score_scale = HD ** (-0.5)
    second_out, second_back = jax.vjp(layer_norm, second_in, gains[1], offsets[3])
    d_second, d_gain_two, d_offset_three = second_back(grad_rows.astype(jnp.float32))
    d_mixed = lax.all_gather(d_second.astype(jnp.bfloat16), "mp", axis=0, tiled=True)
    grad_down = jnp.einsum("rf,rd->fd", activated, d_mixed, preferred_element_type=jnp.float32)
    d_activated = jnp.einsum("rd,fd->rf", d_mixed, w_down, preferred_element_type=jnp.float32)
    gelu_out, gelu_back = jax.vjp(gelu_exact, hidden)
    d_hidden = gelu_back(d_activated)[0].astype(jnp.bfloat16)
    grad_up = jnp.einsum("rd,rf->df", whole_first, d_hidden, preferred_element_type=jnp.float32)
    grad_up_bias = jnp.sum(d_hidden, axis=0, dtype=jnp.float32)
    selected = d_hidden
    d_first = d_second + lax.psum_scatter(
        jnp.einsum("rf,df->rd", selected, w_up, preferred_element_type=jnp.float32).astype(
            jnp.bfloat16
        ),
        "mp",
        scatter_dimension=0,
        tiled=True,
    ).astype(jnp.float32)
    first_out, first_back = jax.vjp(layer_norm, first_in, gains[0], offsets[1])
    d_first_in, d_gain_one, d_offset_one = first_back(d_first)
    d_attended = lax.all_gather(d_first_in.astype(jnp.bfloat16), "mp", axis=0, tiled=True)
    grad_out = jnp.einsum("rc,rd->cd", context, d_attended, preferred_element_type=jnp.float32)
    d_context = jnp.einsum("rd,cd->rc", d_attended, w_out, preferred_element_type=jnp.float32)
    d_context = d_context.astype(jnp.bfloat16).reshape(group_rows, head_count, HD)
    scores = (
        jnp.einsum("qhe,khe->hqk", heads_qkv[0], heads_qkv[1], preferred_element_type=jnp.float32)
        * score_scale
    )
    scores = jnp.where(allowed[None], scores, -1000000000.0)
    probabilities = jnp.exp(scores - log_total)
    probs_low = probabilities.astype(jnp.bfloat16)
    d_probs = jnp.einsum(
        "qhe,khe->hqk", d_context, heads_qkv[2], preferred_element_type=jnp.float32
    )
    d_values = jnp.einsum("hqk,qhe->khe", probs_low, d_context, preferred_element_type=jnp.float32)
    inner_sum = jnp.sum(d_probs * probabilities, axis=-1, keepdims=True)
    d_scores = (probabilities * (d_probs - inner_sum)).astype(jnp.bfloat16)
    d_queries = (
        jnp.einsum("hqk,khe->qhe", d_scores, heads_qkv[1], preferred_element_type=jnp.float32)
        * score_scale
    )
    d_keys = (
        jnp.einsum("hqk,qhe->khe", d_scores, heads_qkv[0], preferred_element_type=jnp.float32)
        * score_scale
    )
    d_qkv = (
        jnp.stack([d_queries, d_keys, d_values])
        .reshape(3, group_rows, head_cols)
        .astype(jnp.bfloat16)
    )
    grad_qkv = jnp.einsum("rd,tre->tde", whole_rows, d_qkv, preferred_element_type=jnp.float32)
    grad_q_bias = jnp.sum(d_qkv[0], axis=0, dtype=jnp.float32)
    grad_v_bias = jnp.sum(d_qkv[2], axis=0, dtype=jnp.float32)
    selected = d_qkv
    grad_in = d_first_in + lax.psum_scatter(
        jnp.einsum("tre,tde->rd", selected, w_qkv, preferred_element_type=jnp.float32).astype(
            jnp.bfloat16
        ),
        "mp",
        scatter_dimension=0,
        tiled=True,
    ).astype(jnp.float32)
    grad_unit = jnp.concatenate([grad_q_bias, grad_v_bias, grad_up_bias])[None, :]
    grad_gains = jnp.stack([d_gain_one, d_gain_two])
    grad_offsets = jnp.stack(
        [jnp.sum(d_first_in, axis=0), d_offset_one, jnp.sum(d_second, axis=0), d_offset_three]
    )
    return (
        grad_in,
        (grad_qkv, grad_out, grad_up, grad_down, grad_unit),
        (grad_gains, grad_offsets),
    )


def body(
    inputs, w_qkv, w_out, w_up, w_down, unit_bias, norm_gain, norm_bias, seq_lengths, cotangent
):
    shards = (w_qkv, w_out, w_up, w_down, unit_bias)
    vectors = (norm_gain, norm_bias)
    groups = lax.axis_size("dp")
    model_width = inputs.shape[2]
    big_shapes = (
        (w_qkv.shape[0], w_qkv.shape[1] * groups, w_qkv.shape[2]),
        (w_out.shape[0], w_out.shape[1] * groups),
        (w_up.shape[0] * groups, w_up.shape[1]),
        (w_down.shape[0], w_down.shape[1] * groups),
        (unit_bias.shape[0], unit_bias.shape[1] * groups),
    )
    small_shapes = ((norm_gain.shape[0], model_width), (norm_bias.shape[0], model_width))
    big_start = tuple((jnp.zeros(member, jnp.float32) for member in big_shapes))
    small_start = tuple((jnp.zeros(member, jnp.float32) for member in small_shapes))

    def micro_step(position, state_now):
        big_total, small_total, result_rows, grad_inputs = state_now
        rows_in = lax.dynamic_index_in_dim(inputs, position, 0, keepdims=False)
        lengths = lax.dynamic_index_in_dim(seq_lengths, position, 0, keepdims=False)
        grad_rows = lax.dynamic_index_in_dim(cotangent, position, 0, keepdims=False)
        full_weights, vector_full = collect_weights(shards, vectors)
        result, stored = forward_pass(full_weights, vector_full, rows_in, lengths)
        again_shards, again_vectors, stored = lax.optimization_barrier((shards, vectors, stored))
        back_weights, back_vectors = collect_weights(again_shards, again_vectors)
        grad_in, big_terms, small_terms = backward_pass(
            back_weights, back_vectors, stored, grad_rows
        )
        big_total = jax.tree.map(jnp.add, big_total, big_terms)
        small_total = jax.tree.map(jnp.add, small_total, small_terms)
        result_rows = lax.dynamic_update_index_in_dim(result_rows, result, position, 0)
        grad_inputs = lax.dynamic_update_index_in_dim(grad_inputs, grad_in, position, 0)
        return (big_total, small_total, result_rows, grad_inputs)

    start_state = (
        big_start,
        small_start,
        jnp.zeros(inputs.shape, jnp.bfloat16),
        jnp.zeros(inputs.shape, jnp.float32),
    )
    big_total, small_total, result_rows, grad_inputs = lax.fori_loop(
        0, inputs.shape[0], micro_step, start_state
    )
    big_total, small_total = reduce_grads(big_total, small_total)
    return (
        result_rows,
        grad_inputs,
        big_total[0],
        big_total[1],
        big_total[2],
        big_total[3],
        big_total[4],
        small_total[0],
        small_total[1],
    )


def solution(mesh):
    placed = (
        P("dp", "mp", None),
        P(None, "dp", "mp"),
        P("mp", "dp"),
        P("dp", "mp"),
        P("mp", "dp"),
        P("mp", "dp"),
        P(None, ("dp", "mp")),
        P(None, ("dp", "mp")),
        P("dp", None),
        P("dp", "mp", None),
    )
    return jax.shard_map(
        body,
        mesh=mesh,
        in_specs=placed,
        out_specs=(
            P("dp", "mp", None),
            P("dp", "mp", None),
            P(None, "dp", "mp"),
            P("mp", "dp"),
            P("dp", "mp"),
            P("mp", "dp"),
            P("mp", "dp"),
            P(None, ("dp", "mp")),
            P(None, ("dp", "mp")),
        ),
        check_vma=False,
    )
```

profile of v0, /device:TPU:0, one launch (start us, length us, event | category | flops | bytes accessed | tf_op | source)
XLA Modules:
  0.0 1243.9 jit_solution(15172153917116789738)
XLA Ops:
  9.6 879.3 %while.30 = (s32[]{:T(128)}, f32[3,768,192]{1,2,0:T(8,128)}, f32[192,768]{1,0:T(8,128)}, f32[768,768]{1,0:T(8,128)}, f32[768,768]{1,0:T(8,128)}, /*index=5*/f32[...) while((s32[]{:T(128)}, f32[3,768,192]{1,2,0:T(8,128)}, ...), condition=%wide.region_31.32_spmd.clone, body=%wide.region_0.31_spmd.clone.sunk | while | flops 6229220352 | bytes 207543120 | solution.py:261
  13.4 23.1 %all-reduce.6 = bf16[1152]{0:T(1024)(128)(2,1)S(1)} all-reduce(bf16[1152]{0:T(1024)(128)(2,1)S(1)} %dynamic-update-slice.3), channel_id=1, replica_groups=mesh['dp'=8,'mp'=4] {'dp'}, use_global_device_ids=true, to_apply=%add | all-reduce | flops 1152 | bytes 4608 | tf_op jit(solution)/shard_map/while
  38.8 33.3 %all_gather.135 = bf16[192,768]{0,1:T(8,128)(2,1)} all-gather(bf16[192,96]{0,1:T(8,128)(2,1)} %get-tuple-element.827), channel_id=1, replica_groups=mesh['dp'=8,'mp'=4] {'dp'}, dimensions={1}, use_global_device_ids=true | all-gather | bytes 331776 | tf_op jit(solution)/shard_map/while/body/eval_jaxpr/all_gather | solution.py:29
  80.8 36.8 %all_gather.134 = bf16[3,768,192]{2,0,1:T(4,128)(2,1)S(1)} all-gather(bf16[3,96,192]{2,0,1:T(4,128)(2,1)S(1)} %copy.97), channel_id=1, replica_groups=mesh['dp'=8,'mp'=4] {'dp'}, dimensions={1}, use_global_device_ids=true | all-gather | bytes 995328 | tf_op jit(solution)/shard_map/while/body/eval_jaxpr/all_gather | solution.py:28
  124.8 38.7 %all-gather.14 = bf16[32,24,2]{1,2,0:T(2,128)(2,1)S(1)} all-gather(bf16[1,24,2]{1,2,0:T(2,128)(2,1)S(1)} %bitcast.296), channel_id=1, replica_groups=mesh['dp'=8,'mp'=4] {'dp','mp'}, dimensions={0}, use_global_device_ids=true | all-gather | bytes 3168 | tf_op jit(solution)/shard_map/while/body/eval_jaxpr/all_gather | solution.py:35
  163.7 36.7 %all-gather.13 = bf16[32,24,4]{1,2,0:T(4,128)(2,1)S(1)} all-gather(bf16[1,24,4]{1,2,0:T(4,128)(2,1)S(1)} %bitcast.298), channel_id=1, replica_groups=mesh['dp'=8,'mp'=4] {'dp','mp'}, dimensions={0}, use_global_device_ids=true | all-gather | bytes 6336 | tf_op jit(solution)/shard_map/while/body/eval_jaxpr/all_gather | solution.py:36
  243.3 40.4 %all-gather.15 = bf16[32,24,2]{1,2,0:T(2,128)(2,1)S(1)} all-gather(bf16[1,24,2]{1,2,0:T(2,128)(2,1)S(1)} %bitcast.297), channel_id=1, replica_groups=mesh['dp'=8,'mp'=4] {'dp','mp'}, dimensions={0}, use_global_device_ids=true | all-gather | bytes 3168 | tf_op jit(solution)/shard_map/while/body/eval_jaxpr/all_gather | solution.py:35
  301.8 24.9 %all-gather.27.cloned.1.call-done = bf16[768,768]{1,0:T(8,128)(2,1)} async-done(((bf16[96,768]{1,0:T(8,128)(2,1)}), bf16[768,768]{1,0:T(8,128)(2,1)}) %all-gather.27.cloned.1.call-update) | async-done | bytes 1179664 | tf_op jit(solution)/shard_map/while/body/eval_jaxpr/all_gather | solution.py:30
  329.8 33.5 %all_gather.143 = bf16[192,768]{0,1:T(8,128)(2,1)} all-gather(bf16[192,96]{0,1:T(8,128)(2,1)} %get-tuple-element.827), channel_id=1, replica_groups=mesh['dp'=8,'mp'=4] {'dp'}, dimensions={1}, use_global_device_ids=true | all-gather | bytes 331776 | tf_op jit(solution)/shard_map/while/body/eval_jaxpr/all_gather | solution.py:29
  367.8 35.2 %all_gather.144 = bf16[3,768,192]{2,1,0:T(8,128)(2,1)} all-gather(bf16[3,96,192]{2,1,0:T(8,128)(2,1)S(1)} %copy-done.28), channel_id=1, replica_groups=mesh['dp'=8,'mp'=4] {'dp'}, dimensions={1}, use_global_device_ids=true | all-gather | bytes 995328 | tf_op jit(solution)/shard_map/while/body/eval_jaxpr/all_gather | solution.py:28
  451.7 21.4 %all-reduce.6 = bf16[1152]{0:T(1024)(128)(2,1)S(1)} all-reduce(bf16[1152]{0:T(1024)(128)(2,1)S(1)} %dynamic-update-slice.3), channel_id=1, replica_groups=mesh['dp'=8,'mp'=4] {'dp'}, use_global_device_ids=true, to_apply=%add | all-reduce | flops 1152 | bytes 4608 | tf_op jit(solution)/shard_map/while
  475.3 33.3 %all_gather.135 = bf16[192,768]{0,1:T(8,128)(2,1)} all-gather(bf16[192,96]{0,1:T(8,128)(2,1)} %get-tuple-element.827), channel_id=1, replica_groups=mesh['dp'=8,'mp'=4] {'dp'}, dimensions={1}, use_global_device_ids=true | all-gather | bytes 331776 | tf_op jit(solution)/shard_map/while/body/eval_jaxpr/all_gather | solution.py:29
  516.3 37.8 %all_gather.134 = bf16[3,768,192]{2,0,1:T(4,128)(2,1)S(1)} all-gather(bf16[3,96,192]{2,0,1:T(4,128)(2,1)S(1)} %copy.97), channel_id=1, replica_groups=mesh['dp'=8,'mp'=4] {'dp'}, dimensions={1}, use_global_device_ids=true | all-gather | bytes 995328 | tf_op jit(solution)/shard_map/while/body/eval_jaxpr/all_gather | solution.py:28
  561.6 39.6 %all-gather.14 = bf16[32,24,2]{1,2,0:T(2,128)(2,1)S(1)} all-gather(bf16[1,24,2]{1,2,0:T(2,128)(2,1)S(1)} %bitcast.296), channel_id=1, replica_groups=mesh['dp'=8,'mp'=4] {'dp','mp'}, dimensions={0}, use_global_device_ids=true | all-gather | bytes 3168 | tf_op jit(solution)/shard_map/while/body/eval_jaxpr/all_gather | solution.py:35
  601.5 36.7 %all-gather.13 = bf16[32,24,4]{1,2,0:T(4,128)(2,1)S(1)} all-gather(bf16[1,24,4]{1,2,0:T(4,128)(2,1)S(1)} %bitcast.298), channel_id=1, replica_groups=mesh['dp'=8,'mp'=4] {'dp','mp'}, dimensions={0}, use_global_device_ids=true | all-gather | bytes 6336 | tf_op jit(solution)/shard_map/while/body/eval_jaxpr/all_gather | solution.py:36
  681.1 40.4 %all-gather.15 = bf16[32,24,2]{1,2,0:T(2,128)(2,1)S(1)} all-gather(bf16[1,24,2]{1,2,0:T(2,128)(2,1)S(1)} %bitcast.297), channel_id=1, replica_groups=mesh['dp'=8,'mp'=4] {'dp','mp'}, dimensions={0}, use_global_device_ids=true | all-gather | bytes 3168 | tf_op jit(solution)/shard_map/while/body/eval_jaxpr/all_gather | solution.py:35
  739.6 24.8 %all-gather.27.cloned.1.call-done = bf16[768,768]{1,0:T(8,128)(2,1)} async-done(((bf16[96,768]{1,0:T(8,128)(2,1)}), bf16[768,768]{1,0:T(8,128)(2,1)}) %all-gather.27.cloned.1.call-update) | async-done | bytes 1179664 | tf_op jit(solution)/shard_map/while/body/eval_jaxpr/all_gather | solution.py:30
  767.5 33.4 %all_gather.143 = bf16[192,768]{0,1:T(8,128)(2,1)} all-gather(bf16[192,96]{0,1:T(8,128)(2,1)} %get-tuple-element.827), channel_id=1, replica_groups=mesh['dp'=8,'mp'=4] {'dp'}, dimensions={1}, use_global_device_ids=true | all-gather | bytes 331776 | tf_op jit(solution)/shard_map/while/body/eval_jaxpr/all_gather | solution.py:29
  807.1 35.1 %all_gather.144 = bf16[3,768,192]{2,1,0:T(8,128)(2,1)} all-gather(bf16[3,96,192]{2,1,0:T(8,128)(2,1)S(1)} %copy-done.28), channel_id=1, replica_groups=mesh['dp'=8,'mp'=4] {'dp'}, dimensions={1}, use_global_device_ids=true | all-gather | bytes 995328 | tf_op jit(solution)/shard_map/while/body/eval_jaxpr/all_gather | solution.py:28
  898.6 39.8 %all-reduce.4 = (f32[2,768]{1,0:T(2,128)S(1)}, f32[4,768]{1,0:T(4,128)S(1)}) all-reduce(f32[2,768]{1,0:T(2,128)S(1)} %copy-done.31, f32[4,768]{1,0:T(4,128)S(1)} %copy-done.30), channel_id=12, replica_groups=mesh['dp'=8,'mp'=4] {'dp','mp'}, use_global_device_ids=true, to_apply=%region_37.38.clone | all-reduce | flops 4608 | bytes 36864
  956.7 63.6 %reduce-scatter.22.cloned.1.call-done = f32[96,192]{1,0:T(8,128)} async-done(((f32[768,192]{1,0:T(8,128)}), f32[96,192]{1,0:T(8,128)}) %reduce-scatter.22.cloned.1.call-update) | async-done | bytes 73744
  1021.9 70.4 %reduce-scatter.16.cloned.1.call-done = f32[3,96,192]{2,1,0:T(8,128)} async-done(((f32[3,768,192]{2,1,0:T(8,128)}), f32[3,96,192]{2,1,0:T(8,128)}) %reduce-scatter.16.cloned.1.call-update) | async-done | bytes 221200 | tf_op jit(solution)/shard_map/reduce_scatter | solution.py:43
  1092.3 72.4 %reduce-scatter.18.cloned.1.call-done = f32[96,768]{1,0:T(8,128)} async-done(((f32[768,768]{1,0:T(8,128)}), f32[96,768]{1,0:T(8,128)}) %reduce-scatter.18.cloned.1.call-update) | async-done | bytes 294928 | tf_op jit(solution)/shard_map/reduce_scatter | solution.py:45
  1164.7 72.2 %reduce-scatter.20.cloned.1.call-done = f32[768,96]{0,1:T(8,128)} async-done(((f32[768,768]{0,1:T(8,128)}), f32[768,96]{0,1:T(8,128)}) %reduce-scatter.20.cloned.1.call-update) | async-done | bytes 294928 | tf_op jit(solution)/shard_map/reduce_scatter | solution.py:46
  (435 shorter events, 302.5 us)
Async XLA Ops:
  9.6 191.1 %reduce-scatter.26.cloned.1.call-start = ((), (), s32[]{:S(2)}) async-start(), calls=%async_computation.14 | async-start | bytes 983040 | tf_op jit(solution)/shard_map/while/body/eval_jaxpr/reduce_scatter | solution.py:90
  38.8 82.2 %copy-start.15 = (pred[512,512]{0,1:T(8,128)(4,1)}, pred[512,512]{0,1:T(8,128)(4,1)S(1)}, u32[]{:S(2)}) copy-start(pred[512,512]{0,1:T(8,128)(4,1)S(1)} %broadcast_compare_fusion.2) | copy-start | bytes 786436 | tf_op jit(solution)/shard_map/while
  123.5 87.7 %all-gather.21.cloned.1.call-start = ((), (), s32[]{:S(2)}) async-start(), calls=%async_computation.15 | async-start | bytes 1327104 | tf_op jit(solution)/shard_map/while/body/eval_jaxpr/all_gather | solution.py:30
  124.1 93.5 %all-gather.23.cloned.1.call-start = ((), (), s32[]{:S(2)}) async-start(), calls=%async_computation.16 | async-start | bytes 1327104 | tf_op jit(solution)/shard_map/while/body/eval_jaxpr/all_gather | solution.py:31
  124.7 117.0 %reduce-scatter.28.cloned.1.call-start = ((), (), s32[]{:S(2)}) async-start(), calls=%async_computation.17 | async-start | bytes 983040 | tf_op jit(solution)/shard_map/while/body/eval_jaxpr/reduce_scatter | solution.py:102
  220.8 74.3 %all-gather.25.cloned.1.call-start = ((), (), s32[]{:S(2)}) async-start(), calls=%async_computation.18 | async-start | bytes 1327104 | tf_op jit(solution)/shard_map/while/body/eval_jaxpr/all_gather | solution.py:31
  242.9 83.9 %all-gather.27.cloned.1.call-start = ((), (), s32[]{:S(2)}) async-start(), calls=%async_computation.19 | async-start | bytes 1327104 | tf_op jit(solution)/shard_map/while/body/eval_jaxpr/all_gather | solution.py:30
  285.5 119.7 %reduce-scatter.30.cloned.1.call-start = ((), (), s32[]{:S(2)}) async-start(), calls=%async_computation.20 | async-start | bytes 983040 | tf_op jit(solution)/shard_map/while/body/eval_jaxpr/reduce_scatter | solution.py:155
  329.8 116.3 %reduce-scatter.32.cloned.1.call-start = ((), (), s32[]{:S(2)}) async-start(), calls=%async_computation.21 | async-start | bytes 983040 | tf_op jit(solution)/shard_map/while/body/eval_jaxpr/reduce_scatter | solution.py:199
  447.8 190.7 %reduce-scatter.26.cloned.1.call-start = ((), (), s32[]{:S(2)}) async-start(), calls=%async_computation.14 | async-start | bytes 983040 | tf_op jit(solution)/shard_map/while/body/eval_jaxpr/reduce_scatter | solution.py:90
  475.3 82.2 %copy-start.15 = (pred[512,512]{0,1:T(8,128)(4,1)}, pred[512,512]{0,1:T(8,128)(4,1)S(1)}, u32[]{:S(2)}) copy-start(pred[512,512]{0,1:T(8,128)(4,1)S(1)} %broadcast_compare_fusion.2) | copy-start | bytes 786436 | tf_op jit(solution)/shard_map/while
  558.6 81.0 %copy-start.27 = (bf16[3,64,512]{2,1,0:T(8,128)(2,1)}, bf16[3,64,512]{2,1,0:T(8,128)(2,1)S(1)}, u32[]{:S(2)}) copy-start(bf16[3,64,512]{2,1,0:T(8,128)(2,1)S(1)} %fusion.199) | copy-start | bytes 589828 | tf_op jit(solution)/shard_map/while
  560.0 88.9 %all-gather.21.cloned.1.call-start = ((), (), s32[]{:S(2)}) async-start(), calls=%async_computation.15 | async-start | bytes 1327104 | tf_op jit(solution)/shard_map/while/body/eval_jaxpr/all_gather | solution.py:30
  560.8 94.5 %all-gather.23.cloned.1.call-start = ((), (), s32[]{:S(2)}) async-start(), calls=%async_computation.16 | async-start | bytes 1327104 | tf_op jit(solution)/shard_map/while/body/eval_jaxpr/all_gather | solution.py:31
  561.5 117.9 %reduce-scatter.28.cloned.1.call-start = ((), (), s32[]{:S(2)}) async-start(), calls=%async_computation.17 | async-start | bytes 983040 | tf_op jit(solution)/shard_map/while/body/eval_jaxpr/reduce_scatter | solution.py:102
  658.6 74.3 %all-gather.25.cloned.1.call-start = ((), (), s32[]{:S(2)}) async-start(), calls=%async_computation.18 | async-start | bytes 1327104 | tf_op jit(solution)/shard_map/while/body/eval_jaxpr/all_gather | solution.py:31
  680.6 83.7 %all-gather.27.cloned.1.call-start = ((), (), s32[]{:S(2)}) async-start(), calls=%async_computation.19 | async-start | bytes 1327104 | tf_op jit(solution)/shard_map/while/body/eval_jaxpr/all_gather | solution.py:30
  723.3 122.8 %reduce-scatter.30.cloned.1.call-start = ((), (), s32[]{:S(2)}) async-start(), calls=%async_computation.20 | async-start | bytes 983040 | tf_op jit(solution)/shard_map/while/body/eval_jaxpr/reduce_scatter | solution.py:155
  767.4 119.7 %reduce-scatter.32.cloned.1.call-start = ((), (), s32[]{:S(2)}) async-start(), calls=%async_computation.21 | async-start | bytes 983040 | tf_op jit(solution)/shard_map/while/body/eval_jaxpr/reduce_scatter | solution.py:199
  888.9 66.2 %reduce-scatter.24.cloned.1.call-start = ((), (), s32[]{:S(2)}) async-start(), calls=%async_computation.13 | async-start | bytes 663552
  890.9 129.4 %reduce-scatter.22.cloned.1.call-start = ((), (), s32[]{:S(2)}) async-start(), calls=%async_computation.12 | async-start | bytes 884736
  892.1 200.1 %reduce-scatter.16.cloned.1.call-start = ((), (), s32[]{:S(2)}) async-start(), calls=%async_computation.9 | async-start | bytes 2654208 | tf_op jit(solution)/shard_map/reduce_scatter | solution.py:43
  894.2 270.4 %reduce-scatter.18.cloned.1.call-start = ((), (), s32[]{:S(2)}) async-start(), calls=%async_computation.10 | async-start | bytes 2654208 | tf_op jit(solution)/shard_map/reduce_scatter | solution.py:45
  894.8 342.0 %reduce-scatter.20.cloned.1.call-start = ((), (), s32[]{:S(2)}) async-start(), calls=%async_computation.11 | async-start | bytes 2654208 | tf_op jit(solution)/shard_map/reduce_scatter | solution.py:46
  (79 other events, 1115.8 us)
Sparse Core Ops, SparseCore 0:
  123.6 21.6 reduce-scatter.25
  221.0 20.6 reduce-scatter.27
  329.9 21.7 reduce-scatter.29
  425.5 20.4 reduce-scatter.31
  560.1 22.5 reduce-scatter.25
  658.7 20.6 reduce-scatter.27
  767.5 21.7 reduce-scatter.29
  866.4 20.6 reduce-scatter.31
  893.0 62.0 reduce-scatter.23
  958.6 61.6 reduce-scatter.21
  1024.4 67.8 reduce-scatter.15
  1096.2 68.3 reduce-scatter.17
  1168.7 68.0 reduce-scatter.19
Sparse Core Ops, SparseCore 1:
  126.4 39.7 all-gather.20
  168.4 40.0 all-gather.22
  242.9 41.6 all-gather.24
  286.8 39.9 all-gather.26
  563.2 40.7 all-gather.20
  606.5 39.9 all-gather.22
  680.7 41.2 all-gather.24
  724.1 40.3 all-gather.26
where the time goes:
time: 1250 us; the launch traced here: 1240 us
  blocking collectives  664 us (53%)
  waiting for transfers between devices  405 us (32%)
  matrix products  80.4 us (6%)
  local copies, waits for them, and re-layouts  39.1 us (3%)
  other arithmetic  36.7 us (3%)
  between operations  15.3 us (1%)
    all_gather x4, blocking collectives, collect_weights(): lax.all_gather(vectors[0], ('dp', 'mp'), axis=1, tiled=True)  159 us
    all_gather x4, blocking collectives, collect_weights(): lax.all_gather(shards[0], 'dp', axis=1, tiled=True)  145 us
    all_gather x4, blocking collectives, collect_weights(): lax.all_gather(shards[1], 'dp', axis=1, tiled=True)  134 us
    unnamed x7, waiting for transfers between devices  79.7 us
    all_gather x2, blocking collectives, collect_weights(): lax.all_gather(vectors[1], ('dp', 'mp'), axis=1, tiled=True)  73.3 us
    reduce_scatter x1, waiting for transfers between devices, reduce_grads(): lax.psum_scatter(big_terms[2], 'dp', scatter_dimension=0, tiled=True)  72.4 us
    reduce_scatter x1, waiting for transfers between devices, reduce_grads(): lax.psum_scatter(big_terms[3], 'dp', scatter_dimension=1, tiled=True)  72.2 us
    reduce_scatter x1, waiting for transfers between devices, reduce_grads(): lax.psum_scatter(big_terms[0], 'dp', scatter_dimension=1, tiled=True)  70.4 us
  transfers between devices with their start and end apart: 21, of which 11 were waited for; matrix products, arithmetic and copies ran while one was open for 7% of the time, Pallas kernels for 0%

commit v1 on v0

v1 whole, which is shorter than its diff:
```python
import jax
import jax.numpy as jnp
from jax import lax
from jax.sharding import PartitionSpec as P

HD = 64
EXTRA = 16
BF = jnp.bfloat16
F32 = jnp.float32


def dot(left, right, dims):
    return lax.dot_general(left, right, (dims, ((), ())), preferred_element_type=F32)


class Place:
    def __init__(self):
        self.groups = lax.axis_size("dp")
        self.line_size = self.groups // 2
        data, model = lax.axis_index("dp"), lax.axis_index("mp")
        self.line, self.pair = data // 2, data % 2
        self.row, self.core = model // 2, model % 2

    def core_swap(self, value):
        return lax.ppermute(value, "mp", [(0, 1), (1, 0), (2, 3), (3, 2)])

    def row_swap(self, value):
        return lax.ppermute(value, "mp", [(0, 2), (2, 0), (1, 3), (3, 1)])

    def line_shift(self, value, step):
        n = self.line_size
        pairs = [(i * 2 + j, ((i + step) % n) * 2 + j) for i in range(n) for j in range(2)]
        return lax.ppermute(value, "dp", pairs)

    def cross(self, value, along_row):
        pairs = []
        for data in range(self.groups):
            for model in range(4):
                if model % 2 == along_row:
                    pairs.append((data * 4 + model, data * 4 + (model ^ 2)))
                else:
                    pairs.append((data * 4 + model, (data ^ 1) * 4 + model))
        return lax.ppermute(value, ("dp", "mp"), pairs)

    def quarters(self):
        other_row, other_pair = 1 - self.row, 1 - self.pair
        swap = self.core == 0
        first = (jnp.where(swap, other_row, self.row), jnp.where(swap, self.pair, other_pair))
        second = (jnp.where(swap, self.row, other_row), jnp.where(swap, other_pair, self.pair))
        return (self.row, self.pair), first, second, (other_row, other_pair)


def gather_group(place, shard):
    n = place.line_size
    parts = [shard] + [place.line_shift(shard, step) for step in range(1, n)]
    own = jnp.stack(parts)
    first = place.cross(own, 0)
    rest = place.cross(jnp.stack([own, first]), 1)
    whole = jnp.zeros((2, n, 2) + shard.shape, shard.dtype)
    for piece, (row, pair) in zip((own, first, rest[0], rest[1]), place.quarters()):
        for step in range(n):
            start = (row, (place.line - step) % n, pair, 0, 0)
            whole = lax.dynamic_update_slice(whole, piece[step][None, None, None], start)
    return whole


def scatter_group(place, terms):
    n = place.line_size

    def quarter(at):
        row, pair = at
        size = (1, n, 1) + terms.shape[3:]
        return lax.dynamic_slice(terms, (row, 0, pair, 0, 0), size).reshape((n,) + terms.shape[3:])

    own, first, second, far = (quarter(at) for at in place.quarters())
    got = place.cross(jnp.stack([first, far]).astype(BF), 0)
    second = second.astype(F32) + got[1].astype(F32)
    got_second = place.cross(second.astype(BF), 1)
    own = own.astype(F32) + got[0].astype(F32) + got_second.astype(F32)
    own_low = own.astype(BF)
    total = lax.dynamic_index_in_dim(own, place.line, 0, keepdims=False)
    for step in range(1, n):
        send = lax.dynamic_index_in_dim(own_low, (place.line + step) % n, 0, keepdims=False)
        total = total + place.line_shift(send, step).astype(F32)
    return total


def norm_parts(values):
    centred = values - jnp.mean(values, axis=-1, keepdims=True)
    rate = lax.rsqrt(jnp.mean(centred * centred, axis=-1, keepdims=True) + 1e-06)
    return centred * rate, rate


def norm_back(grad, unit, rate, scale):
    inner = grad * scale
    return rate * (
        inner
        - jnp.mean(inner, axis=-1, keepdims=True)
        - unit * jnp.mean(inner * unit, axis=-1, keepdims=True)
    )


def body(
    inputs, w_qkv, w_out, w_up, w_down, unit_bias, norm_gain, norm_bias, seq_lengths, cotangent
):
    place = Place()
    n, row, core = place.line_size, place.row, place.core
    groups = place.groups
    block, width = inputs.shape[1], inputs.shape[2]
    rows = 4 * block
    depth, head_cols = w_qkv.shape[1], w_qkv.shape[2]
    units = w_up.shape[1]
    share = unit_bias.shape[1]
    small = norm_gain.shape[1]
    heads = 2 * head_cols // HD
    scale = HD ** (-0.5)

    keep = lambda array, index: lax.dynamic_index_in_dim(array, index, 0, keepdims=False)
    outgoing = jnp.stack([keep(inputs, 1 - row), keep(cotangent, 1 - row)])
    incoming = place.row_swap(outgoing)
    mine = jnp.stack([keep(inputs, row), keep(cotangent, row)])
    low_rows = jnp.where(row == 0, mine, incoming)
    high_rows = jnp.where(row == 0, incoming, mine)
    half = jnp.concatenate([low_rows, high_rows], axis=1)
    other = place.core_swap(half)
    both = jnp.where(
        core == 0,
        jnp.concatenate([half, other], axis=1),
        jnp.concatenate([other, half], axis=1),
    )
    x, grad_rows = both[0], both[1]

    vector = jnp.concatenate([unit_bias[0], norm_gain.reshape(-1), norm_bias.reshape(-1)])
    vector = jnp.pad(vector[None], ((0, EXTRA - 1), (0, width - vector.shape[0])))
    first_shard = jnp.concatenate(
        [w_qkv[0], w_qkv[1], w_qkv[2], jnp.transpose(w_out)], axis=1
    )
    first_whole = gather_group(place, jnp.concatenate([first_shard, vector], axis=0))
    up_whole = gather_group(place, w_up).reshape(2, width, units)
    down_whole = gather_group(place, jnp.transpose(w_down)).reshape(2, width, units)
    attn_whole = first_whole[:, :, :, :depth].reshape(2, width, width)
    vectors = first_whole[:, :, :, depth, : share + 6 * small].reshape(2, groups, -1)
    unit_values = vectors[:, :, :share].reshape(2, groups * share).astype(F32)
    norm_here = vectors[:, :, share:]
    norm_there = place.core_swap(norm_here)
    norm_all = jnp.where(
        core == 0,
        jnp.stack([norm_here, norm_there], axis=2),
        jnp.stack([norm_there, norm_here], axis=2),
    )
    norm_all = norm_all.reshape(2, groups, 2, 6, small)
    norm_all = jnp.transpose(norm_all, (3, 1, 0, 2, 4)).reshape(6, width).astype(F32)
    gains, offsets = norm_all[:2], norm_all[2:]
    q_bias = unit_values[:, :head_cols].reshape(-1)
    v_bias = unit_values[:, head_cols : 2 * head_cols].reshape(-1)
    up_bias = unit_values[:, 2 * head_cols :].reshape(-1)

    lengths = keep(seq_lengths, row)
    bounds = jnp.cumsum(lengths, dtype=jnp.int32)
    ids = jnp.arange(rows, dtype=jnp.int32).reshape(2, 2, block)
    places = jnp.transpose(ids, (1, 0, 2)).reshape(rows)
    labels = jnp.sum((places[:, None] >= bounds[None, :]).astype(jnp.int32), axis=1)
    allowed = labels[:, None] == labels[None, :]

    def columns(index):
        lo = index * head_cols
        return attn_whole[:, :, lo : lo + head_cols]

    def project(index):
        parts = [dot(x, columns(index)[j], ((1,), (0,))) for j in range(2)]
        return jnp.concatenate(parts, axis=1)

    def split(flat):
        return flat.reshape(rows, heads, HD)

    queries = split((project(0) + q_bias).astype(BF))
    keys = split(project(1).astype(BF))
    values = split((project(2) + v_bias).astype(BF))
    scores = jnp.einsum("qhe,khe->hqk", queries, keys, preferred_element_type=F32) * scale
    scores = jnp.where(allowed[None], scores, -1000000000.0)
    peak = jnp.max(scores, axis=-1, keepdims=True)
    exponent = jnp.exp(scores - peak)
    probs = exponent / jnp.sum(exponent, axis=-1, keepdims=True)
    probs_low = probs.astype(BF)
    context = jnp.einsum("hqk,khe->qhe", probs_low, values, preferred_element_type=F32)
    context = context.reshape(rows, 2 * head_cols).astype(BF)
    w_out_t = [columns(3)[j] for j in range(2)]
    attended = dot(context[:, :head_cols], w_out_t[0], ((1,), (1,))) + dot(
        context[:, head_cols:], w_out_t[1], ((1,), (1,))
    )

    def pair_sum(partial):
        low = partial.astype(BF)
        return low.astype(F32) + place.core_swap(low).astype(F32)

    first_in = x.astype(F32) + pair_sum(attended) + offsets[0]
    unit_one, rate_one = norm_parts(first_in)
    normed_first = unit_one * gains[0] + offsets[1]
    first_low = normed_first.astype(BF)
    hidden = jnp.concatenate(
        [dot(first_low, up_whole[j], ((1,), (0,))) for j in range(2)], axis=1
    ) + up_bias
    cdf = 0.5 * lax.erfc(-hidden * (0.5**0.5))
    activated = (hidden * cdf).astype(BF)
    slope = cdf + hidden * jnp.exp(-0.5 * hidden * hidden) * 0.3989422804014327
    down = sum(
        dot(activated[:, j * units : (j + 1) * units], down_whole[j], ((1,), (1,)))
        for j in range(2)
    )
    second_in = normed_first + pair_sum(down) + offsets[2]
    unit_two, rate_two = norm_parts(second_in)
    result = (unit_two * gains[1] + offsets[3]).astype(BF)

    dy = grad_rows.astype(F32)
    d_second = norm_back(dy, unit_two, rate_two, gains[1])
    d_mixed = d_second.astype(BF)

    def outer(left, right):
        return dot(left, right, ((0,), (0,))).astype(BF)

    def shaped(terms):
        return jnp.stack(terms).reshape(2, n, 2, depth, -1)

    down_terms = shaped(
        [outer(d_mixed, activated[:, j * units : (j + 1) * units]) for j in range(2)]
    )
    grad_down = jnp.transpose(scatter_group(place, down_terms))
    d_activated = jnp.concatenate(
        [dot(d_mixed, down_whole[j], ((1,), (0,))) for j in range(2)], axis=1
    )
    d_hidden = (d_activated * slope).astype(BF)
    up_terms = shaped(
        [outer(first_low, d_hidden[:, j * units : (j + 1) * units]) for j in range(2)]
    )
    grad_up = scatter_group(place, up_terms)
    d_up_bias = jnp.sum(d_hidden.astype(F32), axis=0)
    d_normed = sum(
        dot(d_hidden[:, j * units : (j + 1) * units], up_whole[j], ((1,), (1,)))
        for j in range(2)
    )
    d_first = d_second + pair_sum(d_normed)
    d_first_in = norm_back(d_first, unit_one, rate_one, gains[0])
    d_attended = d_first_in.astype(BF)
    d_context = jnp.concatenate(
        [dot(d_attended, w_out_t[j], ((1,), (0,))) for j in range(2)], axis=1
    )
    d_context = split(d_context.astype(BF))
    d_probs = jnp.einsum("qhe,khe->hqk", d_context, values, preferred_element_type=F32)
    d_values = jnp.einsum("hqk,qhe->khe", probs_low, d_context, preferred_element_type=F32)
    inner = jnp.sum(d_probs * probs, axis=-1, keepdims=True)
    d_scores = (probs * (d_probs - inner)).astype(BF)
    d_queries = jnp.einsum("hqk,khe->qhe", d_scores, keys, preferred_element_type=F32) * scale
    d_keys = jnp.einsum("hqk,qhe->khe", d_scores, queries, preferred_element_type=F32) * scale
    flat = lambda array: array.reshape(rows, 2 * head_cols).astype(BF)
    d_queries, d_keys, d_values = flat(d_queries), flat(d_keys), flat(d_values)
    d_parts = []
    for j in range(2):
        cut = slice(j * head_cols, (j + 1) * head_cols)
        d_parts.append(jnp.concatenate([d_queries[:, cut], d_keys[:, cut], d_values[:, cut]], axis=1))
    attn_terms = shaped(
        [
            jnp.concatenate(
                [
                    outer(x, d_parts[j]),
                    outer(d_attended, context[:, j * head_cols : (j + 1) * head_cols]),
                ],
                axis=1,
            )
            for j in range(2)
        ]
    )
    total = lambda array: jnp.sum(array.astype(F32), axis=0)
    unit_terms = jnp.concatenate(
        [
            total(d_queries).reshape(2, head_cols),
            total(d_values).reshape(2, head_cols),
            d_up_bias.reshape(2, units),
        ],
        axis=1,
    ).reshape(2, groups, share)
    norm_terms = jnp.stack(
        [
            total(d_first * unit_one),
            total(dy * unit_two),
            total(d_first_in),
            total(d_first),
            total(d_second),
            total(dy),
        ]
    ).reshape(6, groups, 2, 2, small)
    norm_terms = lax.dynamic_index_in_dim(norm_terms, core, 3, keepdims=False)
    norm_terms = jnp.transpose(norm_terms, (2, 1, 0, 3)).reshape(2, groups, 6 * small)
    vector_terms = jnp.concatenate([unit_terms, norm_terms], axis=2)
    vector_terms = jnp.pad(
        vector_terms[:, :, None],
        ((0, 0), (0, 0), (0, EXTRA - 1), (0, width - vector_terms.shape[2])),
    ).reshape(2, n, 2, EXTRA, width)
    attn_grad = scatter_group(
        place, jnp.concatenate([attn_terms, vector_terms.astype(BF)], axis=3)
    )
    d_inputs = sum(
        dot(d_parts[j], attn_whole[j][:, : 3 * head_cols], ((1,), (1,))) for j in range(2)
    )
    grad_in = d_first_in + pair_sum(d_inputs)

    def hand_back(full):
        mine = lax.dynamic_slice_in_dim(full, core * 2 * block, 2 * block, 0)
        mine = mine.reshape(2, block, width)
        kept = keep(mine, row)
        got = place.row_swap(keep(mine, 1 - row).astype(BF)).astype(full.dtype)
        return jnp.where(row == 0, jnp.stack([kept, got]), jnp.stack([got, kept]))

    grad_qkv = jnp.stack(
        [attn_grad[:depth, t * head_cols : (t + 1) * head_cols] for t in range(3)]
    )
    grad_out = jnp.transpose(attn_grad[:depth, 3 * head_cols :])
    vector_grad = attn_grad[depth]
    norm_grad = vector_grad[share : share + 6 * small].reshape(6, small)
    return (
        hand_back(result),
        hand_back(grad_in),
        grad_qkv,
        grad_out,
        grad_up,
        grad_down,
        vector_grad[None, :share],
        norm_grad[:2],
        norm_grad[2:],
    )


def solution(mesh):
    placed = (
        P("dp", "mp", None),
        P(None, "dp", "mp"),
        P("mp", "dp"),
        P("dp", "mp"),
        P("mp", "dp"),
        P("mp", "dp"),
        P(None, ("dp", "mp")),
        P(None, ("dp", "mp")),
        P("dp", None),
        P("dp", "mp", None),
    )
    return jax.shard_map(
        body,
        mesh=mesh,
        in_specs=placed,
        out_specs=(
            P("dp", "mp", None),
            P("dp", "mp", None),
            P(None, "dp", "mp"),
            P("mp", "dp"),
            P("dp", "mp"),
            P("mp", "dp"),
            P("mp", "dp"),
            P(None, ("dp", "mp")),
            P(None, ("dp", "mp")),
        ),
        check_vma=False,
    )
```

time: 1250 us -> 341 us (0.27)
  blocking collectives: 664 us -> 0 us
  waiting for transfers between devices: 405 us -> 76.8 us
  local copies, waits for them, and re-layouts: 39.1 us -> 103 us
  starting transfers between devices: 0.83 us -> 58 us
  matrix products: 80.4 us -> 51.4 us
  between operations: 15.3 us -> 2.17 us
    all_gather x22 -> x0, blocking collectives: 579 us -> none  [the longest x4 159 us: collect_weights(): lax.all_gather(vectors[0], ('dp', 'mp'), axis=1, tiled=True)]
    reduce_scatter x11 -> x0, waiting for transfers between devices: 273 us -> none  [the longest x1 72.4 us: reduce_grads(): lax.psum_scatter(big_terms[2], 'dp', scatter_dimension=0, tiled=True)]
    unnamed x7 -> x0, waiting for transfers between devices: 79.7 us -> none
    ppermute x0 -> x39, waiting for transfers between devices: none -> 76.8 us  [the longest x12 54.5 us: cross(): return lax.ppermute(value, ('dp', 'mp'), pairs)]
    ppermute x0 -> x39, starting transfers between devices: none -> 58 us  [the longest x18 38.6 us: line_shift(): return lax.ppermute(value, 'dp', pairs)]
    all_gather x8 -> x0, waiting for transfers between devices: 49.8 us -> none  [the longest x4 49.7 us: collect_weights(): lax.all_gather(shards[2], 'dp', axis=0, tiled=True)]
    while x2 -> x0, blocking collectives: 44.5 us -> none
    unnamed x1 -> x0, blocking collectives: 39.8 us -> none
  transfers between devices with their start and end apart: 21 -> 39, of which waited for: 11 -> 11; matrix products, arithmetic and copies ran while one was open for 7% -> 36% of each run, Pallas kernels for 0% -> 0%
where the time goes in v1:
time: 341 us; the launch traced here: 337 us
  local copies, waits for them, and re-layouts  103 us (30%)
  waiting for transfers between devices  76.8 us (23%)
  starting transfers between devices  58 us (17%)
  matrix products  51.4 us (15%)
  other arithmetic  46 us (13%)
    ppermute x12, waiting for transfers between devices, cross(): return lax.ppermute(value, ('dp', 'mp'), pairs)  54.5 us
    ppermute x18, starting transfers between devices, line_shift(): return lax.ppermute(value, 'dp', pairs)  38.6 us
    dot_general x28, matrix products, dot(): lax.dot_general(left, right, (dims, ((), ())), preferred_element_type=F32)  35.9 us
    dynamic_update_slice x46, local copies, waits for them, and re-layouts, gather_group(): lax.dynamic_update_slice(whole, piece[step][None, None, None], start)  25.6 us
    ppermute x18, waiting for transfers between devices, line_shift(): return lax.ppermute(value, 'dp', pairs)  20.7 us
    unnamed x180, local copies, waits for them, and re-layouts  16.9 us
    ppermute x12, starting transfers between devices, cross(): return lax.ppermute(value, ('dp', 'mp'), pairs)  13.1 us
    dot_general x9, local copies, waits for them, and re-layouts, dot(): lax.dot_general(left, right, (dims, ((), ())), preferred_element_type=F32)  10.9 us
  transfers between devices with their start and end apart: 39, of which 11 were waited for; matrix products, arithmetic and copies ran while one was open for 36% of the time, Pallas kernels for 0%

profile of v1, /device:TPU:0, one launch (start us, length us, event | category | flops | bytes accessed | tf_op | source)
XLA Modules:
  0.0 336.9 jit_solution(8509132157210525912)
XLA Ops:
  0.7 4.1 %collective-permute-start.15 = (bf16[96,768]{1,0:T(8,128)(2,1)}, bf16[96,768]{1,0:T(8,128)(2,1)}, u32[]{:S(2)}, u32[]{:S(2)}) collective-permute-start(bf16[96,768]{1,0:T(8,128)(2,1)} %bitcast.547), channel_id=1, source_target_pairs={{0,16},{4,20},{8,24},{12,28},{16,0},{20,4},{24,8},{28,12},{1,17},{... | collective-permute-start | bytes 442376 | tf_op jit(solution)/shard_map/ppermute | solution.py:33
  22.1 3.3 collective-permute-start.11
  29.2 9.9 %collective-permute-start.3 = (bf16[112,768]{1,0:T(8,128)(2,1)}, bf16[112,768]{1,0:T(8,128)(2,1)S(1)}, u32[]{:S(2)}, u32[]{:S(2)}) collective-permute-start(bf16[112,768]{1,0:T(8,128)(2,1)} %get-tuple-element.82), channel_id=1, source_target_pairs={{0,16},{4,20},{8,24},{12,28},{16,0},{20,4},{24,8},{28,12},{1,17},{... | collective-permute-start | bytes 516104 | tf_op jit(solution)/shard_map/ppermute | solution.py:33
  55.2 14.7 %collective-permute-done.17 = bf16[4,96,768]{2,1,0:T(8,128)(2,1)S(1)} collective-permute-done((bf16[4,96,768]{2,1,0:T(8,128)(2,1)S(1)}, bf16[4,96,768]{2,1,0:T(8,128)(2,1)S(1)}, u32[]{:S(2)}, u32[]{:S(2)}) %collective-permute-start.17) | collective-permute-done | bytes 589856 | tf_op jit(solution)/shard_map/ppermute | solution.py:43
  77.7 7.0 %collective-permute-done.5 = bf16[4,112,768]{2,1,0:T(8,128)(2,1)S(1)} collective-permute-done((bf16[4,112,768]{2,1,0:T(8,128)(2,1)S(1)}, bf16[4,112,768]{2,1,0:T(8,128)(2,1)S(1)}, u32[]{:S(2)}, u32[]{:S(2)}) %collective-permute-start.5) | collective-permute-done | bytes 688160 | tf_op jit(solution)/shard_map/ppermute | solution.py:43
  93.0 6.0 %collective-permute-done.13 = bf16[2,4,96,768]{3,2,1,0:T(8,128)(2,1)S(1)} collective-permute-done((bf16[2,4,96,768]{3,2,1,0:T(8,128)(2,1)S(1)}, bf16[2,4,96,768]{3,2,1,0:T(8,128)(2,1)S(1)}, u32[]{:S(2)}, u32[]{:S(2)}) %collective-permute-start.13) | collective-permute-done | bytes 1179680 | tf_op jit(solution)/shard_map/ppermute | solution.py:43
  104.3 9.4 %collective-permute-done.6 = bf16[2,4,112,768]{3,2,1,0:T(8,128)(2,1)S(1)} collective-permute-done((bf16[2,4,112,768]{3,2,1,0:T(8,128)(2,1)S(1)}, bf16[2,4,112,768]{3,2,1,0:T(8,128)(2,1)S(1)}, u32[]{:S(2)}, u32[]{:S(2)}) %collective-permute-start.6) | collective-permute-done | bytes 1376288 | tf_op jit(solution)/shard_map/ppermute | solution.py:43
  117.9 3.8 %slice_bitcast_fusion.13 = (bf16[192,768]{0,1:T(8,128)(2,1)}, bf16[192,768]{0,1:T(8,128)(2,1)}, bf16[192,768]{0,1:T(8,128)(2,1)}, bf16[192,768]{0,1:T(8,128)(2,1...) fusion(bf16[2,768,768]{2,1,0:T(8,128)(2,1)} %bitcast.498), kind=kLoop, calls=%fused_computation.211 | loop fusion | bytes 4718592 | tf_op jit(solution)/shard_map/dot_general | solution.py:13
  131.6 6.2 %fusion.206 = (f32[6,512]{1,0:T(8,128)S(1)}, f32[6,512,512]{1,2,0:T(8,128)}) fusion(pred[512,512]{0,1:T(8,128)(4,1)S(1)} %copy-done.57, bf16[512,6,64]{0,2,1:T(8,128)(2,1)S(1)} %fusion.53, bf16[512,3,64]{0,2,1:T(8,128)(2,1)} %convolution_convert_fusion.10, bf16[512,3,64]{0,2,1:T(8,128)(2,1)} %convolution_convert_fusion.11), kind=kOutput, calls=%fused_computation.410 | convolution fusion | flops 207815168 | bytes 7352320 | tf_op jit(solution)/shard_map/sub | solution.py:182
  137.9 3.5 %fusion.37 = bf16[6,64,512]{2,1,0:T(8,128)(2,1)S(1)} fusion(f32[512,3,64]{0,2,1:T(8,128)S(1)} %copy-done.80, f32[512,3,64]{0,2,1:T(8,128)S(1)} %copy-done.82, f32[6,64]{1,0:T(8,128)S(1)} %copy-done.78, f32[6,512,512]{1,2,0:T(8,128)} %get-tuple-element.150, f32[6,512]{1,0:T(8,128)S(1)} %get-tuple-element.149), kind=kOutput, calls=%fused_computation.102 | convolution fusion | flops 205258752 | bytes 7484928 | tf_op jit(solution)/shard_map/hqk,khe->qhe/dot_general | solution.py:185
  145.8 3.3 fusion.198
  149.3 3.2 fusion.199
  160.0 7.7 %multiply_convert_fusion.1 = (bf16[512,1536]{1,0:T(8,128)(2,1)S(1)}, f32[512,1536]{1,0:T(8,128)}) fusion(f32[512,768]{1,0:T(8,128)S(1)} %fusion.210, f32[512,768]{1,0:T(8,128)S(1)} %fusion.209, f32[1536]{0:T(1024)S(1)} %add.569), kind=kLoop, calls=%fused_computation.33 | loop fusion | flops 52690944 | bytes 7870464 | tf_op jit(solution)/shard_map/convert_element_type | solution.py:204
  177.3 3.2 fusion.197
  214.4 3.0 add_convert_fusion.1
  261.2 2.6 add_convert_fusion
  272.3 11.9 %collective-permute-done.30 = bf16[4,96,768]{2,1,0:T(8,128)(2,1)S(1)} collective-permute-done((bf16[4,96,768]{2,1,0:T(8,128)(2,1)S(1)}, bf16[4,96,768]{2,1,0:T(8,128)(2,1)S(1)}, u32[]{:S(2)}, u32[]{:S(2)}) %collective-permute-start.30) | collective-permute-done | bytes 589856 | tf_op jit(solution)/shard_map/ppermute | solution.py:43
  286.0 3.6 %collective-permute-start.33 = (bf16[96,768]{1,0:T(8,128)(2,1)S(1)}, bf16[96,768]{1,0:T(8,128)(2,1)S(1)}, u32[]{:S(2)}, u32[]{:S(2)}) collective-permute-start(bf16[96,768]{1,0:T(8,128)(2,1)S(1)} %get-tuple-element.114), channel_id=1, source_target_pairs={{0,24},{4,28},{8,0},{12,4},{16,8},{20,12},{24,16},{28,20},{1,25},{... | collective-permute-start | bytes 442376 | tf_op jit(solution)/shard_map/ppermute | solution.py:33
  289.5 5.5 %collective-permute-done.35 = bf16[4,96,768]{2,1,0:T(8,128)(2,1)S(1)} collective-permute-done((bf16[4,96,768]{2,1,0:T(8,128)(2,1)S(1)}, bf16[4,96,768]{2,1,0:T(8,128)(2,1)S(1)}, u32[]{:S(2)}, u32[]{:S(2)}) %collective-permute-start.35) | collective-permute-done | bytes 589856 | tf_op jit(solution)/shard_map/ppermute | solution.py:43
  302.0 3.0 collective-permute-start.38
  305.0 3.7 %collective-permute-done.32 = bf16[96,768]{1,0:T(8,128)(2,1)S(1)} collective-permute-done((bf16[96,768]{1,0:T(8,128)(2,1)S(1)}, bf16[96,768]{1,0:T(8,128)(2,1)S(1)}, u32[]{:S(2)}, u32[]{:S(2)}) %collective-permute-start.32) | collective-permute-done | bytes 147488 | tf_op jit(solution)/shard_map/ppermute | solution.py:33
  310.8 2.9 collective-permute-start.28
  315.6 10.0 %collective-permute-done.37 = bf16[96,768]{1,0:T(8,128)(2,1)S(1)} collective-permute-done((bf16[96,768]{1,0:T(8,128)(2,1)S(1)}, bf16[96,768]{1,0:T(8,128)(2,1)S(1)}, u32[]{:S(2)}, u32[]{:S(2)}) %collective-permute-start.37) | collective-permute-done | bytes 147488 | tf_op jit(solution)/shard_map/ppermute | solution.py:33
  326.4 6.6 %collective-permute-done.27 = bf16[112,768]{1,0:T(8,128)(2,1)S(1)} collective-permute-done((bf16[112,768]{1,0:T(8,128)(2,1)S(1)}, bf16[112,768]{1,0:T(8,128)(2,1)S(1)}, u32[]{:S(2)}, u32[]{:S(2)}) %collective-permute-start.27) | collective-permute-done | bytes 172064 | tf_op jit(solution)/shard_map/ppermute | solution.py:33
  (464 shorter events, 196.7 us)
Async XLA Ops:
  0.7 28.5 %collective-permute-start.15 = (bf16[96,768]{1,0:T(8,128)(2,1)}, bf16[96,768]{1,0:T(8,128)(2,1)}, u32[]{:S(2)}, u32[]{:S(2)}) collective-permute-start(bf16[96,768]{1,0:T(8,128)(2,1)} %bitcast.547), channel_id=1, source_target_pairs={{0,16},{4,20},{8,24},{12,28},{16,0},{20,4},{24,8},{28,12},{1,17},{... | collective-permute-start | bytes 442376 | tf_op jit(solution)/shard_map/ppermute | solution.py:33
  4.8 17.3 %collective-permute-start.14 = (bf16[96,768]{1,0:T(8,128)(2,1)}, bf16[96,768]{1,0:T(8,128)(2,1)}, u32[]{:S(2)}, u32[]{:S(2)}) collective-permute-start(bf16[96,768]{1,0:T(8,128)(2,1)} %bitcast.548), channel_id=1, source_target_pairs={{0,8},{4,12},{8,16},{12,20},{16,24},{20,28},{24,0},{28,4},{1,9},{5... | collective-permute-start | bytes 442376 | tf_op jit(solution)/shard_map/ppermute | solution.py:33
  6.3 41.6 %collective-permute-start.16 = (bf16[96,768]{1,0:T(8,128)(2,1)}, bf16[96,768]{1,0:T(8,128)(2,1)}, u32[]{:S(2)}, u32[]{:S(2)}) collective-permute-start(bf16[96,768]{1,0:T(8,128)(2,1)} %bitcast.549), channel_id=1, source_target_pairs={{0,24},{4,28},{8,0},{12,4},{16,8},{20,12},{24,16},{28,20},{1,25},{... | collective-permute-start | bytes 442376 | tf_op jit(solution)/shard_map/ppermute | solution.py:33
  8.6 32.0 %collective-permute-start.10 = (bf16[96,768]{1,0:T(8,128)(2,1)}, bf16[96,768]{1,0:T(8,128)(2,1)}, u32[]{:S(2)}, u32[]{:S(2)}) collective-permute-start(bf16[96,768]{1,0:T(8,128)(2,1)} %param.13), channel_id=1, source_target_pairs={{0,16},{4,20},{8,24},{12,28},{16,0},{20,4},{24,8},{28,12},{1,17},{... | collective-permute-start | bytes 442376 | tf_op jit(solution)/shard_map/ppermute | solution.py:33
  8.6 18.4 %collective-permute-start.9 = (bf16[96,768]{1,0:T(8,128)(2,1)}, bf16[96,768]{1,0:T(8,128)(2,1)}, u32[]{:S(2)}, u32[]{:S(2)}) collective-permute-start(bf16[96,768]{1,0:T(8,128)(2,1)} %param.13), channel_id=1, source_target_pairs={{0,8},{4,12},{8,16},{12,20},{16,24},{20,28},{24,0},{28,4},{1,9},{5... | collective-permute-start | bytes 442376 | tf_op jit(solution)/shard_map/ppermute | solution.py:33
  22.1 22.6 %collective-permute-start.11 = (bf16[96,768]{1,0:T(8,128)(2,1)}, bf16[96,768]{1,0:T(8,128)(2,1)S(1)}, u32[]{:S(2)}, u32[]{:S(2)}) collective-permute-start(bf16[96,768]{1,0:T(8,128)(2,1)} %param.13), channel_id=1, source_target_pairs={{0,24},{4,28},{8,0},{12,4},{16,8},{20,12},{24,16},{28,20},{1,25},{... | collective-permute-start | bytes 442376 | tf_op jit(solution)/shard_map/ppermute | solution.py:33
  26.9 24.3 %collective-permute-start.4 = (bf16[112,768]{1,0:T(8,128)(2,1)}, bf16[112,768]{1,0:T(8,128)(2,1)S(1)}, u32[]{:S(2)}, u32[]{:S(2)}) collective-permute-start(bf16[112,768]{1,0:T(8,128)(2,1)} %get-tuple-element.82), channel_id=1, source_target_pairs={{0,24},{4,28},{8,0},{12,4},{16,8},{20,12},{24,16},{28,20},{1,25},{... | collective-permute-start | bytes 516104 | tf_op jit(solution)/shard_map/ppermute | solution.py:33
  29.2 24.1 %collective-permute-start.3 = (bf16[112,768]{1,0:T(8,128)(2,1)}, bf16[112,768]{1,0:T(8,128)(2,1)S(1)}, u32[]{:S(2)}, u32[]{:S(2)}) collective-permute-start(bf16[112,768]{1,0:T(8,128)(2,1)} %get-tuple-element.82), channel_id=1, source_target_pairs={{0,16},{4,20},{8,24},{12,28},{16,0},{20,4},{24,8},{28,12},{1,17},{... | collective-permute-start | bytes 516104 | tf_op jit(solution)/shard_map/ppermute | solution.py:33
  48.0 23.7 %collective-permute-start.12 = (bf16[4,96,768]{2,1,0:T(8,128)(2,1)S(1)}, bf16[4,96,768]{2,1,0:T(8,128)(2,1)S(1)}, u32[]{:S(2)}, u32[]{:S(2)}) collective-permute-start(bf16[4,96,768]{2,1,0:T(8,128)(2,1)S(1)} %get-tuple-element.117), channel_id=1, source_target_pairs={{0,2},{1,5},{2,0},{3,7},{4,6},{5,1},{6,4},{7,3},{8,10},{9,13},{10,... | collective-permute-start | bytes 1769480 | tf_op jit(solution)/shard_map/ppermute | solution.py:43
  51.3 18.7 %collective-permute-start.17 = (bf16[4,96,768]{2,1,0:T(8,128)(2,1)S(1)}, bf16[4,96,768]{2,1,0:T(8,128)(2,1)S(1)}, u32[]{:S(2)}, u32[]{:S(2)}) collective-permute-start(bf16[4,96,768]{2,1,0:T(8,128)(2,1)S(1)} %get-tuple-element.119), channel_id=1, source_target_pairs={{0,2},{1,5},{2,0},{3,7},{4,6},{5,1},{6,4},{7,3},{8,10},{9,13},{10,... | collective-permute-start | bytes 1769480 | tf_op jit(solution)/shard_map/ppermute | solution.py:43
  53.4 31.4 %collective-permute-start.5 = (bf16[4,112,768]{2,1,0:T(8,128)(2,1)S(1)}, bf16[4,112,768]{2,1,0:T(8,128)(2,1)S(1)}, u32[]{:S(2)}, u32[]{:S(2)}) collective-permute-start(bf16[4,112,768]{2,1,0:T(8,128)(2,1)S(1)} %get-tuple-element.109), channel_id=1, source_target_pairs={{0,2},{1,5},{2,0},{3,7},{4,6},{5,1},{6,4},{7,3},{8,10},{9,13},{10,... | collective-permute-start | bytes 2064392 | tf_op jit(solution)/shard_map/ppermute | solution.py:43
  55.2 31.4 %collective-permute-start.1 = (bf16[2,256,768]{2,1,0:T(8,128)(2,1)S(1)}, bf16[2,256,768]{2,1,0:T(8,128)(2,1)S(1)}, u32[]{:S(2)}, u32[]{:S(2)}) collective-permute-start(bf16[2,256,768]{2,1,0:T(8,128)(2,1)S(1)} %pad_maximum_fusion.9), channel_id=1, source_target_pairs={{0,1},{1,0},{2,3},{3,2},{4,5},{5,4},{6,7},{7,6},{8,9},{9,8},{10,11... | collective-permute-start | bytes 2359304 | tf_op jit(solution)/shard_map/ppermute | solution.py:25
  70.1 18.3 %collective-permute-start.18 = (bf16[2,4,96,768]{3,2,1,0:T(8,128)(2,1)S(1)}, bf16[2,4,96,768]{3,2,1,0:T(8,128)(2,1)S(1)}, u32[]{:S(2)}, u32[]{:S(2)}) collective-permute-start(bf16[2,4,96,768]{3,2,1,0:T(8,128)(2,1)S(1)} %pad_maximum_fusion.4), channel_id=1, source_target_pairs={{0,4},{1,3},{2,6},{3,1},{4,0},{5,7},{6,2},{7,5},{8,12},{9,11},{10,... | collective-permute-start | bytes 3538952 | tf_op jit(solution)/shard_map/ppermute | solution.py:43
  71.8 27.2 %collective-permute-start.13 = (bf16[2,4,96,768]{3,2,1,0:T(8,128)(2,1)S(1)}, bf16[2,4,96,768]{3,2,1,0:T(8,128)(2,1)S(1)}, u32[]{:S(2)}, u32[]{:S(2)}) collective-permute-start(bf16[2,4,96,768]{3,2,1,0:T(8,128)(2,1)S(1)} %pad_maximum_fusion.3), channel_id=1, source_target_pairs={{0,4},{1,3},{2,6},{3,1},{4,0},{5,7},{6,2},{7,5},{8,12},{9,11},{10,... | collective-permute-start | bytes 3538952 | tf_op jit(solution)/shard_map/ppermute | solution.py:43
  84.8 28.9 %collective-permute-start.6 = (bf16[2,4,112,768]{3,2,1,0:T(8,128)(2,1)S(1)}, bf16[2,4,112,768]{3,2,1,0:T(8,128)(2,1)S(1)}, u32[]{:S(2)}, u32[]{:S(2)}) collective-permute-start(bf16[2,4,112,768]{3,2,1,0:T(8,128)(2,1)S(1)} %pad_maximum_fusion.1), channel_id=1, source_target_pairs={{0,4},{1,3},{2,6},{3,1},{4,0},{5,7},{6,2},{7,5},{8,12},{9,11},{10,... | collective-permute-start | bytes 4128776 | tf_op jit(solution)/shard_map/ppermute | solution.py:43
  171.2 16.8 %collective-permute-start.19 = (bf16[512,768]{1,0:T(8,128)(2,1)}, bf16[512,768]{1,0:T(8,128)(2,1)}, u32[]{:S(2)}, u32[]{:S(2)}) collective-permute-start(bf16[512,768]{1,0:T(8,128)(2,1)} %add_convert_fusion.2), channel_id=1, source_target_pairs={{0,1},{1,0},{2,3},{3,2},{4,5},{5,4},{6,7},{7,6},{8,9},{9,8},{10,11... | collective-permute-start | bytes 2359304 | tf_op jit(solution)/shard_map/ppermute | solution.py:25
  219.1 46.3 %collective-permute-start.29 = (bf16[2,4,96,768]{3,2,1,0:T(8,128)(2,1)}, bf16[2,4,96,768]{3,2,1,0:T(8,128)(2,1)}, u32[]{:S(2)}, u32[]{:S(2)}) collective-permute-start(bf16[2,4,96,768]{3,2,1,0:T(8,128)(2,1)} %pad_maximum_fusion.7), channel_id=1, source_target_pairs={{0,2},{1,5},{2,0},{3,7},{4,6},{5,1},{6,4},{7,3},{8,10},{9,13},{10,... | collective-permute-start | bytes 3538952 | tf_op jit(solution)/shard_map/ppermute | solution.py:43
  222.9 45.9 %collective-permute-start.34 = (bf16[2,4,96,768]{3,2,1,0:T(8,128)(2,1)}, bf16[2,4,96,768]{3,2,1,0:T(8,128)(2,1)}, u32[]{:S(2)}, u32[]{:S(2)}) collective-permute-start(bf16[2,4,96,768]{3,2,1,0:T(8,128)(2,1)} %pad_maximum_fusion.8), channel_id=1, source_target_pairs={{0,2},{1,5},{2,0},{3,7},{4,6},{5,1},{6,4},{7,3},{8,10},{9,13},{10,... | collective-permute-start | bytes 3538952 | tf_op jit(solution)/shard_map/ppermute | solution.py:43
  265.0 31.8 %collective-permute-start.24 = (bf16[2,4,112,768]{3,2,1,0:T(8,128)(2,1)S(1)}, bf16[2,4,112,768]{3,2,1,0:T(8,128)(2,1)S(1)}, u32[]{:S(2)}, u32[]{:S(2)}) collective-permute-start(bf16[2,4,112,768]{3,2,1,0:T(8,128)(2,1)S(1)} %pad_maximum_fusion.2), channel_id=1, source_target_pairs={{0,2},{1,5},{2,0},{3,7},{4,6},{5,1},{6,4},{7,3},{8,10},{9,13},{10,... | collective-permute-start | bytes 4128776 | tf_op jit(solution)/shard_map/ppermute | solution.py:43
  270.3 24.8 %collective-permute-start.35 = (bf16[4,96,768]{2,1,0:T(8,128)(2,1)S(1)}, bf16[4,96,768]{2,1,0:T(8,128)(2,1)S(1)}, u32[]{:S(2)}, u32[]{:S(2)}) collective-permute-start(bf16[4,96,768]{2,1,0:T(8,128)(2,1)S(1)} %fusion.43), channel_id=1, source_target_pairs={{0,4},{1,3},{2,6},{3,1},{4,0},{5,7},{6,2},{7,5},{8,12},{9,11},{10,... | collective-permute-start | bytes 1769480 | tf_op jit(solution)/shard_map/ppermute | solution.py:43
  271.5 28.7 %collective-permute-start.23 = (bf16[128,768]{1,0:T(8,128)(2,1)S(1)}, bf16[128,768]{1,0:T(8,128)(2,1)S(1)}, u32[]{:S(2)}, u32[]{:S(2)}) collective-permute-start(bf16[128,768]{1,0:T(8,128)(2,1)S(1)} %fusion.110), channel_id=1, source_target_pairs={{0,2},{2,0},{1,3},{3,1},{4,6},{6,4},{5,7},{7,5},{8,10},{10,8},{9,1... | collective-permute-start | bytes 589832 | tf_op jit(solution)/shard_map/ppermute | solution.py:28
  286.0 19.0 %collective-permute-start.33 = (bf16[96,768]{1,0:T(8,128)(2,1)S(1)}, bf16[96,768]{1,0:T(8,128)(2,1)S(1)}, u32[]{:S(2)}, u32[]{:S(2)}) collective-permute-start(bf16[96,768]{1,0:T(8,128)(2,1)S(1)} %get-tuple-element.114), channel_id=1, source_target_pairs={{0,24},{4,28},{8,0},{12,4},{16,8},{20,12},{24,16},{28,20},{1,25},{... | collective-permute-start | bytes 442376 | tf_op jit(solution)/shard_map/ppermute | solution.py:33
  305.0 20.6 %collective-permute-start.37 = (bf16[96,768]{1,0:T(8,128)(2,1)S(1)}, bf16[96,768]{1,0:T(8,128)(2,1)S(1)}, u32[]{:S(2)}, u32[]{:S(2)}) collective-permute-start(bf16[96,768]{1,0:T(8,128)(2,1)S(1)} %get-tuple-element.112), channel_id=1, source_target_pairs={{0,16},{4,20},{8,24},{12,28},{16,0},{20,4},{24,8},{28,12},{1,17},{... | collective-permute-start | bytes 442376 | tf_op jit(solution)/shard_map/ppermute | solution.py:33
  313.7 19.3 %collective-permute-start.27 = (bf16[112,768]{1,0:T(8,128)(2,1)S(1)}, bf16[112,768]{1,0:T(8,128)(2,1)S(1)}, u32[]{:S(2)}, u32[]{:S(2)}) collective-permute-start(bf16[112,768]{1,0:T(8,128)(2,1)S(1)} %get-tuple-element.107), channel_id=1, source_target_pairs={{0,16},{4,20},{8,24},{12,28},{16,0},{20,4},{24,8},{28,12},{1,17},{... | collective-permute-start | bytes 516104 | tf_op jit(solution)/shard_map/ppermute | solution.py:33
  (101 other events, 594.2 us)

commit v2 on v1

v2 whole, which is shorter than its diff:
```python
import functools

import jax
import jax.numpy as jnp
from jax import lax
from jax.experimental import pallas as pl
from jax.experimental.pallas import tpu as pltpu
from jax.sharding import PartitionSpec as P

HD = 64
LANES = 128
EXTRA = 16
BF = jnp.bfloat16
F32 = jnp.float32
LIMIT = 56 * 1024 * 1024
NN = ((1,), (0,))
NT = ((1,), (1,))
TN = ((0,), (0,))


def dot(left, right, dims=NN):
    return lax.dot_general(left, right, (dims, ((), ())), preferred_element_type=F32)


def call(kernel, outs, args, scalars=0, scratch=(), flops=0):
    return pl.pallas_call(
        kernel,
        out_shape=[jax.ShapeDtypeStruct(shape, kind) for shape, kind in outs],
        in_specs=[pl.BlockSpec(memory_space=pltpu.SMEM)] * scalars
        + [pl.BlockSpec(memory_space=pltpu.VMEM)] * (len(args) - scalars),
        out_specs=[pl.BlockSpec(memory_space=pltpu.VMEM)] * len(outs),
        scratch_shapes=list(scratch),
        compiler_params=pltpu.CompilerParams(vmem_limit_bytes=LIMIT),
        cost_estimate=pl.CostEstimate(
            flops=flops,
            bytes_accessed=sum(a.size * a.dtype.itemsize for a in args),
            transcendentals=0,
        ),
    )(*args)


class Place:
    def __init__(self):
        self.groups = lax.axis_size("dp")
        self.line_size = self.groups // 2
        data, model = lax.axis_index("dp"), lax.axis_index("mp")
        self.line, self.pair = data // 2, data % 2
        self.row, self.core = model // 2, model % 2

    def core_swap(self, value):
        return lax.ppermute(value, "mp", [(0, 1), (1, 0), (2, 3), (3, 2)])

    def row_swap(self, value):
        return lax.ppermute(value, "mp", [(0, 2), (2, 0), (1, 3), (3, 1)])

    def line_swap(self, value, step):
        pairs = [(i, i ^ (2 * step)) for i in range(self.groups)]
        return lax.ppermute(value, "dp", pairs)

    def cross(self, value, along_row):
        pairs = []
        for data in range(self.groups):
            for model in range(4):
                if model % 2 == along_row:
                    pairs.append((data * 4 + model, data * 4 + (model ^ 2)))
                else:
                    pairs.append((data * 4 + model, (data ^ 1) * 4 + model))
        return lax.ppermute(value, ("dp", "mp"), pairs)

    def quarters(self):
        other_row, other_pair = 1 - self.row, 1 - self.pair
        swap = self.core == 0
        first = (jnp.where(swap, other_row, self.row), jnp.where(swap, self.pair, other_pair))
        second = (jnp.where(swap, self.row, other_row), jnp.where(swap, other_pair, self.pair))
        return (self.row, self.pair), first, second, (other_row, other_pair)

    def scatter_table(self):
        flags, slots = [], []
        for row in range(2):
            for pair in range(2):
                same_row, same_pair = self.row == row, self.pair == pair
                own = same_row & same_pair
                far = ~same_row & ~same_pair
                first = jnp.where(self.core == 0, ~same_row & same_pair, same_row & ~same_pair)
                flags.append((far | first).astype(jnp.int32))
                slots.append((far | ~(own | first | far)).astype(jnp.int32))
        return jnp.stack(flags + slots + [self.line]).astype(jnp.int32)


def gather_line(place, shard):
    n = place.line_size
    if n <= 4:
        return jnp.stack([shard] + [place.line_swap(shard, step) for step in range(1, n)])
    held, step = shard[None], 1
    while step < n:
        held, step = jnp.concatenate([held, place.line_swap(held, step)]), step * 2
    return held


def scatter_line(place, terms):
    n = place.line_size
    if n <= 4:
        low = terms.astype(BF)
        total = terms[0]
        for step in range(1, n):
            total = total + place.line_swap(low[step], step).astype(F32)
        return total
    step = n // 2
    while step:
        got = place.line_swap(terms[step:].astype(BF), step)
        terms, step = terms[:step] + got.astype(F32), step // 2
    return terms[0]


def place_kernel(depth, n, extra, where, own, first, rest, whole, *more):
    for quarter in range(4):
        row, pair = where[2 * quarter], where[2 * quarter + 1]
        source = (own, first, rest.at[0], rest.at[1])[quarter]
        for step in range(n):
            data = jnp.bitwise_xor(where[8], step) * 2 + pair
            start = pl.multiple_of(data * depth, 16)
            whole[row, pl.ds(start, depth), :] = source[step, :depth]
            if extra:
                more[0][row, data] = source[step, depth:]


def gather_group(place, own, depth):
    n, rows, width = own.shape
    first = place.cross(own, 0)
    rest = place.cross(jnp.stack([own, first]), 1)
    extra = rows > depth
    if depth % 16 == 0:
        spots = [scalar for spot in place.quarters() for scalar in spot] + [place.line]
        outs = [((2, 2 * n * depth, width), own.dtype)]
        if extra:
            outs.append(((2, 2 * n, EXTRA, width), own.dtype))
        return call(
            functools.partial(place_kernel, depth, n, extra),
            outs,
            [jnp.stack(spots).astype(jnp.int32), own, first, rest],
            scalars=1,
        )
    whole = jnp.zeros((2, n, 2, rows, width), own.dtype)
    for piece, (row, pair) in zip((own, first, rest[0], rest[1]), place.quarters()):
        for step in range(n):
            start = (row, place.line ^ step, pair, 0, 0)
            whole = lax.dynamic_update_slice(whole, piece[step][None, None, None], start)
    out = [whole[:, :, :, :depth].reshape(2, 2 * n * depth, width)]
    if extra:
        out.append(whole[:, :, :, depth:].reshape(2, 2 * n, EXTRA, width))
    return out


def spread(place, terms, depth, vectors=None):
    n = place.line_size
    terms = terms.reshape(2, n, 2, depth, terms.shape[-1])
    if vectors is not None:
        vectors = jnp.broadcast_to(vectors.reshape(2, n, 2, 1, -1), (2, n, 2, EXTRA, vectors.shape[-1]))
        terms = jnp.concatenate([terms, vectors.astype(terms.dtype)], axis=3)
    order = lax.iota(jnp.int32, n) ^ place.line
    terms = jnp.take(terms, order, axis=1)

    def quarter(at):
        size = (1, n, 1) + terms.shape[3:]
        return lax.dynamic_slice(terms, (at[0], 0, at[1], 0, 0), size).reshape((n,) + terms.shape[3:])

    own, first, second, far = (quarter(at) for at in place.quarters())
    return jnp.stack([first, far]), jnp.stack([own, second])


def scatter_group(place, send, keep):
    got = place.cross(send, 0)
    second = (keep[1].astype(F32) + got[1].astype(F32)).astype(BF)
    got_second = place.cross(second, 1)
    own = keep[0].astype(F32) + got[0].astype(F32) + got_second.astype(F32)
    return scatter_line(place, own)


def store_quarters(table, n, depth, row, value, send, keep, vectors=None):
    for pair in range(2):
        flag, slot = table[row * 2 + pair], table[4 + row * 2 + pair]

        def put(ref):
            for line in range(n):
                at = jnp.bitwise_xor(table[8], line)
                data = line * 2 + pair
                ref[slot, at, :depth] = value[data * depth : (data + 1) * depth]
                if vectors is not None:
                    extra = vectors[pl.ds(row * 2 * n + data, 1), :]
                    ref[slot, at, depth:] = jnp.broadcast_to(extra, (EXTRA, extra.shape[1])).astype(BF)

        pl.when(flag == 1)(lambda: put(send))
        pl.when(flag == 0)(lambda: put(keep))


def outer_kernel(n, depth, table, left, right, send, keep):
    width = send.shape[-1]
    for row in range(2):
        value = dot(left[...], right[:, row * width : (row + 1) * width], TN).astype(BF)
        store_quarters(table, n, depth, row, value, send, keep)


def outer(place, table, left, right, depth):
    n, width = place.line_size, right.shape[1] // 2
    if depth % 16:
        halves = [dot(left, right[:, i * width : (i + 1) * width], TN).astype(BF) for i in range(2)]
        return spread(place, jnp.stack(halves), depth)
    shape = ((2, n, depth, width), BF)
    return call(
        functools.partial(outer_kernel, n, depth),
        [shape, shape],
        [table, left, right],
        scalars=1,
        flops=2 * left.size * right.shape[1],
    )


def by_row(value, row, cols):
    kinds = value.shape[1] // (2 * cols)
    return jnp.concatenate(
        [value[:, (2 * t + row) * cols : (2 * t + row + 1) * cols] for t in range(kinds)], axis=1
    )


def outer_attn_kernel(n, depth, cols, table, x, d_qkv, d_att, ctx, vectors, send, keep):
    whole = jnp.concatenate(
        [dot(x[...], d_qkv[...], TN).astype(BF), dot(d_att[...], ctx[...], TN).astype(BF)], axis=1
    )
    for row in range(2):
        store_quarters(table, n, depth, row, by_row(whole, row, cols), send, keep, vectors)


def outer_attn(place, table, x, d_qkv, d_att, ctx, vectors, depth):
    n, cols, width = place.line_size, ctx.shape[1] // 2, x.shape[1]
    if depth % 16:
        whole = jnp.concatenate([dot(x, d_qkv, TN), dot(d_att, ctx, TN)], axis=1).astype(BF)
        return spread(place, jnp.stack([by_row(whole, i, cols) for i in range(2)]), depth, vectors)
    shape = ((2, n, depth + EXTRA, width), BF)
    return call(
        functools.partial(outer_attn_kernel, n, depth, cols),
        [shape, shape],
        [table, x, d_qkv, d_att, ctx, vectors],
        scalars=1,
        flops=2 * x.size * (d_qkv.shape[1] + ctx.shape[1]),
    )


def head_lanes(rows, head):
    lane = lax.broadcasted_iota(jnp.int32, (rows, LANES), 1)
    return (lane < HD) if head == 0 else (lane >= HD)


def attend_kernel(block, chunk, bounds, x, weights, q_bias, v_bias, joined, qkv, probs, ctx, part, mask):
    rows, cols = x.shape[0], q_bias.shape[1]
    half = cols // 2
    for kind in range(4):
        cut = slice(kind * half, (kind + 1) * half)
        joined[:, kind * cols : (kind + 1) * cols] = jnp.concatenate(
            [weights[0, :, cut], weights[1, :, cut]], axis=1
        )

    def labels(index):
        part_of = index // block
        place = index + jnp.where(part_of == 1, block, jnp.where(part_of == 2, -block, 0))
        total = jnp.zeros_like(index)
        for j in range(4):
            total = total + (place >= bounds[j]).astype(jnp.int32)
        return total

    across = labels(lax.broadcasted_iota(jnp.int32, (1, rows), 1))
    down = labels(lax.broadcasted_iota(jnp.int32, (rows, 1), 0))
    mask[...] = jnp.where(down == across, 0.0, -1000000000.0)
    qkv[:, :cols] = (
        (dot(x[...], joined[:, :cols]) + q_bias[...]).astype(BF).astype(F32) * HD ** (-0.5)
    ).astype(BF)
    qkv[:, cols : 2 * cols] = dot(x[...], joined[:, cols : 2 * cols]).astype(BF)
    qkv[:, 2 * cols :] = (dot(x[...], joined[:, 2 * cols : 3 * cols]) + v_bias[...]).astype(BF)

    def pair_step(pair, carry):
        def lanes(kind):
            return pl.ds(pl.multiple_of(kind * cols + pair * LANES, LANES), LANES)

        def row_step(step, inner_carry):
            at = pl.ds(pl.multiple_of(step * chunk, chunk), chunk)
            queries = qkv[at, lanes(0)]
            outs = []
            for head in range(2):
                one = jnp.where(head_lanes(chunk, head), queries, jnp.zeros_like(queries))
                scores = dot(one, qkv[:, lanes(1)], NT) + mask[at, :]
                exponent = jnp.exp(scores - jnp.max(scores, axis=1, keepdims=True))
                low = (exponent * (1.0 / jnp.sum(exponent, axis=1, keepdims=True))).astype(BF)
                probs[pair * 2 + head, at, :] = low
                outs.append(dot(low, qkv[:, lanes(2)]))
            ctx[at, pl.ds(pl.multiple_of(pair * LANES, LANES), LANES)] = jnp.where(
                head_lanes(chunk, 0), outs[0], outs[1]
            ).astype(BF)
            return inner_carry

        return lax.fori_loop(0, rows // chunk, row_step, carry)

    lax.fori_loop(0, cols // LANES, pair_step, 0)
    part[...] = dot(ctx[...], joined[:, 3 * cols :], NT).astype(BF)


def norm_parts(values):
    centred = values - jnp.mean(values, axis=-1, keepdims=True)
    rate = lax.rsqrt(jnp.mean(centred * centred, axis=-1, keepdims=True) + 1e-06)
    return centred * rate, rate


def norm_back(grad, unit, rate, scale):
    inner = grad * scale
    return rate * (
        inner
        - jnp.mean(inner, axis=-1, keepdims=True)
        - unit * jnp.mean(inner * unit, axis=-1, keepdims=True)
    )


def loop_rows(rows, chunk, step):
    def one(index, carry):
        step(pl.ds(pl.multiple_of(index * chunk, chunk), chunk))
        return carry

    lax.fori_loop(0, rows // chunk, one, 0)


def up_kernel(chunk, x, mine, other, norms, up_bias, weights, unit, rate, low, activated, slope, hidden):
    rows, width = x.shape
    units = weights.shape[2]

    def first(at):
        value = x[at, :].astype(F32) + mine[at, :].astype(F32) + other[at, :].astype(F32) + norms[2:3]
        one, scale = norm_parts(value)
        unit[at, :] = one
        rate[at, :] = jnp.broadcast_to(scale, (chunk, LANES))
        low[at, :] = (one * norms[0:1] + norms[3:4]).astype(BF)

    loop_rows(rows, chunk, first)
    for half in range(2):
        cut = slice(half * units, (half + 1) * units)
        hidden[...] = dot(low[...], weights[half])

        def act(at):
            value = hidden[at, :] + up_bias[:, cut]
            share = 0.5 + 0.5 * lax.erf(value * (0.5**0.5))
            activated[at, cut] = (value * share).astype(BF)
            bell = jnp.exp(-0.5 * value * value) * 0.3989422804014327
            slope[at, cut] = (share + value * bell).astype(BF)

        loop_rows(rows, chunk, act)


def down_kernel(activated, weights, part):
    units = weights.shape[2]
    part[...] = (
        dot(activated[:, :units], weights[0], NT) + dot(activated[:, units:], weights[1], NT)
    ).astype(BF)


def column_sums(totals, index, value):
    totals[index : index + 1, :] = totals[index : index + 1, :] + jnp.sum(value, axis=0, keepdims=True)


def second_kernel(chunk, unit, mine, other, grad, norms, result, d_second, d_mixed, totals):
    totals[...] = jnp.zeros_like(totals)

    def step(at):
        normed = unit[at, :] * norms[0:1] + norms[3:4]
        value = normed + mine[at, :].astype(F32) + other[at, :].astype(F32) + norms[4:5]
        one, rate = norm_parts(value)
        result[at, :] = (one * norms[1:2] + norms[5:6]).astype(BF)
        dy = grad[at, :].astype(F32)
        back = norm_back(dy, one, rate, norms[1:2])
        d_second[at, :] = back
        d_mixed[at, :] = back.astype(BF)
        column_sums(totals, 0, dy * one)
        column_sums(totals, 1, back)
        column_sums(totals, 2, dy)

    loop_rows(unit.shape[0], chunk, step)


def hidden_back_kernel(chunk, d_mixed, down, up, slope, d_hidden, part, sums, d_act):
    rows, units = d_mixed.shape[0], down.shape[2]
    sums[...] = jnp.zeros_like(sums)
    for half in range(2):
        cut = slice(half * units, (half + 1) * units)
        d_act[...] = dot(d_mixed[...], down[half])

        def step(at):
            low = (d_act[at, :] * slope[at, cut].astype(F32)).astype(BF)
            d_hidden[at, cut] = low
            sums[0:1, cut] = sums[0:1, cut] + jnp.sum(low.astype(F32), axis=0, keepdims=True)

        loop_rows(rows, chunk, step)
    part[...] = (
        dot(d_hidden[:, :units], up[0], NT) + dot(d_hidden[:, units:], up[1], NT)
    ).astype(BF)


def first_back_kernel(chunk, d_second, mine, other, unit, rate, norms, joined, d_first_in, d_att, d_ctx, totals):
    rows, cols = d_second.shape[0], d_ctx.shape[1]
    totals[...] = jnp.zeros_like(totals)

    def step(at):
        d_first = d_second[at, :] + mine[at, :].astype(F32) + other[at, :].astype(F32)
        one = unit[at, :]
        back = norm_back(d_first, one, rate[at, 0:1], norms[0:1])
        d_first_in[at, :] = back
        d_att[at, :] = back.astype(BF)
        column_sums(totals, 0, d_first * one)
        column_sums(totals, 1, back)
        column_sums(totals, 2, d_first)

    loop_rows(rows, chunk, step)
    d_ctx[...] = dot(d_att[...], joined[:, 3 * cols :]).astype(BF)


def attend_back_kernel(chunk, d_ctx, qkv, probs, ctx, joined, d_qkv, sums, part, d_scores):
    rows, cols = ctx.shape
    sums[...] = jnp.zeros_like(sums)

    def pair_step(pair, carry):
        def lanes(kind):
            return pl.ds(pl.multiple_of(kind * cols + pair * LANES, LANES), LANES)

        def row_step(step, inner_carry):
            at = pl.ds(pl.multiple_of(step * chunk, chunk), chunk)
            grads = d_ctx[at, lanes(0)]
            with_context = grads.astype(F32) * ctx[at, lanes(0)].astype(F32)
            outs = []
            for head in range(2):
                inside = head_lanes(chunk, head)
                one = jnp.where(inside, grads, jnp.zeros_like(grads))
                d_probs = dot(one, qkv[:, lanes(2)], NT)
                inner = jnp.sum(jnp.where(inside, with_context, 0.0), axis=1, keepdims=True)
                low = (probs[pair * 2 + head, at, :].astype(F32) * (d_probs - inner)).astype(BF)
                d_scores[head, at, :] = low
                outs.append(dot(low, qkv[:, lanes(1)]))
            d_queries = (jnp.where(head_lanes(chunk, 0), outs[0], outs[1]) * HD ** (-0.5)).astype(BF)
            d_qkv[at, lanes(0)] = d_queries
            sums[0:1, lanes(0)] = sums[0:1, lanes(0)] + jnp.sum(
                d_queries.astype(F32), axis=0, keepdims=True
            )
            return inner_carry

        lax.fori_loop(0, rows // chunk, row_step, 0)
        d_keys, d_values = 0.0, 0.0
        for head in range(2):
            inside = head_lanes(rows, head)
            queries, grads = qkv[:, lanes(0)], d_ctx[:, lanes(0)]
            d_keys += dot(d_scores[head], jnp.where(inside, queries, jnp.zeros_like(queries)), TN)
            d_values += dot(probs[pair * 2 + head], jnp.where(inside, grads, jnp.zeros_like(grads)), TN)
        d_qkv[:, lanes(1)] = d_keys.astype(BF)
        d_values = d_values.astype(BF)
        d_qkv[:, lanes(2)] = d_values
        sums[0:1, lanes(1)] = jnp.sum(d_values.astype(F32), axis=0, keepdims=True)
        return carry

    lax.fori_loop(0, cols // LANES, pair_step, 0)
    part[...] = dot(d_qkv[...], joined[:, : 3 * cols], NT).astype(BF)


def body(
    inputs, w_qkv, w_out, w_up, w_down, unit_bias, norm_gain, norm_bias, seq_lengths, cotangent
):
    place = Place()
    row, core = place.row, place.core
    groups = place.groups
    block, width = inputs.shape[1], inputs.shape[2]
    rows = 4 * block
    depth, head_cols = w_qkv.shape[1], w_qkv.shape[2]
    units = w_up.shape[1]
    share = unit_bias.shape[1]
    small = norm_gain.shape[1]
    cols = 2 * head_cols
    heads = cols // HD
    chunk = 32

    vector = jnp.concatenate([unit_bias[0], norm_gain.reshape(-1), norm_bias.reshape(-1)])
    vector = jnp.pad(vector[None], ((0, EXTRA - 1), (0, width - vector.shape[0])))
    attn_shard = jnp.concatenate([w_qkv[0], w_qkv[1], w_qkv[2], jnp.transpose(w_out)], axis=1)
    attn_shard = jnp.concatenate([attn_shard, vector], axis=0)
    attn_line = gather_line(place, attn_shard)
    up_shard, attn_line = lax.optimization_barrier((w_up, attn_line))
    up_line = gather_line(place, up_shard)
    down_shard, up_line = lax.optimization_barrier((jnp.transpose(w_down), up_line))
    down_line = gather_line(place, down_shard)

    keep = lambda array, index: lax.dynamic_index_in_dim(array, index, 0, keepdims=False)
    outgoing = jnp.stack([keep(inputs, 1 - row), keep(cotangent, 1 - row)])
    incoming = place.row_swap(outgoing)
    mine = jnp.stack([keep(inputs, row), keep(cotangent, row)])
    low_rows = jnp.where(row == 0, mine, incoming)
    high_rows = jnp.where(row == 0, incoming, mine)
    half = jnp.concatenate([low_rows, high_rows], axis=1)
    other = place.core_swap(half)
    both = jnp.where(
        core == 0,
        jnp.concatenate([half, other], axis=1),
        jnp.concatenate([other, half], axis=1),
    )
    x, grad_rows = both[0], both[1]

    attn_whole, extras = gather_group(place, attn_line, depth)
    up_whole = gather_group(place, up_line, depth)[0]
    down_whole = gather_group(place, down_line, depth)[0]
    vectors = extras[:, :, 0, : share + 6 * small]
    unit_values = vectors[:, :, :share].reshape(2, groups * share).astype(F32)
    norm_here = vectors[:, :, share:]
    norm_there = place.core_swap(norm_here)
    norm_all = jnp.where(
        core == 0,
        jnp.stack([norm_here, norm_there], axis=2),
        jnp.stack([norm_there, norm_here], axis=2),
    )
    norm_all = norm_all.reshape(2, groups, 2, 6, small)
    norm_all = jnp.transpose(norm_all, (3, 1, 0, 2, 4)).reshape(6, width).astype(F32)
    norms = jnp.pad(norm_all, ((0, 2), (0, 0)))
    q_bias = unit_values[:, :head_cols].reshape(1, cols)
    v_bias = unit_values[:, head_cols:cols].reshape(1, cols)
    up_bias = unit_values[:, cols:].reshape(1, 2 * units)
    table = place.scatter_table()

    bounds = jnp.cumsum(keep(seq_lengths, row), dtype=jnp.int32)
    wide = rows * width
    joined, qkv, probs, ctx, part = call(
        functools.partial(attend_kernel, block, 128),
        [
            ((width, 4 * cols), BF),
            ((rows, 3 * cols), BF),
            ((heads, rows, rows), BF),
            ((rows, cols), BF),
            ((rows, width), BF),
        ],
        [bounds, x, attn_whole, q_bias, v_bias],
        scalars=1,
        scratch=[pltpu.VMEM((rows, rows), F32)],
        flops=8 * wide * cols,
    )
    unit, rate, first_low, activated, slope = call(
        functools.partial(up_kernel, chunk),
        [
            ((rows, width), F32),
            ((rows, LANES), F32),
            ((rows, width), BF),
            ((rows, 2 * units), BF),
            ((rows, 2 * units), BF),
        ],
        [x, part, place.core_swap(part), norms, up_bias, up_whole],
        scratch=[pltpu.VMEM((rows, units), F32)],
        flops=4 * wide * units,
    )
    (part,) = call(down_kernel, [((rows, width), BF)], [activated, down_whole], flops=4 * wide * units)
    result, d_second, d_mixed, totals_two = call(
        functools.partial(second_kernel, chunk),
        [((rows, width), BF), ((rows, width), F32), ((rows, width), BF), ((8, width), F32)],
        [unit, part, place.core_swap(part), grad_rows, norms],
        flops=60 * wide,
    )

    down_send, down_keep = outer(place, table, d_mixed, activated, depth)
    grad_down = scatter_group(place, down_send, down_keep)
    d_hidden, part, up_sums = call(
        functools.partial(hidden_back_kernel, chunk),
        [((rows, 2 * units), BF), ((rows, width), BF), ((8, 2 * units), F32)],
        [d_mixed, down_whole, up_whole, slope],
        scratch=[pltpu.VMEM((rows, units), F32)],
        flops=8 * wide * units,
    )
    up_send, up_keep = outer(place, table, first_low, d_hidden, depth)
    grad_up = scatter_group(place, up_send, up_keep)
    d_first_in, d_att, d_ctx, totals_one = call(
        functools.partial(first_back_kernel, chunk),
        [((rows, width), F32), ((rows, width), BF), ((rows, cols), BF), ((8, width), F32)],
        [d_second, part, place.core_swap(part), unit, rate, norms, joined],
        flops=2 * wide * cols,
    )
    d_qkv, attn_sums, part = call(
        functools.partial(attend_back_kernel, 128),
        [((rows, 3 * cols), BF), ((8, 2 * cols), F32), ((rows, width), BF)],
        [d_ctx, qkv, probs, ctx, joined],
        scratch=[pltpu.VMEM((2, rows, rows), BF)],
        flops=10 * wide * cols,
    )
    unit_terms = jnp.concatenate(
        [attn_sums[0, :cols].reshape(2, head_cols), attn_sums[0, cols:].reshape(2, head_cols),
         up_sums[0].reshape(2, units)],
        axis=1,
    ).reshape(2, groups, share)
    norm_terms = jnp.stack(
        [totals_one[0], totals_two[0], totals_one[1], totals_one[2], totals_two[1], totals_two[2]]
    ).reshape(6, groups, 2, 2, small)
    norm_terms = lax.dynamic_index_in_dim(norm_terms, core, 3, keepdims=False)
    norm_terms = jnp.transpose(norm_terms, (2, 1, 0, 3)).reshape(2, groups, 6 * small)
    vector_terms = jnp.concatenate([unit_terms, norm_terms], axis=2)
    vector_terms = jnp.pad(vector_terms, ((0, 0), (0, 0), (0, width - vector_terms.shape[2])))
    attn_send, attn_keep = outer_attn(
        place, table, x, d_qkv, d_att, ctx, vector_terms.reshape(2 * groups, width), depth
    )
    attn_grad = scatter_group(place, attn_send, attn_keep)
    grad_in = d_first_in + part.astype(F32) + place.core_swap(part).astype(F32)

    def hand_back(full):
        mine = lax.dynamic_slice_in_dim(full, core * 2 * block, 2 * block, 0)
        mine = mine.reshape(2, block, width)
        kept = keep(mine, row)
        got = place.row_swap(keep(mine, 1 - row).astype(BF)).astype(full.dtype)
        return jnp.where(row == 0, jnp.stack([kept, got]), jnp.stack([got, kept]))

    grad_qkv = jnp.stack(
        [attn_grad[:depth, t * head_cols : (t + 1) * head_cols] for t in range(3)]
    )
    grad_out = jnp.transpose(attn_grad[:depth, 3 * head_cols :])
    vector_grad = attn_grad[depth]
    norm_grad = vector_grad[share : share + 6 * small].reshape(6, small)
    return (
        hand_back(result),
        hand_back(grad_in),
        grad_qkv,
        grad_out,
        grad_up,
        jnp.transpose(grad_down),
        vector_grad[None, :share],
        norm_grad[:2],
        norm_grad[2:],
    )

def solution(mesh):
    placed = (
        P("dp", "mp", None),
        P(None, "dp", "mp"),
        P("mp", "dp"),
        P("dp", "mp"),
        P("mp", "dp"),
        P("mp", "dp"),
        P(None, ("dp", "mp")),
        P(None, ("dp", "mp")),
        P("dp", None),
        P("dp", "mp", None),
    )
    return jax.shard_map(
        body,
        mesh=mesh,
        in_specs=placed,
        out_specs=(
            P("dp", "mp", None),
            P("dp", "mp", None),
            P(None, "dp", "mp"),
            P("mp", "dp"),
            P("dp", "mp"),
            P("mp", "dp"),
            P("mp", "dp"),
            P(None, ("dp", "mp")),
            P(None, ("dp", "mp")),
        ),
        check_vma=False,
    )
```

time: 341 us -> 275 us (0.81)
  Pallas kernels: 0 us -> 98.1 us
  local copies, waits for them, and re-layouts: 103 us -> 23.4 us
  matrix products: 51.4 us -> 0 us
  other arithmetic: 46 us -> 20.2 us
  starting transfers between devices: 58 us -> 42.7 us
  waiting for transfers between devices: 76.8 us -> 88.7 us
    pallas_call x0 -> x13, Pallas kernels: none -> 98.1 us  [call(): pl.pallas_call(kernel, out_shape=[jax.ShapeDtypeStruct(shape, kind) for s...]
    dot_general x33 -> x0, matrix products: 45.1 us -> none  [the longest x28 35.9 us: dot(): lax.dot_general(left, right, (dims, ((), ())), preferred_element_type=F32)]
    dynamic_update_slice x46 -> x0, local copies, waits for them, and re-layouts: 25.6 us -> none  [gather_group(): lax.dynamic_update_slice(whole, piece[step][None, None, None], start)]
    ppermute x18, waiting for transfers between devices: 20.7 us -> 37.7 us  [line_swap(): return lax.ppermute(value, 'dp', pairs)]
    ppermute x12, waiting for transfers between devices: 54.5 us -> 37.6 us  [cross(): return lax.ppermute(value, ('dp', 'mp'), pairs)]
    convert_element_type x14 -> x6, other arithmetic: 17.4 us -> 1.14 us  [the longest x3 0.69 us: scatter_line(): low = terms.astype(BF)]
    ppermute x18, starting transfers between devices: 38.6 us -> 25.2 us  [line_swap(): return lax.ppermute(value, 'dp', pairs)]
    slice x20 -> x8, local copies, waits for them, and re-layouts: 18.6 us -> 6.09 us  [the longest x1 1.33 us: body(): totals_two[1]]
  transfers between devices with their start and end apart: 39 -> 39, of which waited for: 11 -> 16; matrix products, arithmetic and copies ran while one was open for 36% -> 12% of each run, Pallas kernels for 0% -> 23%
where the time goes in v2:
time: 275 us; the launch traced here: 274 us
  Pallas kernels  98.1 us (36%)
  waiting for transfers between devices  88.7 us (32%)
  starting transfers between devices  42.7 us (16%)
  local copies, waits for them, and re-layouts  23.4 us (9%)
  other arithmetic  20.2 us (7%)
    pallas_call x13, Pallas kernels, call(): pl.pallas_call(kernel, out_shape=[jax.ShapeDtypeStruct(shape, kind) for s...  98.1 us
    ppermute x18, waiting for transfers between devices, line_swap(): return lax.ppermute(value, 'dp', pairs)  37.7 us
    ppermute x12, waiting for transfers between devices, cross(): return lax.ppermute(value, ('dp', 'mp'), pairs)  37.6 us
    ppermute x18, starting transfers between devices, line_swap(): return lax.ppermute(value, 'dp', pairs)  25.2 us
    ppermute x12, starting transfers between devices, cross(): return lax.ppermute(value, ('dp', 'mp'), pairs)  13.9 us
    ppermute x3, waiting for transfers between devices, row_swap(): return lax.ppermute(value, 'mp', [(0, 2), (2, 0), (1, 3), (3, 1)])  10.9 us
    another operation x4, other arithmetic, gather_group(): rest = place.cross(jnp.stack([own, first]), 1)  5.56 us
  transfers between devices with their start and end apart: 39, of which 16 were waited for; matrix products, arithmetic and copies ran while one was open for 12% of the time, Pallas kernels for 23%

profile of v2, /device:TPU:0, one launch (start us, length us, event | category | flops | bytes accessed | tf_op | source)
XLA Modules:
  0.0 274.2 jit_solution(12287356685155294968)
XLA Ops:
  4.8 5.1 %collective-permute-start.4 = (bf16[112,768]{1,0:T(8,128)(2,1)S(1)}, bf16[112,768]{1,0:T(8,128)(2,1)S(1)}, u32[]{:S(2)}, u32[]{:S(2)}) collective-permute-start(bf16[112,768]{1,0:T(8,128)(2,1)S(1)} %fusion.16), channel_id=1, source_target_pairs={{0,24},{4,28},{8,16},{12,20},{16,8},{20,12},{24,0},{28,4},{1,25},{... | collective-permute-start | bytes 516104 | tf_op jit(solution)/shard_map/ppermute | solution.py:58
  15.2 9.3 %collective-permute-done.3 = bf16[112,768]{1,0:T(8,128)(2,1)S(1)} collective-permute-done((bf16[112,768]{1,0:T(8,128)(2,1)S(1)}, bf16[112,768]{1,0:T(8,128)(2,1)S(1)}, u32[]{:S(2)}, u32[]{:S(2)}) %collective-permute-start.3) | collective-permute-done | bytes 172064 | tf_op jit(solution)/shard_map/ppermute | solution.py:58
  30.6 4.2 %collective-permute-done.11 = bf16[96,768]{1,0:T(8,128)(2,1)S(1)} collective-permute-done((bf16[96,768]{1,0:T(8,128)(2,1)S(1)}, bf16[96,768]{1,0:T(8,128)(2,1)S(1)}, u32[]{:S(2)}, u32[]{:S(2)}) %collective-permute-start.11) | collective-permute-done | bytes 147488 | tf_op jit(solution)/shard_map/ppermute | solution.py:58
  34.8 5.1 %collective-permute-done.10 = bf16[96,768]{1,0:T(8,128)(2,1)S(1)} collective-permute-done((bf16[96,768]{1,0:T(8,128)(2,1)S(1)}, bf16[96,768]{1,0:T(8,128)(2,1)S(1)}, u32[]{:S(2)}, u32[]{:S(2)}) %collective-permute-start.10) | collective-permute-done | bytes 147488 | tf_op jit(solution)/shard_map/ppermute | solution.py:58
  50.0 3.9 %collective-permute-done.15 = bf16[96,768]{1,0:T(8,128)(2,1)S(1)} collective-permute-done((bf16[96,768]{1,0:T(8,128)(2,1)}, bf16[96,768]{1,0:T(8,128)(2,1)S(1)}, u32[]{:S(2)}, u32[]{:S(2)}) %collective-permute-start.15) | collective-permute-done | bytes 147488 | tf_op jit(solution)/shard_map/ppermute | solution.py:58
  60.3 11.7 %collective-permute-done.17.first = bf16[4,96,768]{2,1,0:T(8,128)(2,1)S(1)} collective-permute-done((bf16[4,96,768]{2,1,0:T(8,128)(2,1)S(1)}, bf16[4,96,768]{2,1,0:T(8,128)(2,1)S(1)}, u32[]{:S(2)}, u32[]{:S(2)}) %collective-permute-start.17) | collective-permute-done | bytes 589856 | tf_op jit(solution)/shard_map/ppermute | solution.py:68
  76.9 3.5 %shard_map.169 = (bf16[2,768,768]{2,1,0:T(8,128)(2,1)}, bf16[2,8,16,768]{3,2,1,0:T(8,128)(2,1)}) custom-call(s32[9]{0:T(128)} %stack.252.where, bf16[4,112,768]{2,1,0:T(8,128)(2,1)} %copy-done.2, bf16[4,112,768]{2,1,0:T(8,128)(2,1)} %copy-done.4, bf16[2,4,112,768]{3,2,1,0:T(8,128)(2,1)} %collective-permute-done.6.rest), custom_call_target="tpu_custom_call" | custom-call | bytes 2752548 | tf_op jit(solution)/shard_map/pallas_call | solution.py:26
  82.8 16.9 %shard_map.170 = (bf16[768,1536]{1,0:T(8,128)(2,1)}, bf16[512,1152]{1,0:T(8,128)(2,1)}, bf16[6,512,512]{2,1,0:T(8,128)(2,1)}, bf16[512,384]{1,0:T(8,128)(2,1)}, bf16[512,768]{1,0:T(8,128)(2,1)}) custom-call(s32[4]{0:T(128)} %bitcast.171, bf16[512,768]{1,0:T(8,128)(2,1)} %get-tuple-element.108.x, bf16[2,768,768]{2,1,0:T(8,128)(2,1)} %get-tuple-element.46.weights, ...), custom_call_target="tpu_custom_call" | custom-call | flops 1207959552 | bytes 3148816 | tf_op jit(solution)/shard_map/pallas_call | solution.py:26
  99.8 3.3 %shard_map.171.weights.up = bf16[2,768,768]{2,1,0:T(8,128)(2,1)} custom-call(s32[9]{0:T(128)} %stack.252.where, bf16[4,96,768]{2,1,0:T(8,128)(2,1)} %copy-done.3, bf16[4,96,768]{2,1,0:T(8,128)(2,1)} %copy-done.6, bf16[2,4,96,768]{3,2,1,0:T(8,128)(2,1)} %collective-permute-done.13.rest), custom_call_target="tpu_custom_call" | custom-call | bytes 2359332 | tf_op jit(solution)/shard_map/pallas_call | solution.py:26
  104.3 3.3 %shard_map.173.weights.down = bf16[2,768,768]{2,1,0:T(8,128)(2,1)} custom-call(s32[9]{0:T(128)} %stack.252.where, bf16[4,96,768]{2,1,0:T(8,128)(2,1)} %copy-done.5, bf16[4,96,768]{2,1,0:T(8,128)(2,1)} %copy-done.7, bf16[2,4,96,768]{3,2,1,0:T(8,128)(2,1)} %collective-permute-done.18.rest), custom_call_target="tpu_custom_call" | custom-call | bytes 2359332 | tf_op jit(solution)/shard_map/pallas_call | solution.py:26
  109.4 12.0 %shard_map.172 = (f32[512,768]{1,0:T(8,128)}, f32[512,128]{1,0:T(8,128)}, bf16[512,768]{1,0:T(8,128)(2,1)}, bf16[512,1536]{1,0:T(8,128)(2,1)}, bf16[512,1536]{1,0:T(8,128)(2,1)}) custom-call(bf16[512,768]{1,0:T(8,128)(2,1)} %get-tuple-element.108.x, bf16[512,768]{1,0:T(8,128)(2,1)} %get-tuple-element.48.mine, bf16[512,768]{1,0:T(8,128)(2,1)} %copy-done.12, ...), custom_call_target="tpu_custom_call" | custom-call | flops 1207959552 | bytes 4749312 | tf_op jit(solution)/shard_map/pallas_call | solution.py:26
  121.3 4.5 %shard_map.174.mine = bf16[512,768]{1,0:T(8,128)(2,1)} custom-call(bf16[512,1536]{1,0:T(8,128)(2,1)} %get-tuple-element.52.activated.right, bf16[2,768,768]{2,1,0:T(8,128)(2,1)} %shard_map.173.weights.down), custom_call_target="tpu_custom_call" | custom-call | flops 1207959552 | bytes 3932160 | tf_op jit(solution)/shard_map/pallas_call | solution.py:26
  129.2 8.7 %shard_map.175 = (bf16[512,768]{1,0:T(8,128)(2,1)}, f32[512,768]{1,0:T(8,128)}, bf16[512,768]{1,0:T(8,128)(2,1)}, f32[8,768]{1,0:T(8,128)}) custom-call(f32[512,768]{1,0:T(8,128)} %get-tuple-element.51.unit, bf16[512,768]{1,0:T(8,128)(2,1)} %shard_map.174.mine, bf16[512,768]{1,0:T(8,128)(2,1)} %copy-done.14, bf16[512,768]{1,0:T(8,128)(2,1)} %get-tuple-element.107.grad, ...), custom_call_target="tpu_custom_call" | custom-call | flops 23592960 | bytes 3956736 | tf_op jit(solution)/shard_map/pallas_call | solution.py:26
  137.9 8.7 %shard_map.176 = (bf16[512,1536]{1,0:T(8,128)(2,1)}, bf16[512,768]{1,0:T(8,128)(2,1)}, f32[8,1536]{1,0:T(8,128)}) custom-call(bf16[512,768]{1,0:T(8,128)(2,1)} %get-tuple-element.56.d_mixed.left, bf16[2,768,768]{2,1,0:T(8,128)(2,1)} %shard_map.173.weights.down, bf16[2,768,768]{2,1,0:T(8,128)(2,1)} %shard_map.171.weights.up, ...), custom_call_target="tpu_custom_call" | custom-call | flops 2415919104 | bytes 7077888 | tf_op jit(solution)/shard_map/pallas_call | solution.py:26
  147.4 5.4 %shard_map.180 = (bf16[2,4,96,768]{3,2,1,0:T(8,128)(2,1)}, bf16[2,4,96,768]{3,2,1,0:T(8,128)(2,1)}) custom-call(s32[9]{0:T(128)} %stack.304.table, bf16[512,768]{1,0:T(8,128)(2,1)} %get-tuple-element.75.left, bf16[512,1536]{1,0:T(8,128)(2,1)} %get-tuple-element.76.right), custom_call_target="tpu_custom_call" | custom-call | flops 1207959552 | bytes 2359332 | tf_op jit(solution)/shard_map/pallas_call | solution.py:26
  155.0 5.3 %shard_map.181 = (bf16[2,4,96,768]{3,2,1,0:T(8,128)(2,1)}, bf16[2,4,96,768]{3,2,1,0:T(8,128)(2,1)}) custom-call(s32[9]{0:T(128)} %stack.304.table, bf16[512,768]{1,0:T(8,128)(2,1)} %get-tuple-element.56.d_mixed.left, bf16[512,1536]{1,0:T(8,128)(2,1)} %get-tuple-element.52.activated.right), custom_call_target="tpu_custom_call" | custom-call | flops 1207959552 | bytes 2359332 | tf_op jit(solution)/shard_map/pallas_call | solution.py:26
  165.3 8.2 %collective-permute-done.20 = bf16[128,768]{1,0:T(8,128)(2,1)} collective-permute-done((bf16[128,768]{1,0:T(8,128)(2,1)S(1)}, bf16[128,768]{1,0:T(8,128)(2,1)}, u32[]{:S(2)}, u32[]{:S(2)}) %collective-permute-start.20) | collective-permute-done | bytes 196640 | tf_op jit(solution)/shard_map/ppermute | solution.py:54
  176.3 7.1 %shard_map.177 = (f32[512,768]{1,0:T(8,128)}, bf16[512,768]{1,0:T(8,128)(2,1)}, bf16[512,384]{1,0:T(8,128)(2,1)}, f32[8,768]{1,0:T(8,128)}) custom-call(f32[512,768]{1,0:T(8,128)} %get-tuple-element.55.d_second, bf16[512,768]{1,0:T(8,128)(2,1)} %get-tuple-element.58.mine, bf16[512,768]{1,0:T(8,128)(2,1)} %copy-done.13, f32[512,768]{1,0:T(8,128)} %get-tuple-element.51.unit, ...), custom_call_target="tpu_custom_call" | custom-call | flops 301989888 | bytes 7364608 | tf_op jit(solution)/shard_map/pallas_call | solution.py:26
  184.9 13.9 %shard_map.178 = (bf16[512,1152]{1,0:T(8,128)(2,1)}, f32[8,768]{1,0:T(8,128)}, bf16[512,768]{1,0:T(8,128)(2,1)}) custom-call(bf16[512,384]{1,0:T(8,128)(2,1)} %get-tuple-element.62.d_ctx, bf16[512,1152]{1,0:T(8,128)(2,1)} %get-tuple-element.63.qkv, bf16[6,512,512]{2,1,0:T(8,128)(2,1)} %get-tuple-element.64.probs, bf16[512,384]{1,0:T(8,128)(2,1)} %get-tuple-element.65.ctx, ...), custom_call_target="tpu_custom_call" | custom-call | flops 1509949440 | bytes 7471104 | tf_op jit(solution)/shard_map/pallas_call | solution.py:26
  201.0 5.6 %shard_map.179 = (bf16[2,4,112,768]{3,2,1,0:T(8,128)(2,1)}, bf16[2,4,112,768]{3,2,1,0:T(8,128)(2,1)}) custom-call(s32[9]{0:T(128)} %stack.304.table, bf16[512,768]{1,0:T(8,128)(2,1)} %get-tuple-element.108.x, bf16[512,1152]{1,0:T(8,128)(2,1)} %get-tuple-element.67.d_qkv, bf16[512,768]{1,0:T(8,128)(2,1)} %get-tuple-element.68.d_att, ...), custom_call_target="tpu_custom_call" | custom-call | flops 1207959552 | bytes 3194916 | tf_op jit(solution)/shard_map/pallas_call | solution.py:26
  212.4 12.2 %collective-permute-done.30 = bf16[4,96,768]{2,1,0:T(8,128)(2,1)S(1)} collective-permute-done((bf16[4,96,768]{2,1,0:T(8,128)(2,1)S(1)}, bf16[4,96,768]{2,1,0:T(8,128)(2,1)S(1)}, u32[]{:S(2)}, u32[]{:S(2)}) %collective-permute-start.30) | collective-permute-done | bytes 589856 | tf_op jit(solution)/shard_map/ppermute | solution.py:68
  226.6 10.6 %collective-permute-done.35 = bf16[4,96,768]{2,1,0:T(8,128)(2,1)S(1)} collective-permute-done((bf16[4,96,768]{2,1,0:T(8,128)(2,1)S(1)}, bf16[4,96,768]{2,1,0:T(8,128)(2,1)S(1)}, u32[]{:S(2)}, u32[]{:S(2)}) %collective-permute-start.35) | collective-permute-done | bytes 589856 | tf_op jit(solution)/shard_map/ppermute | solution.py:68
  255.5 9.1 %collective-permute-done.37 = bf16[96,768]{1,0:T(8,128)(2,1)S(1)} collective-permute-done((bf16[96,768]{1,0:T(8,128)(2,1)S(1)}, bf16[96,768]{1,0:T(8,128)(2,1)S(1)}, u32[]{:S(2)}, u32[]{:S(2)}) %collective-permute-start.37) | collective-permute-done | bytes 147488 | tf_op jit(solution)/shard_map/ppermute | solution.py:58
  265.4 5.0 %collective-permute-done.27 = bf16[112,768]{1,0:T(8,128)(2,1)S(1)} collective-permute-done((bf16[112,768]{1,0:T(8,128)(2,1)S(1)}, bf16[112,768]{1,0:T(8,128)(2,1)S(1)}, u32[]{:S(2)}, u32[]{:S(2)}) %collective-permute-start.27) | collective-permute-done | bytes 172064 | tf_op jit(solution)/shard_map/ppermute | solution.py:58
  (194 shorter events, 90.6 us)
Async XLA Ops:
  9.9 14.6 %collective-permute-start.3 = (bf16[112,768]{1,0:T(8,128)(2,1)S(1)}, bf16[112,768]{1,0:T(8,128)(2,1)S(1)}, u32[]{:S(2)}, u32[]{:S(2)}) collective-permute-start(bf16[112,768]{1,0:T(8,128)(2,1)S(1)} %fusion.16), channel_id=1, source_target_pairs={{0,16},{4,20},{8,24},{12,28},{16,0},{20,4},{24,8},{28,12},{1,17},{... | collective-permute-start | bytes 516104 | tf_op jit(solution)/shard_map/ppermute | solution.py:58
  9.9 14.6 %collective-permute-start.2 = (bf16[112,768]{1,0:T(8,128)(2,1)S(1)}, bf16[112,768]{1,0:T(8,128)(2,1)S(1)}, u32[]{:S(2)}, u32[]{:S(2)}) collective-permute-start(bf16[112,768]{1,0:T(8,128)(2,1)S(1)} %fusion.16), channel_id=1, source_target_pairs={{0,8},{4,12},{8,0},{12,4},{16,24},{20,28},{24,16},{28,20},{1,9},{5... | collective-permute-start | bytes 516104 | tf_op jit(solution)/shard_map/ppermute | solution.py:58
  12.6 31.9 %collective-permute-start = (bf16[2,128,768]{2,1,0:T(8,128)(2,1)S(1)}, bf16[2,128,768]{2,1,0:T(8,128)(2,1)}, u32[]{:S(2)}, u32[]{:S(2)}) collective-permute-start(bf16[2,128,768]{2,1,0:T(8,128)(2,1)S(1)} %pad_maximum_fusion.8), channel_id=1, source_target_pairs={{0,2},{2,0},{1,3},{3,1},{4,6},{6,4},{5,7},{7,5},{8,10},{10,8},{9,1... | collective-permute-start | bytes 1179656 | tf_op jit(solution)/shard_map/ppermute | solution.py:54
  24.6 22.7 %collective-permute-start.5 = (bf16[4,112,768]{2,1,0:T(8,128)(2,1)S(1)}, bf16[4,112,768]{2,1,0:T(8,128)(2,1)S(1)}, u32[]{:S(2)}, u32[]{:S(2)}) collective-permute-start(bf16[4,112,768]{2,1,0:T(8,128)(2,1)S(1)} %pad_maximum_fusion.4.own), channel_id=1, source_target_pairs={{0,2},{1,5},{2,0},{3,7},{4,6},{5,1},{6,4},{7,3},{8,10},{9,13},{10,... | collective-permute-start | bytes 2064392 | tf_op jit(solution)/shard_map/ppermute | solution.py:68
  47.3 26.4 %collective-permute-start.1 = (bf16[2,256,768]{2,1,0:T(8,128)(2,1)}, bf16[2,256,768]{2,1,0:T(8,128)(2,1)}, u32[]{:S(2)}, u32[]{:S(2)}) collective-permute-start(bf16[2,256,768]{2,1,0:T(8,128)(2,1)} %pad_maximum_fusion.3), channel_id=1, source_target_pairs={{0,1},{1,0},{2,3},{3,2},{4,5},{5,4},{6,7},{7,6},{8,9},{9,8},{10,11... | collective-permute-start | bytes 2359304 | tf_op jit(solution)/shard_map/ppermute | solution.py:51
  48.9 28.0 %collective-permute-start.6 = (bf16[2,4,112,768]{3,2,1,0:T(8,128)(2,1)}, bf16[2,4,112,768]{3,2,1,0:T(8,128)(2,1)}, u32[]{:S(2)}, u32[]{:S(2)}) collective-permute-start(bf16[2,4,112,768]{3,2,1,0:T(8,128)(2,1)} %pad_maximum_fusion), channel_id=1, source_target_pairs={{0,4},{1,3},{2,6},{3,1},{4,0},{5,7},{6,2},{7,5},{8,12},{9,11},{10,... | collective-permute-start | bytes 4128776 | tf_op jit(solution)/shard_map/ppermute | solution.py:68
  55.7 16.3 %collective-permute-start.17 = (bf16[4,96,768]{2,1,0:T(8,128)(2,1)S(1)}, bf16[4,96,768]{2,1,0:T(8,128)(2,1)S(1)}, u32[]{:S(2)}, u32[]{:S(2)}) collective-permute-start(bf16[4,96,768]{2,1,0:T(8,128)(2,1)S(1)} %get-tuple-element.121.own), channel_id=1, source_target_pairs={{0,2},{1,5},{2,0},{3,7},{4,6},{5,1},{6,4},{7,3},{8,10},{9,13},{10,... | collective-permute-start | bytes 1769480 | tf_op jit(solution)/shard_map/ppermute | solution.py:68
  59.8 40.0 %collective-permute-start.13 = (bf16[2,4,96,768]{3,2,1,0:T(8,128)(2,1)}, bf16[2,4,96,768]{3,2,1,0:T(8,128)(2,1)}, u32[]{:S(2)}, u32[]{:S(2)}) collective-permute-start(bf16[2,4,96,768]{3,2,1,0:T(8,128)(2,1)} %pad_maximum_fusion.1), channel_id=1, source_target_pairs={{0,4},{1,3},{2,6},{3,1},{4,0},{5,7},{6,2},{7,5},{8,12},{9,11},{10,... | collective-permute-start | bytes 3538952 | tf_op jit(solution)/shard_map/ppermute | solution.py:68
  73.2 31.1 %collective-permute-start.18 = (bf16[2,4,96,768]{3,2,1,0:T(8,128)(2,1)}, bf16[2,4,96,768]{3,2,1,0:T(8,128)(2,1)}, u32[]{:S(2)}, u32[]{:S(2)}) collective-permute-start(bf16[2,4,96,768]{3,2,1,0:T(8,128)(2,1)} %pad_maximum_fusion.2), channel_id=1, source_target_pairs={{0,4},{1,3},{2,6},{3,1},{4,0},{5,7},{6,2},{7,5},{8,12},{9,11},{10,... | collective-permute-start | bytes 3538952 | tf_op jit(solution)/shard_map/ppermute | solution.py:68
  146.6 28.8 %collective-permute-start.21 = (bf16[512,768]{1,0:T(8,128)(2,1)}, bf16[512,768]{1,0:T(8,128)(2,1)S(1)}, u32[]{:S(2)}, u32[]{:S(2)}) collective-permute-start(bf16[512,768]{1,0:T(8,128)(2,1)} %get-tuple-element.58.mine), channel_id=1, source_target_pairs={{0,1},{1,0},{2,3},{3,2},{4,5},{5,4},{6,7},{7,6},{8,9},{9,8},{10,11... | collective-permute-start | bytes 2359304 | tf_op jit(solution)/shard_map/ppermute | solution.py:51
  152.8 55.2 %collective-permute-start.29 = (bf16[2,4,96,768]{3,2,1,0:T(8,128)(2,1)}, bf16[2,4,96,768]{3,2,1,0:T(8,128)(2,1)S(1)}, u32[]{:S(2)}, u32[]{:S(2)}) collective-permute-start(bf16[2,4,96,768]{3,2,1,0:T(8,128)(2,1)} %get-tuple-element.78), channel_id=1, source_target_pairs={{0,2},{1,5},{2,0},{3,7},{4,6},{5,1},{6,4},{7,3},{8,10},{9,13},{10,... | collective-permute-start | bytes 3538952 | tf_op jit(solution)/shard_map/ppermute | solution.py:68
  154.4 19.1 %collective-permute-start.20 = (bf16[128,768]{1,0:T(8,128)(2,1)S(1)}, bf16[128,768]{1,0:T(8,128)(2,1)}, u32[]{:S(2)}, u32[]{:S(2)}) collective-permute-start(bf16[128,768]{1,0:T(8,128)(2,1)S(1)} %get-tuple-element.123), channel_id=1, source_target_pairs={{0,2},{2,0},{1,3},{3,1},{4,6},{6,4},{5,7},{7,5},{8,10},{10,8},{9,1... | collective-permute-start | bytes 589832 | tf_op jit(solution)/shard_map/ppermute | solution.py:54
  160.3 49.1 %collective-permute-start.34 = (bf16[2,4,96,768]{3,2,1,0:T(8,128)(2,1)}, bf16[2,4,96,768]{3,2,1,0:T(8,128)(2,1)S(1)}, u32[]{:S(2)}, u32[]{:S(2)}) collective-permute-start(bf16[2,4,96,768]{3,2,1,0:T(8,128)(2,1)} %get-tuple-element.80), channel_id=1, source_target_pairs={{0,2},{1,5},{2,0},{3,7},{4,6},{5,1},{6,4},{7,3},{8,10},{9,13},{10,... | collective-permute-start | bytes 3538952 | tf_op jit(solution)/shard_map/ppermute | solution.py:68
  206.6 33.0 %collective-permute-start.24 = (bf16[2,4,112,768]{3,2,1,0:T(8,128)(2,1)}, bf16[2,4,112,768]{3,2,1,0:T(8,128)(2,1)S(1)}, u32[]{:S(2)}, u32[]{:S(2)}) collective-permute-start(bf16[2,4,112,768]{3,2,1,0:T(8,128)(2,1)} %get-tuple-element.74), channel_id=1, source_target_pairs={{0,2},{1,5},{2,0},{3,7},{4,6},{5,1},{6,4},{7,3},{8,10},{9,13},{10,... | collective-permute-start | bytes 4128776 | tf_op jit(solution)/shard_map/ppermute | solution.py:68
  208.2 16.3 %collective-permute-start.30 = (bf16[4,96,768]{2,1,0:T(8,128)(2,1)S(1)}, bf16[4,96,768]{2,1,0:T(8,128)(2,1)S(1)}, u32[]{:S(2)}, u32[]{:S(2)}) collective-permute-start(bf16[4,96,768]{2,1,0:T(8,128)(2,1)S(1)} %fusion.2), channel_id=1, source_target_pairs={{0,4},{1,3},{2,6},{3,1},{4,0},{5,7},{6,2},{7,5},{8,12},{9,11},{10,... | collective-permute-start | bytes 1769480 | tf_op jit(solution)/shard_map/ppermute | solution.py:68
  209.6 27.6 %collective-permute-start.35 = (bf16[4,96,768]{2,1,0:T(8,128)(2,1)S(1)}, bf16[4,96,768]{2,1,0:T(8,128)(2,1)S(1)}, u32[]{:S(2)}, u32[]{:S(2)}) collective-permute-start(bf16[4,96,768]{2,1,0:T(8,128)(2,1)S(1)} %fusion.3), channel_id=1, source_target_pairs={{0,4},{1,3},{2,6},{3,1},{4,0},{5,7},{6,2},{7,5},{8,12},{9,11},{10,... | collective-permute-start | bytes 1769480 | tf_op jit(solution)/shard_map/ppermute | solution.py:68
  211.8 31.9 %collective-permute-start.23 = (bf16[128,768]{1,0:T(8,128)(2,1)S(1)}, bf16[128,768]{1,0:T(8,128)(2,1)S(1)}, u32[]{:S(2)}, u32[]{:S(2)}) collective-permute-start(bf16[128,768]{1,0:T(8,128)(2,1)S(1)} %fusion.15), channel_id=1, source_target_pairs={{0,2},{2,0},{1,3},{3,1},{4,6},{6,4},{5,7},{7,5},{8,10},{10,8},{9,1... | collective-permute-start | bytes 589832 | tf_op jit(solution)/shard_map/ppermute | solution.py:54
  224.8 21.8 %collective-permute-start.33 = (bf16[96,768]{1,0:T(8,128)(2,1)S(1)}, bf16[96,768]{1,0:T(8,128)(2,1)S(1)}, u32[]{:S(2)}, u32[]{:S(2)}) collective-permute-start(bf16[96,768]{1,0:T(8,128)(2,1)S(1)} %get-tuple-element.118), channel_id=1, source_target_pairs={{0,24},{4,28},{8,16},{12,20},{16,8},{20,12},{24,0},{28,4},{1,25},{... | collective-permute-start | bytes 442376 | tf_op jit(solution)/shard_map/ppermute | solution.py:58
  226.6 20.1 %collective-permute-start.32 = (bf16[96,768]{1,0:T(8,128)(2,1)S(1)}, bf16[96,768]{1,0:T(8,128)(2,1)S(1)}, u32[]{:S(2)}, u32[]{:S(2)}) collective-permute-start(bf16[96,768]{1,0:T(8,128)(2,1)S(1)} %get-tuple-element.119), channel_id=1, source_target_pairs={{0,16},{4,20},{8,24},{12,28},{16,0},{20,4},{24,8},{28,12},{1,17},{... | collective-permute-start | bytes 442376 | tf_op jit(solution)/shard_map/ppermute | solution.py:58
  246.6 18.0 %collective-permute-start.37 = (bf16[96,768]{1,0:T(8,128)(2,1)S(1)}, bf16[96,768]{1,0:T(8,128)(2,1)S(1)}, u32[]{:S(2)}, u32[]{:S(2)}) collective-permute-start(bf16[96,768]{1,0:T(8,128)(2,1)S(1)} %get-tuple-element.116), channel_id=1, source_target_pairs={{0,16},{4,20},{8,24},{12,28},{16,0},{20,4},{24,8},{28,12},{1,17},{... | collective-permute-start | bytes 442376 | tf_op jit(solution)/shard_map/ppermute | solution.py:58
  246.7 17.9 %collective-permute-start.36 = (bf16[96,768]{1,0:T(8,128)(2,1)S(1)}, bf16[96,768]{1,0:T(8,128)(2,1)S(1)}, u32[]{:S(2)}, u32[]{:S(2)}) collective-permute-start(bf16[96,768]{1,0:T(8,128)(2,1)S(1)} %get-tuple-element.114), channel_id=1, source_target_pairs={{0,8},{4,12},{8,0},{12,4},{16,24},{20,28},{24,16},{28,20},{1,9},{5... | collective-permute-start | bytes 442376 | tf_op jit(solution)/shard_map/ppermute | solution.py:58
  251.0 14.3 %collective-permute-start.28 = (bf16[112,768]{1,0:T(8,128)(2,1)S(1)}, bf16[112,768]{1,0:T(8,128)(2,1)S(1)}, u32[]{:S(2)}, u32[]{:S(2)}) collective-permute-start(bf16[112,768]{1,0:T(8,128)(2,1)S(1)} %get-tuple-element.112), channel_id=1, source_target_pairs={{0,24},{4,28},{8,16},{12,20},{16,8},{20,12},{24,0},{28,4},{1,25},{... | collective-permute-start | bytes 516104 | tf_op jit(solution)/shard_map/ppermute | solution.py:58
  253.2 17.3 %collective-permute-start.27 = (bf16[112,768]{1,0:T(8,128)(2,1)S(1)}, bf16[112,768]{1,0:T(8,128)(2,1)S(1)}, u32[]{:S(2)}, u32[]{:S(2)}) collective-permute-start(bf16[112,768]{1,0:T(8,128)(2,1)S(1)} %get-tuple-element.113), channel_id=1, source_target_pairs={{0,16},{4,20},{8,24},{12,28},{16,0},{20,4},{24,8},{28,12},{1,17},{... | collective-permute-start | bytes 516104 | tf_op jit(solution)/shard_map/ppermute | solution.py:58
  253.2 17.3 %collective-permute-start.26 = (bf16[112,768]{1,0:T(8,128)(2,1)S(1)}, bf16[112,768]{1,0:T(8,128)(2,1)S(1)}, u32[]{:S(2)}, u32[]{:S(2)}) collective-permute-start(bf16[112,768]{1,0:T(8,128)(2,1)S(1)} %get-tuple-element.111), channel_id=1, source_target_pairs={{0,8},{4,12},{8,0},{12,4},{16,24},{20,28},{24,16},{28,20},{1,9},{5... | collective-permute-start | bytes 516104 | tf_op jit(solution)/shard_map/ppermute | solution.py:58
  (36 other events, 370.9 us)

commit v3 on v2

v3 whole, which is shorter than its diff:
```python
import functools

import jax
import jax.numpy as jnp
from jax import lax
from jax.experimental import pallas as pl
from jax.experimental.pallas import tpu as pltpu
from jax.sharding import PartitionSpec as P

HD = 64
LANES = 128
EXTRA = 16
BF = jnp.bfloat16
F32 = jnp.float32
LIMIT = 56 * 1024 * 1024
NN = ((1,), (0,))
NT = ((1,), (1,))
TN = ((0,), (0,))


def dot(left, right, dims=NN):
    return lax.dot_general(left, right, (dims, ((), ())), preferred_element_type=F32)


def call(kernel, outs, args, scalars=0, scratch=(), steps=None):
    args = [arg if isinstance(arg, tuple) else (arg, False) for arg in args]
    outs = [out if len(out) == 3 else out + (False,) for out in outs]

    def spec(shape, cut):
        if steps is None:
            return pl.BlockSpec(memory_space=pltpu.VMEM)
        if cut:
            rest = (0,) * (len(shape) - 1)
            return pl.BlockSpec((shape[0] // steps,) + tuple(shape[1:]), lambda i: (i,) + rest)
        return pl.BlockSpec(tuple(shape), lambda i: (0,) * len(shape))

    return pl.pallas_call(
        kernel,
        out_shape=[jax.ShapeDtypeStruct(shape, kind) for shape, kind, _ in outs],
        grid=() if steps is None else (steps,),
        in_specs=[pl.BlockSpec(memory_space=pltpu.SMEM)] * scalars
        + [spec(arg.shape, cut) for arg, cut in args[scalars:]],
        out_specs=[spec(shape, cut) for shape, _, cut in outs],
        scratch_shapes=list(scratch),
        compiler_params=pltpu.CompilerParams(vmem_limit_bytes=LIMIT),
        cost_estimate=pl.CostEstimate(flops=0, bytes_accessed=0, transcendentals=0),
    )(*[arg for arg, _ in args])


def after(value, *others):
    return lax.optimization_barrier((value,) + others)[0]


class Place:
    def __init__(self):
        self.groups = lax.axis_size("dp")
        self.line_size = self.groups // 2
        data, model = lax.axis_index("dp"), lax.axis_index("mp")
        self.line, self.pair = data // 2, data % 2
        self.row, self.core = model // 2, model % 2

    def core_swap(self, value):
        return lax.ppermute(value, "mp", [(0, 1), (1, 0), (2, 3), (3, 2)])

    def row_swap(self, value):
        return lax.ppermute(value, "mp", [(0, 2), (2, 0), (1, 3), (3, 1)])

    def line_swap(self, value, step):
        pairs = [(i, i ^ (2 * step)) for i in range(self.groups)]
        return lax.ppermute(value, "dp", pairs)

    def cross(self, value, along_row):
        pairs = []
        for data in range(self.groups):
            for model in range(4):
                if model % 2 == along_row:
                    pairs.append((data * 4 + model, data * 4 + (model ^ 2)))
                else:
                    pairs.append((data * 4 + model, (data ^ 1) * 4 + model))
        return lax.ppermute(value, ("dp", "mp"), pairs)

    def quarters(self):
        other_row, other_pair = 1 - self.row, 1 - self.pair
        swap = self.core == 0
        first = (jnp.where(swap, other_row, self.row), jnp.where(swap, self.pair, other_pair))
        second = (jnp.where(swap, self.row, other_row), jnp.where(swap, other_pair, self.pair))
        return (self.row, self.pair), first, second, (other_row, other_pair)

    def roles(self):
        found = []
        for row in range(2):
            for pair in range(2):
                other_row, other_pair = self.row != row, self.pair != pair
                near, far = (other_row, other_pair)
                near = jnp.where(self.core == 0, other_row, other_pair)
                far = jnp.where(self.core == 0, other_pair, other_row)
                found.append(near.astype(jnp.int32) + 2 * far.astype(jnp.int32))
        return jnp.stack(found + [self.line, self.core]).astype(jnp.int32)


def line_parts(place, shard):
    n = place.line_size
    if n <= 4:
        return [shard] + [place.line_swap(shard, step) for step in range(1, n)]
    held, step = shard[None], 1
    while step < n:
        held, step = jnp.concatenate([held, place.line_swap(held, step)]), step * 2
    return [held[i] for i in range(n)]


def scatter_line(place, terms):
    n = place.line_size
    if n <= 4:
        low = terms.astype(BF)
        total = terms[0]
        for step in range(1, n):
            total = total + place.line_swap(low[step], step).astype(F32)
        return total
    step = n // 2
    while step:
        got = place.line_swap(terms[step:].astype(BF), step)
        terms, step = terms[:step] + got.astype(F32), step // 2
    return terms[0]


def place_kernel(depth, n, where, own, first, second, far, whole, extras=None):
    for quarter, source in enumerate((own, first, second, far)):
        row, pair = where[2 * quarter], where[2 * quarter + 1]
        for step in range(n):
            data = jnp.bitwise_xor(where[8], step) * 2 + pair
            start = pl.multiple_of(data * depth, 16)
            whole[row, pl.ds(start, depth), :] = source[step, :depth]
            if extras is not None:
                extras[row, data] = source[step, depth:]


def place_attn_kernel(depth, n, share, where, own, first, second, far, whole, extras, unit):
    place_kernel(depth, n, where, own, first, second, far, whole, extras)
    unit[...] = jnp.zeros_like(unit)
    for row in range(2):
        for data in range(2 * n):
            value = extras[row, data].astype(F32)
            unit[row : row + 1, data * share : (data + 1) * share] = value[0:1, :share]


def place_spots(place):
    spots = [scalar for spot in place.quarters() for scalar in spot] + [place.line]
    return jnp.stack(spots).astype(jnp.int32)


def place_group(place, quarters, depth, share=None):
    n, rows, width = quarters[0].shape
    kind = quarters[0].dtype
    outs = [((2, 2 * n * depth, width), kind)]
    if share is not None:
        outs += [((2, 2 * n, EXTRA, width), kind), ((8, 2 * n * share), F32)]
    if depth % 16 == 0:
        kernel = functools.partial(place_kernel, depth, n)
        if share is not None:
            kernel = functools.partial(place_attn_kernel, depth, n, share)
        return call(kernel, outs, [place_spots(place)] + list(quarters), scalars=1)
    whole = jnp.zeros((2, n, 2, rows, width), kind)
    for piece, (row, pair) in zip(quarters, place.quarters()):
        for step in range(n):
            start = (row, place.line ^ step, pair, 0, 0)
            whole = lax.dynamic_update_slice(whole, piece[step][None, None, None], start)
    out = [whole[:, :, :, :depth].reshape(outs[0][0])]
    if share is not None:
        extras = whole[:, :, :, depth:].reshape(outs[1][0])
        unit = extras[:, :, 0, :share].reshape(2, 2 * n * share).astype(F32)
        out += [extras, jnp.pad(unit, ((0, 6), (0, 0)))]
    return out


def spread(place, terms, depth, vectors=None):
    n = place.line_size
    terms = terms.reshape(2, n, 2, depth, terms.shape[-1])
    if vectors is not None:
        vectors = jnp.pad(vectors, ((0, 0), (0, 0), (0, terms.shape[-1] - vectors.shape[-1])))
        vectors = vectors.reshape(2, n, 2, EXTRA, -1)
        terms = jnp.concatenate([terms, vectors.astype(terms.dtype)], axis=3)
    order = lax.iota(jnp.int32, n) ^ place.line
    terms = jnp.take(terms, order, axis=1)

    def quarter(at):
        size = (1, n, 1) + terms.shape[3:]
        return lax.dynamic_slice(terms, (at[0], 0, at[1], 0, 0), size).reshape((n,) + terms.shape[3:])

    return [quarter(at) for at in place.quarters()]


def store_quarters(table, n, depth, row, value, refs, extra=None):
    for pair in range(2):
        role = table[row * 2 + pair]

        def put(ref):
            for line in range(n):
                at = jnp.bitwise_xor(table[4], line)
                data = line * 2 + pair
                ref[at, :depth] = value[data * depth : (data + 1) * depth]
                if extra is not None:
                    rows = extra(row, data)
                    known = rows.shape[1]
                    ref[at, depth:, :known] = rows
                    ref[at, depth:, known:] = jnp.zeros((EXTRA, ref.shape[2] - known), BF)

        for index in range(4):
            pl.when(role == index)(functools.partial(put, refs[index]))


def outer_kernel(n, depth, table, left, right, *refs):
    width = refs[0].shape[-1]
    turned = left[...].T
    for row in range(2):
        value = dot(turned, right[:, row * width : (row + 1) * width]).astype(BF)
        store_quarters(table, n, depth, row, value, refs)


def outer(place, table, left, right, depth):
    n, width = place.line_size, right.shape[1] // 2
    if depth % 16:
        halves = [dot(left, right[:, i * width : (i + 1) * width], TN).astype(BF) for i in range(2)]
        return spread(place, jnp.stack(halves), depth)
    shape = ((n, depth, width), BF)
    return call(
        functools.partial(outer_kernel, n, depth),
        [shape] * 4,
        [table, left, right],
        scalars=1,
    )


def by_row(value, row, cols):
    kinds = value.shape[1] // (2 * cols)
    return jnp.concatenate(
        [value[:, (2 * t + row) * cols : (2 * t + row + 1) * cols] for t in range(kinds)], axis=1
    )


def vector_rows(groups, cols, units, small, core, attn_sums, up_sums, totals_one, totals_two):
    share = (2 * cols + units) // groups
    known = -(-share // LANES) * LANES
    norms = jnp.concatenate(
        [totals_one[0:1], totals_two[0:1], totals_one[1:3], totals_two[1:3]], axis=0
    )

    def line(row):
        at = slice(row * cols, (row + 1) * cols)
        later = slice((2 + row) * cols, (3 + row) * cols)
        return jnp.concatenate(
            [attn_sums[0:1, at], attn_sums[0:1, later], up_sums[0:1, row * units : (row + 1) * units]], axis=1
        )

    lines = [line(row) for row in range(2)]

    def rows(row, data):
        first = lines[row][:, data * share : (data + 1) * share]
        start = (data * 4 + row * 2) * small
        norm = jnp.where(core == 0, norms[:, start : start + small], norms[:, start + small : start + 2 * small])
        return jnp.concatenate(
            [
                jnp.pad(first, ((0, 0), (0, known - share))),
                jnp.pad(norm, ((0, 0), (0, known - small))),
                jnp.zeros((EXTRA - 7, known), F32),
            ],
            axis=0,
        ).astype(BF)

    return rows


def outer_attn_kernel(n, depth, cols, table, x, d_qkv, d_att, ctx, attn_sums, up_sums, totals_one, totals_two, *refs):
    whole = jnp.concatenate(
        [dot(x[...], d_qkv[...], TN).astype(BF), dot(d_att[...], ctx[...], TN).astype(BF)], axis=1
    )
    units, width = up_sums.shape[1] // 2, x.shape[1]
    extra = vector_rows(
        2 * n, cols, units, width // (8 * n), table[5],
        attn_sums[...], up_sums[...], totals_one[...], totals_two[...],
    )
    for row in range(2):
        store_quarters(table, n, depth, row, by_row(whole, row, cols), refs, extra)


def outer_attn(place, table, x, d_qkv, d_att, ctx, sums, depth):
    n, cols, width = place.line_size, ctx.shape[1] // 2, x.shape[1]
    if depth % 16:
        whole = jnp.concatenate([dot(x, d_qkv, TN), dot(d_att, ctx, TN)], axis=1).astype(BF)
        extra = vector_rows(2 * n, cols, sums[1].shape[1] // 2, width // (8 * n), place.core, *sums)
        vectors = jnp.stack([extra(row, data) for row in range(2) for data in range(2 * n)])
        return spread(place, jnp.stack([by_row(whole, i, cols) for i in range(2)]), depth, vectors)
    shape = ((n, depth + EXTRA, width), BF)
    return call(
        functools.partial(outer_attn_kernel, n, depth, cols),
        [shape] * 4,
        [table, x, d_qkv, d_att, ctx] + list(sums),
        scalars=1,
    )


def head_lanes(rows, head):
    lane = lax.broadcasted_iota(jnp.int32, (rows, LANES), 1)
    return (lane < HD) if head == 0 else (lane >= HD)


def by_kind(unit, start, size):
    return jnp.concatenate([unit[0:1, start : start + size], unit[1:2, start : start + size]], axis=1)


def project_kernel(x, weights, unit, joined, qkv):
    cols = qkv.shape[1] // 3
    half = cols // 2
    for kind in range(4):
        cut = slice(kind * half, (kind + 1) * half)
        joined[:, kind * cols : (kind + 1) * cols] = jnp.concatenate(
            [weights[0, :, cut], weights[1, :, cut]], axis=1
        )
    qkv[:, :cols] = (
        (dot(x[...], joined[:, :cols]) + by_kind(unit, 0, half)).astype(BF).astype(F32) * HD ** (-0.5)
    ).astype(BF)
    qkv[:, cols : 2 * cols] = dot(x[...], joined[:, cols : 2 * cols]).astype(BF)
    qkv[:, 2 * cols :] = (dot(x[...], joined[:, 2 * cols : 3 * cols]) + by_kind(unit, half, half)).astype(BF)


def attend_kernel(block, chunk, bounds, qkv, joined, probs, ctx, part, mask):
    rows, cols = ctx.shape
    pair = pl.program_id(0)

    def labels(index):
        part_of = index // block
        place = index + jnp.where(part_of == 1, block, jnp.where(part_of == 2, -block, 0))
        total = jnp.zeros_like(index)
        for j in range(4):
            total = total + (place >= bounds[j]).astype(jnp.int32)
        return total

    @pl.when(pair == 0)
    def _():
        across = labels(lax.broadcasted_iota(jnp.int32, (1, rows), 1))
        down = labels(lax.broadcasted_iota(jnp.int32, (rows, 1), 0))
        mask[...] = jnp.where(down == across, 0.0, -1000000000.0)

    def lanes(kind):
        return pl.ds(pl.multiple_of(kind * cols + pair * LANES, LANES), LANES)

    keys, values = qkv[:, lanes(1)], qkv[:, lanes(2)]
    for step in range(rows // chunk):
        at = slice(step * chunk, (step + 1) * chunk)
        queries = qkv[at, lanes(0)]
        outs = []
        for head in range(2):
            one = jnp.where(head_lanes(chunk, head), queries, jnp.zeros_like(queries))
            scores = dot(one, keys, NT) + mask[at, :]
            exponent = jnp.exp(scores - jnp.max(scores, axis=1, keepdims=True))
            low = (exponent * (1.0 / jnp.sum(exponent, axis=1, keepdims=True))).astype(BF)
            probs[head, at, :] = low
            outs.append(dot(low, values))
        ctx[at, lanes(0)] = jnp.where(head_lanes(chunk, 0), outs[0], outs[1]).astype(BF)

    @pl.when(pair == pl.num_programs(0) - 1)
    def _():
        part[...] = dot(ctx[...], joined[:, 3 * cols :], NT).astype(BF)


def norm_parts(values):
    centred = values - jnp.mean(values, axis=-1, keepdims=True)
    rate = lax.rsqrt(jnp.mean(centred * centred, axis=-1, keepdims=True) + 1e-06)
    return centred * rate, rate


def norm_back(grad, unit, rate, scale):
    inner = grad * scale
    return rate * (
        inner
        - jnp.mean(inner, axis=-1, keepdims=True)
        - unit * jnp.mean(inner * unit, axis=-1, keepdims=True)
    )


def loop_rows(rows, chunk, step):
    def one(index, carry):
        step(pl.ds(pl.multiple_of(index * chunk, chunk), chunk))
        return carry

    lax.fori_loop(0, rows // chunk, one, 0)


def start_sums(*refs):
    @pl.when(pl.program_id(0) == 0)
    def _():
        for ref in refs:
            ref[...] = jnp.zeros_like(ref)


def up_kernel(chunk, start, x, mine, other, norms, bias, weights, unit, rate, low, activated, slope, hidden):
    rows, units = x.shape[0], weights.shape[2]

    def first(at):
        value = x[at, :].astype(F32) + mine[at, :].astype(F32) + other[at, :].astype(F32) + norms[2:3]
        one, scale = norm_parts(value)
        unit[at, :] = one
        rate[at, :] = jnp.broadcast_to(scale, (chunk, LANES))
        low[at, :] = (one * norms[0:1] + norms[3:4]).astype(BF)

    loop_rows(rows, chunk, first)
    up_bias = by_kind(bias, start, units)
    for half in range(2):
        cut = slice(half * units, (half + 1) * units)
        hidden[...] = dot(low[...], weights[half])

        def act(at):
            value = hidden[at, :] + up_bias[:, cut]
            share = 0.5 + 0.5 * lax.erf(value * (0.5**0.5))
            activated[at, cut] = (value * share).astype(BF)
            bell = jnp.exp(-0.5 * value * value) * 0.3989422804014327
            slope[at, cut] = (share + value * bell).astype(BF)

        loop_rows(rows, chunk, act)


def down_kernel(depth, n, where, activated, own, first, second, far, part, whole):
    pl.when(pl.program_id(0) == 0)(
        lambda: place_kernel(depth, n, where, own, first, second, far, whole)
    )
    units = whole.shape[2]
    part[...] = (
        dot(activated[:, :units], whole[0], NT) + dot(activated[:, units:], whole[1], NT)
    ).astype(BF)


def plain_down_kernel(activated, weights, part):
    units = weights.shape[2]
    part[...] = (
        dot(activated[:, :units], weights[0], NT) + dot(activated[:, units:], weights[1], NT)
    ).astype(BF)


def down(place, activated, quarters, depth):
    n, _, units = quarters[0].shape
    rows, width = activated.shape[0], 2 * n * depth
    if depth % 16:
        weights = place_group(place, quarters, depth)[0]
        part = call(
            plain_down_kernel, [((rows, width), BF, True)], [(activated, True), weights], steps=2
        )[0]
        return part, weights
    return call(
        functools.partial(down_kernel, depth, n),
        [((rows, width), BF, True), ((2, width, units), BF)],
        [place_spots(place), (activated, True)] + list(quarters),
        scalars=1,
        steps=2,
    )


def column_sums(totals, index, value):
    totals[index : index + 1, :] = totals[index : index + 1, :] + jnp.sum(value, axis=0, keepdims=True)


def second_kernel(chunk, unit, mine, other, grad, norms, result, d_second, d_mixed, totals):
    start_sums(totals)

    def step(at):
        normed = unit[at, :] * norms[0:1] + norms[3:4]
        value = normed + mine[at, :].astype(F32) + other[at, :].astype(F32) + norms[4:5]
        one, rate = norm_parts(value)
        result[at, :] = (one * norms[1:2] + norms[5:6]).astype(BF)
        dy = grad[at, :].astype(F32)
        back = norm_back(dy, one, rate, norms[1:2])
        d_second[at, :] = back
        d_mixed[at, :] = back.astype(BF)
        column_sums(totals, 0, dy * one)
        column_sums(totals, 1, back)
        column_sums(totals, 2, dy)

    loop_rows(unit.shape[0], chunk, step)


def hidden_back_kernel(chunk, d_mixed, down, up, slope, d_hidden, part, sums, d_act):
    rows, units = d_mixed.shape[0], down.shape[2]
    start_sums(sums)
    for half in range(2):
        cut = slice(half * units, (half + 1) * units)
        d_act[...] = dot(d_mixed[...], down[half])

        def step(at):
            low = (d_act[at, :] * slope[at, cut].astype(F32)).astype(BF)
            d_hidden[at, cut] = low
            sums[0:1, cut] = sums[0:1, cut] + jnp.sum(low.astype(F32), axis=0, keepdims=True)

        loop_rows(rows, chunk, step)
    part[...] = (
        dot(d_hidden[:, :units], up[0], NT) + dot(d_hidden[:, units:], up[1], NT)
    ).astype(BF)


def first_back_kernel(chunk, d_second, mine, other, unit, rate, norms, joined, d_first_in, d_att, d_ctx, totals):
    rows, cols = d_second.shape[0], d_ctx.shape[1]
    start_sums(totals)

    def step(at):
        d_first = d_second[at, :] + mine[at, :].astype(F32) + other[at, :].astype(F32)
        one = unit[at, :]
        back = norm_back(d_first, one, rate[at, 0:1], norms[0:1])
        d_first_in[at, :] = back
        d_att[at, :] = back.astype(BF)
        column_sums(totals, 0, d_first * one)
        column_sums(totals, 1, back)
        column_sums(totals, 2, d_first)

    loop_rows(rows, chunk, step)
    d_ctx[...] = dot(d_att[...], joined[:, 3 * cols :]).astype(BF)


def attend_back_kernel(chunk, d_ctx, qkv, probs, ctx, d_qkv, sums, d_scores):
    rows, cols = ctx.shape
    pair = pl.program_id(0)
    start_sums(sums)

    def lanes(kind):
        return pl.ds(pl.multiple_of(kind * cols + pair * LANES, LANES), LANES)

    keys, values = qkv[:, lanes(1)], qkv[:, lanes(2)]
    for step in range(rows // chunk):
        at = slice(step * chunk, (step + 1) * chunk)
        grads = d_ctx[at, lanes(0)]
        with_context = grads.astype(F32) * ctx[at, lanes(0)].astype(F32)
        outs = []
        for head in range(2):
            inside = head_lanes(chunk, head)
            one = jnp.where(inside, grads, jnp.zeros_like(grads))
            d_probs = dot(one, values, NT)
            inner = jnp.sum(jnp.where(inside, with_context, 0.0), axis=1, keepdims=True)
            low = (probs[head, at, :].astype(F32) * (d_probs - inner)).astype(BF)
            d_scores[head, at, :] = low
            outs.append(dot(low, keys))
        d_queries = (jnp.where(head_lanes(chunk, 0), outs[0], outs[1]) * HD ** (-0.5)).astype(BF)
        d_qkv[at, lanes(0)] = d_queries
        sums[0:1, lanes(0)] = sums[0:1, lanes(0)] + jnp.sum(
            d_queries.astype(F32), axis=0, keepdims=True
        )
    d_keys, d_values = 0.0, 0.0
    for head in range(2):
        inside = head_lanes(rows, head)
        queries, grads = qkv[:, lanes(0)], d_ctx[:, lanes(0)]
        d_keys += dot(d_scores[head], jnp.where(inside, queries, jnp.zeros_like(queries)), TN)
        d_values += dot(probs[head], jnp.where(inside, grads, jnp.zeros_like(grads)), TN)
    d_qkv[:, lanes(1)] = d_keys.astype(BF)
    d_values = d_values.astype(BF)
    d_qkv[:, lanes(2)] = d_values
    sums[0:1, lanes(1)] = jnp.sum(d_values.astype(F32), axis=0, keepdims=True)


def inputs_kernel(d_qkv, joined, part):
    part[...] = dot(d_qkv[...], joined[:, : d_qkv.shape[1]], NT).astype(BF)


def pack_kernel(w_qkv, w_out_t, unit_bias, norm_gain, norm_bias, attn):
    depth, cols, width = w_qkv.shape[1], w_qkv.shape[2], attn.shape[1]
    for kind in range(3):
        attn[:depth, kind * cols : (kind + 1) * cols] = w_qkv[kind]
    attn[:depth, 3 * cols :] = w_out_t[...]
    small = [ref[...].astype(F32) for ref in (unit_bias, norm_gain, norm_bias)]
    small = [jnp.pad(value, ((0, 0), (0, width - value.shape[1]))) for value in small]
    small.append(jnp.zeros((EXTRA - 7, width), F32))
    attn[depth:, :] = jnp.concatenate(small, axis=0).astype(BF)


def body(
    inputs, w_qkv, w_out, w_up, w_down, unit_bias, norm_gain, norm_bias, seq_lengths, cotangent
):
    place = Place()
    row, core = place.row, place.core
    groups = place.groups
    block, width = inputs.shape[1], inputs.shape[2]
    rows = 4 * block
    depth, head_cols = w_qkv.shape[1], w_qkv.shape[2]
    units = w_up.shape[1]
    share = unit_bias.shape[1]
    small = norm_gain.shape[1]
    cols = 2 * head_cols
    heads = cols // HD
    chunk = 64

    if depth % 16 == 0:
        (attn_shard,) = call(
            pack_kernel,
            [((depth + EXTRA, width), BF)],
            [w_qkv, w_out.T, unit_bias, norm_gain, norm_bias],
        )
    else:
        small_rows = [
            jnp.pad(part, ((0, 0), (0, width - part.shape[1]))) for part in (unit_bias, norm_gain, norm_bias)
        ]
        small_rows.append(jnp.zeros((EXTRA - 7, width), BF))
        attn_shard = jnp.concatenate([w_qkv[0], w_qkv[1], w_qkv[2], w_out.T], axis=1)
        attn_shard = jnp.concatenate([attn_shard] + small_rows, axis=0)
    keep = lambda array, index: lax.dynamic_index_in_dim(array, index, 0, keepdims=False)
    outgoing = jnp.stack([keep(inputs, 1 - row), keep(cotangent, 1 - row)])
    incoming = place.row_swap(outgoing)
    attn_own = jnp.stack(line_parts(place, after(attn_shard, outgoing)))
    attn_own = after(attn_own, incoming)
    attn_first = place.cross(attn_own, 0)
    attn_second = place.cross(attn_own, 1)
    up_parts = line_parts(place, after(w_up, attn_own))
    attn_first = after(attn_first, attn_second)
    attn_far = place.cross(attn_first, 1)
    up_own = jnp.stack([after(part, attn_first) for part in up_parts])
    up_own = after(up_own, attn_far)
    up_first = place.cross(up_own, 0)
    up_second = place.cross(up_own, 1)
    down_parts = line_parts(place, after(w_down.T, up_own))

    mine = jnp.stack([keep(inputs, row), keep(cotangent, row)])
    low_rows = jnp.where(row == 0, mine, incoming)
    high_rows = jnp.where(row == 0, incoming, mine)
    half = jnp.concatenate([low_rows, high_rows], axis=1)
    other = place.core_swap(half)
    both = jnp.where(
        core == 0,
        jnp.concatenate([half, other], axis=1),
        jnp.concatenate([other, half], axis=1),
    )
    x, grad_rows = both[0], both[1]

    attn_whole, extras, unit_bias = place_group(
        place, (attn_own, attn_first, attn_second, attn_far), depth, share
    )
    norm_here = extras[:, :, 1:7, :small]
    norm_there = place.core_swap(norm_here)
    norm_all = jnp.where(
        core == 0,
        jnp.stack([norm_here, norm_there], axis=2),
        jnp.stack([norm_there, norm_here], axis=2),
    )
    norm_all = jnp.transpose(norm_all, (3, 1, 0, 2, 4)).reshape(6, width).astype(F32)
    norms = jnp.pad(norm_all, ((0, 2), (0, 0)))
    table = place.roles()

    bounds = jnp.cumsum(keep(seq_lengths, row), dtype=jnp.int32)
    wide = rows * width
    joined, qkv = call(
        project_kernel,
        [((width, 4 * cols), BF), ((rows, 3 * cols), BF)],
        [x, attn_whole, unit_bias],
    )
    up_first = after(up_first, up_second, qkv)
    up_far = place.cross(up_first, 1)
    down_own = jnp.stack([after(part, up_first) for part in down_parts])
    down_first = place.cross(down_own, 0)
    down_second = place.cross(down_own, 1)
    probs, ctx, part = call(
        functools.partial(attend_kernel, block, 128),
        [((heads, rows, rows), BF, True), ((rows, cols), BF), ((rows, width), BF)],
        [bounds, after(qkv, down_own, norms), joined],
        scalars=1,
        scratch=[pltpu.VMEM((rows, rows), F32)],
        steps=cols // LANES,
    )
    down_first = after(down_first, down_second, ctx)
    down_far = place.cross(down_first, 1)
    up_far = after(up_far, down_first)
    up_whole = place_group(place, (up_own, up_first, up_second, up_far), depth)[0]
    unit, rate, first_low, activated, slope = call(
        functools.partial(up_kernel, chunk, 2 * head_cols),
        [
            ((rows, width), F32, True),
            ((rows, LANES), F32, True),
            ((rows, width), BF, True),
            ((rows, 2 * units), BF, True),
            ((rows, 2 * units), BF, True),
        ],
        [(x, True), (part, True), (place.core_swap(part), True), norms, unit_bias, up_whole],
        scratch=[pltpu.VMEM((rows // 2, units), F32)],
        steps=2,
    )
    part, down_whole = down(place, activated, (down_own, down_first, down_second, down_far), depth)
    result, d_second, d_mixed, totals_two = call(
        functools.partial(second_kernel, chunk),
        [((rows, width), BF, True), ((rows, width), F32, True), ((rows, width), BF, True), ((8, width), F32)],
        [(unit, True), (part, True), (place.core_swap(part), True), (grad_rows, True), norms],
        steps=4,
    )

    down_own, down_first, down_second, down_far = outer(place, table, d_mixed, activated, depth)
    down_got_far = place.cross(down_far, 0)
    d_hidden, part, up_sums = call(
        functools.partial(hidden_back_kernel, chunk),
        [((rows, 2 * units), BF, True), ((rows, width), BF, True), ((8, 2 * units), F32)],
        [(after(d_mixed, down_far), True), down_whole, up_whole, (slope, True)],
        scratch=[pltpu.VMEM((rows // 2, units), F32)],
        steps=2,
    )
    add = lambda one, other: (one.astype(F32) + other.astype(F32)).astype(BF)
    add_three = lambda one, two, three: one.astype(F32) + two.astype(F32) + three.astype(F32)
    down_second = add(down_second, after(down_got_far, d_hidden))
    down_got_second = place.cross(down_second, 1)
    down_got_first = place.cross(after(down_first, down_second), 0)
    up_own, up_first, up_second, up_far = outer(
        place, table, after(first_low, down_second), d_hidden, depth
    )
    up_got_far = place.cross(up_far, 0)
    d_first_in, d_att, d_ctx, totals_one = call(
        functools.partial(first_back_kernel, chunk),
        [((rows, width), F32, True), ((rows, width), BF, True), ((rows, cols), BF, True), ((8, width), F32)],
        [
            (after(d_second, up_far), True),
            (part, True),
            (place.core_swap(part), True),
            (unit, True),
            (rate, True),
            norms,
            joined,
        ],
        steps=4,
    )
    d_qkv, attn_sums = call(
        functools.partial(attend_back_kernel, 128),
        [((rows, 3 * cols), BF), ((8, 2 * cols), F32)],
        [d_ctx, qkv, (probs, True), ctx],
        scratch=[pltpu.VMEM((2, rows, rows), BF)],
        steps=cols // LANES,
    )
    up_second = add(up_second, after(up_got_far, d_qkv))
    up_got_second = place.cross(up_second, 1)
    up_got_first = place.cross(after(up_first, up_second), 0)
    down_sum = add_three(down_own, down_got_first, after(down_got_second, up_second))
    grad_down = scatter_line(place, down_sum)
    attn_own, attn_first, attn_second, attn_far = outer_attn(
        place, table, x, after(d_qkv, up_second, down_sum), d_att, ctx,
        (attn_sums, up_sums, totals_one, totals_two), depth,
    )
    attn_got_far = place.cross(attn_far, 0)
    (part,) = call(
        inputs_kernel,
        [((rows, width), BF, True)],
        [(after(d_qkv, attn_far), True), joined],
        steps=2,
    )
    attn_second = add(attn_second, after(attn_got_far, part))
    attn_got_second = place.cross(attn_second, 1)
    attn_got_first = place.cross(after(attn_first, attn_second), 0)
    up_sum = add_three(up_own, up_got_first, after(up_got_second, attn_second))
    grad_up = scatter_line(place, up_sum)
    grad_in = d_first_in + part.astype(F32) + place.core_swap(part).astype(F32)
    attn_sum = add_three(attn_own, after(attn_got_first, up_sum), attn_got_second)
    attn_grad = scatter_line(place, attn_sum)

    def hand_back(full):
        mine = lax.dynamic_slice_in_dim(full, core * 2 * block, 2 * block, 0)
        mine = mine.reshape(2, block, width)
        kept = keep(mine, row)
        got = place.row_swap(after(keep(mine, 1 - row).astype(BF), attn_sum)).astype(full.dtype)
        return jnp.where(row == 0, jnp.stack([kept, got]), jnp.stack([got, kept]))

    grad_qkv = jnp.stack(
        [attn_grad[:depth, t * head_cols : (t + 1) * head_cols] for t in range(3)]
    )
    grad_out = jnp.transpose(attn_grad[:depth, 3 * head_cols :])
    norm_grad = attn_grad[depth + 1 : depth + 7, :small]
    return (
        hand_back(result),
        hand_back(grad_in),
        grad_qkv,
        grad_out,
        grad_up,
        jnp.transpose(grad_down),
        attn_grad[depth : depth + 1, :share],
        norm_grad[:2],
        norm_grad[2:],
    )

def solution(mesh):
    placed = (
        P("dp", "mp", None),
        P(None, "dp", "mp"),
        P("mp", "dp"),
        P("dp", "mp"),
        P("mp", "dp"),
        P("mp", "dp"),
        P(None, ("dp", "mp")),
        P(None, ("dp", "mp")),
        P("dp", None),
        P("dp", "mp", None),
    )
    return jax.shard_map(
        body,
        mesh=mesh,
        in_specs=placed,
        out_specs=(
            P("dp", "mp", None),
            P("dp", "mp", None),
            P(None, "dp", "mp"),
            P("mp", "dp"),
            P("dp", "mp"),
            P("mp", "dp"),
            P("mp", "dp"),
            P(None, ("dp", "mp")),
            P(None, ("dp", "mp")),
        ),
        check_vma=False,
    )
```

time: 275 us -> 247 us (0.90)
  other arithmetic: 20.2 us -> 9.61 us
  local copies, waits for them, and re-layouts: 23.4 us -> 14.6 us
  waiting for transfers between devices: 88.7 us -> 80.4 us
  Pallas kernels: 98.1 us -> 92 us
  starting transfers between devices: 42.7 us -> 48.1 us
    ppermute x3, waiting for transfers between devices: 10.9 us -> 0.01 us  [row_swap(): return lax.ppermute(value, 'mp', [(0, 2), (2, 0), (1, 3), (3, 1)])]
    pallas_call x13 -> x15, Pallas kernels: 98.1 us -> 92 us  [call(): pl.pallas_call(kernel, out_shape=[jax.ShapeDtypeStruct(shape, kind) for s...]
    slice x9 -> x1, local copies, waits for them, and re-layouts: 6.66 us -> 0.56 us  [body(): attn_grad[depth:depth + 1, :share]]
    ppermute x12 -> x18, starting transfers between devices: 13.9 us -> 18.9 us  [cross(): return lax.ppermute(value, ('dp', 'mp'), pairs)]
    another operation x9 -> x4, other arithmetic: 6.53 us -> 1.84 us  [the longest x1 1.01 us: body(): attn_own = jnp.stack(line_parts(place, after(attn_shard, outgoing)))]
    ppermute x18, waiting for transfers between devices: 37.7 us -> 40.9 us  [line_swap(): return lax.ppermute(value, 'dp', pairs)]
    reshape x7 -> x0, local copies, waits for them, and re-layouts: 3.16 us -> none  [the longest x1 0.77 us: body(): norm_bias.reshape(-1)]
    unnamed x47 -> x58, local copies, waits for them, and re-layouts: 5.03 us -> 7.11 us
  transfers between devices with their start and end apart: 39 -> 45, of which waited for: 16 -> 17; matrix products, arithmetic and copies ran while one was open for 12% -> 7% of each run, Pallas kernels for 23% -> 28%
where the time goes in v3:
time: 247 us; the launch traced here: 246 us
  Pallas kernels  92 us (37%)
  waiting for transfers between devices  80.4 us (33%)
  starting transfers between devices  48.1 us (19%)
  local copies, waits for them, and re-layouts  14.6 us (6%)
  other arithmetic  9.61 us (4%)
    pallas_call x15, Pallas kernels, call(): pl.pallas_call(kernel, out_shape=[jax.ShapeDtypeStruct(shape, kind) for s...  92 us
    ppermute x18, waiting for transfers between devices, line_swap(): return lax.ppermute(value, 'dp', pairs)  40.9 us
    ppermute x18, waiting for transfers between devices, cross(): return lax.ppermute(value, ('dp', 'mp'), pairs)  37.2 us
    ppermute x18, starting transfers between devices, line_swap(): return lax.ppermute(value, 'dp', pairs)  23.7 us
    ppermute x18, starting transfers between devices, cross(): return lax.ppermute(value, ('dp', 'mp'), pairs)  18.9 us
    unnamed x58, local copies, waits for them, and re-layouts  7.11 us
    ppermute x3, starting transfers between devices, row_swap(): return lax.ppermute(value, 'mp', [(0, 2), (2, 0), (1, 3), (3, 1)])  5.06 us
  transfers between devices with their start and end apart: 45, of which 17 were waited for; matrix products, arithmetic and copies ran while one was open for 7% of the time, Pallas kernels for 28%

profile of v3, /device:TPU:0, one launch (start us, length us, event | category | flops | bytes accessed | tf_op | source)
XLA Modules:
  0.0 245.9 jit_solution(10994798590935494522)
XLA Ops:
  7.5 3.6 %collective-permute-start.4 = (bf16[112,768]{1,0:T(8,128)(2,1)}, bf16[112,768]{1,0:T(8,128)(2,1)S(1)}, u32[]{:S(2)}, u32[]{:S(2)}) collective-permute-start(bf16[112,768]{1,0:T(8,128)(2,1)} %shard_map.169), channel_id=1, source_target_pairs={{0,24},{4,28},{8,16},{12,20},{16,8},{20,12},{24,0},{28,4},{1,25},{... | collective-permute-start | bytes 516104 | tf_op jit(solution)/shard_map/ppermute | solution.py:70
  11.9 5.0 %collective-permute-done.4 = bf16[112,768]{1,0:T(8,128)(2,1)S(1)} collective-permute-done((bf16[112,768]{1,0:T(8,128)(2,1)}, bf16[112,768]{1,0:T(8,128)(2,1)S(1)}, u32[]{:S(2)}, u32[]{:S(2)}) %collective-permute-start.4) | collective-permute-done | bytes 172064 | tf_op jit(solution)/shard_map/ppermute | solution.py:70
  16.9 8.8 %collective-permute-done.3 = bf16[112,768]{1,0:T(8,128)(2,1)S(1)} collective-permute-done((bf16[112,768]{1,0:T(8,128)(2,1)}, bf16[112,768]{1,0:T(8,128)(2,1)S(1)}, u32[]{:S(2)}, u32[]{:S(2)}) %collective-permute-start.3) | collective-permute-done | bytes 172064 | tf_op jit(solution)/shard_map/ppermute | solution.py:70
  28.9 14.6 %collective-permute-done.6.second = bf16[4,112,768]{2,1,0:T(8,128)(2,1)} collective-permute-done((bf16[4,112,768]{2,1,0:T(8,128)(2,1)S(1)}, bf16[4,112,768]{2,1,0:T(8,128)(2,1)}, u32[]{:S(2)}, u32[]{:S(2)}) %collective-permute-start.6) | collective-permute-done | bytes 688160 | tf_op jit(solution)/shard_map/ppermute | solution.py:80
  49.4 4.2 %collective-permute-done.10 = bf16[96,768]{1,0:T(8,128)(2,1)S(1)} collective-permute-done((bf16[96,768]{1,0:T(8,128)(2,1)S(1)}, bf16[96,768]{1,0:T(8,128)(2,1)S(1)}, u32[]{:S(2)}, u32[]{:S(2)}) %collective-permute-start.10) | collective-permute-done | bytes 147488 | tf_op jit(solution)/shard_map/ppermute | solution.py:70
  53.6 4.8 %collective-permute-done.9 = bf16[96,768]{1,0:T(8,128)(2,1)S(1)} collective-permute-done((bf16[96,768]{1,0:T(8,128)(2,1)S(1)}, bf16[96,768]{1,0:T(8,128)(2,1)S(1)}, u32[]{:S(2)}, u32[]{:S(2)}) %collective-permute-start.9) | collective-permute-done | bytes 147488 | tf_op jit(solution)/shard_map/ppermute | solution.py:70
  68.6 3.3 %shard_map.170 = (bf16[2,768,768]{2,1,0:T(8,128)(2,1)}, bf16[2,8,16,768]{3,2,1,0:T(8,128)(2,1)}, f32[8,1152]{1,0:T(8,128)}) custom-call(s32[9]{0:T(128)} %stack.188.where, bf16[4,112,768]{2,1,0:T(8,128)(2,1)} %copy-done.2, bf16[4,112,768]{2,1,0:T(8,128)(2,1)} %collective-permute-done.5.first, bf16[4,112,768]{2,1,0:T(8,128)(2,1)} %collective-permute-done.6.second, ...), custom_call_target="tpu_custom_call" | custom-call | tf_op jit(solution)/shard_map/pallas_call | solution.py:37
  71.9 5.0 %shard_map.171 = (bf16[768,1536]{1,0:T(8,128)(2,1)}, bf16[512,1152]{1,0:T(8,128)(2,1)}) custom-call(bf16[512,768]{1,0:T(8,128)(2,1)} %get-tuple-element.173.x, bf16[2,768,768]{2,1,0:T(8,128)(2,1)} %get-tuple-element.86.weights, f32[8,1152]{1,0:T(8,128)} %get-tuple-element.87.unit.bias), custom_call_target="tpu_custom_call" | custom-call | tf_op jit(solution)/shard_map/pallas_call | solution.py:37
  82.0 13.1 %shard_map.172 = (bf16[6,512,512]{2,1,0:T(8,128)(2,1)}, bf16[512,384]{1,0:T(8,128)(2,1)}, bf16[512,768]{1,0:T(8,128)(2,1)}) custom-call(s32[4]{0:T(128)} %bitcast.125, bf16[512,1152]{1,0:T(8,128)(2,1)} %get-tuple-element.102.qkv, bf16[768,1536]{1,0:T(8,128)(2,1)} %get-tuple-element.103.joined), custom_call_target="tpu_custom_call" | custom-call | tf_op jit(solution)/shard_map/pallas_call | solution.py:37
  97.4 8.0 %collective-permute-done.18.far = bf16[4,96,768]{2,1,0:T(8,128)(2,1)S(1)} collective-permute-done((bf16[4,96,768]{2,1,0:T(8,128)(2,1)}, bf16[4,96,768]{2,1,0:T(8,128)(2,1)S(1)}, u32[]{:S(2)}, u32[]{:S(2)}) %collective-permute-start.18) | collective-permute-done | bytes 589856 | tf_op jit(solution)/shard_map/ppermute | solution.py:80
  110.4 9.5 %shard_map.174 = (f32[512,768]{1,0:T(8,128)}, f32[512,128]{1,0:T(8,128)}, bf16[512,768]{1,0:T(8,128)(2,1)}, bf16[512,1536]{1,0:T(8,128)(2,1)}, bf16[512,1536]{1,0:T(8,128)(2,1)}) custom-call(bf16[512,768]{1,0:T(8,128)(2,1)} %get-tuple-element.173.x, bf16[512,768]{1,0:T(8,128)(2,1)} %get-tuple-element.104.mine, bf16[512,768]{1,0:T(8,128)(2,1)} %copy-done.8, ...), custom_call_target="tpu_custom_call" | custom-call | tf_op jit(solution)/shard_map/pallas_call | solution.py:37
  120.8 4.5 %shard_map.175 = (bf16[512,768]{1,0:T(8,128)(2,1)}, bf16[2,768,768]{2,1,0:T(8,128)(2,1)}) custom-call(s32[9]{0:T(128)} %stack.188.where, bf16[512,1536]{1,0:T(8,128)(2,1)} %get-tuple-element.109.activated.right, bf16[4,96,768]{2,1,0:T(8,128)(2,1)} %copy-done.4, bf16[4,96,768]{2,1,0:T(8,128)(2,1)} %copy-done.19, bf16[4,96,768]{2,1,0:T(8,128)(2,1)} %copy-done.18, ...), custom_call_target="tpu_custom_call" | custom-call | tf_op jit(solution)/shard_map/pallas_call | solution.py:37
  128.7 5.8 %shard_map.176 = (bf16[512,768]{1,0:T(8,128)(2,1)}, f32[512,768]{1,0:T(8,128)}, bf16[512,768]{1,0:T(8,128)(2,1)}, f32[8,768]{1,0:T(8,128)}) custom-call(f32[512,768]{1,0:T(8,128)} %get-tuple-element.108.unit, bf16[512,768]{1,0:T(8,128)(2,1)} %get-tuple-element.110.mine, bf16[512,768]{1,0:T(8,128)(2,1)} %copy-done.6, ...), custom_call_target="tpu_custom_call" | custom-call | tf_op jit(solution)/shard_map/pallas_call | solution.py:37
  134.4 5.5 %shard_map.177 = (bf16[4,96,768]{2,1,0:T(8,128)(2,1)}, bf16[4,96,768]{2,1,0:T(8,128)(2,1)}, bf16[4,96,768]{2,1,0:T(8,128)(2,1)}, bf16[4,96,768]{2,1,0:T(8,128)(2,1)}) custom-call(s32[6]{0:T(128)} %stack.213.table, bf16[512,768]{1,0:T(8,128)(2,1)} %get-tuple-element.117.left.d_mixed, bf16[512,1536]{1,0:T(8,128)(2,1)} %get-tuple-element.109.activated.right), custom_call_target="tpu_custom_call" | custom-call | tf_op jit(solution)/shard_map/pallas_call | solution.py:37
  141.4 8.6 %shard_map.178 = (bf16[512,1536]{1,0:T(8,128)(2,1)}, bf16[512,768]{1,0:T(8,128)(2,1)}, f32[8,1536]{1,0:T(8,128)}) custom-call(bf16[512,768]{1,0:T(8,128)(2,1)} %get-tuple-element.117.left.d_mixed, bf16[2,768,768]{2,1,0:T(8,128)(2,1)} %get-tuple-element.118.down, bf16[2,768,768]{2,1,0:T(8,128)(2,1)} %shard_map.173.weights.up, ...), custom_call_target="tpu_custom_call" | custom-call | tf_op jit(solution)/shard_map/pallas_call | solution.py:37
  150.2 5.4 %shard_map.179 = (bf16[4,96,768]{2,1,0:T(8,128)(2,1)}, bf16[4,96,768]{2,1,0:T(8,128)(2,1)}, bf16[4,96,768]{2,1,0:T(8,128)(2,1)}, bf16[4,96,768]{2,1,0:T(8,128)(2,1)}) custom-call(s32[6]{0:T(128)} %stack.213.table, bf16[512,768]{1,0:T(8,128)(2,1)} %get-tuple-element.122.left, bf16[512,1536]{1,0:T(8,128)(2,1)} %get-tuple-element.120.right), custom_call_target="tpu_custom_call" | custom-call | tf_op jit(solution)/shard_map/pallas_call | solution.py:37
  159.9 6.3 %shard_map.180 = (f32[512,768]{1,0:T(8,128)}, bf16[512,768]{1,0:T(8,128)(2,1)}, bf16[512,384]{1,0:T(8,128)(2,1)}, f32[8,768]{1,0:T(8,128)}) custom-call(f32[512,768]{1,0:T(8,128)} %get-tuple-element.124.d_second, bf16[512,768]{1,0:T(8,128)(2,1)} %get-tuple-element.125.mine, bf16[512,768]{1,0:T(8,128)(2,1)} %copy-done.7, f32[512,768]{1,0:T(8,128)} %get-tuple-element.108.unit, ...), custom_call_target="tpu_custom_call" | custom-call | tf_op jit(solution)/shard_map/pallas_call | solution.py:37
  166.2 9.6 %shard_map.181 = (bf16[512,1152]{1,0:T(8,128)(2,1)}, f32[8,768]{1,0:T(8,128)}) custom-call(bf16[512,384]{1,0:T(8,128)(2,1)} %get-tuple-element.127.d_ctx, bf16[512,1152]{1,0:T(8,128)(2,1)} %get-tuple-element.102.qkv, bf16[6,512,512]{2,1,0:T(8,128)(2,1)} %get-tuple-element.128.probs, bf16[512,384]{1,0:T(8,128)(2,1)} %get-tuple-element.105.ctx), custom_call_target="tpu_custom_call" | custom-call | tf_op jit(solution)/shard_map/pallas_call | solution.py:37
  178.1 6.4 %shard_map.182 = (bf16[4,112,768]{2,1,0:T(8,128)(2,1)}, bf16[4,112,768]{2,1,0:T(8,128)(2,1)}, bf16[4,112,768]{2,1,0:T(8,128)(2,1)}, bf16[4,112,768]{2,1,0:T(8,128)(2,1)}) custom-call(s32[6]{0:T(128)} %stack.213.table, bf16[512,768]{1,0:T(8,128)(2,1)} %get-tuple-element.173.x, bf16[512,1152]{1,0:T(8,128)(2,1)} %get-tuple-element.146.d_qkv, ...), custom_call_target="tpu_custom_call" | custom-call | tf_op jit(solution)/shard_map/pallas_call | solution.py:37
  193.9 4.1 %shard_map.183 = bf16[512,768]{1,0:T(8,128)(2,1)} custom-call(bf16[512,1152]{1,0:T(8,128)(2,1)} %get-tuple-element.146.d_qkv, bf16[768,1536]{1,0:T(8,128)(2,1)} %get-tuple-element.103.joined), custom_call_target="tpu_custom_call" | custom-call | tf_op jit(solution)/shard_map/pallas_call | solution.py:37
  198.1 4.1 %collective-permute-done.43 = bf16[96,768]{1,0:T(8,128)(2,1)S(1)} collective-permute-done((bf16[96,768]{1,0:T(8,128)(2,1)}, bf16[96,768]{1,0:T(8,128)(2,1)S(1)}, u32[]{:S(2)}, u32[]{:S(2)}) %collective-permute-start.43) | collective-permute-done | bytes 147488 | tf_op jit(solution)/shard_map/ppermute | solution.py:70
  207.2 4.0 %collective-permute-done.30 = bf16[4,96,768]{2,1,0:T(8,128)(2,1)S(1)} collective-permute-done((bf16[4,96,768]{2,1,0:T(8,128)(2,1)}, bf16[4,96,768]{2,1,0:T(8,128)(2,1)S(1)}, u32[]{:S(2)}, u32[]{:S(2)}) %collective-permute-start.30) | collective-permute-done | bytes 589856 | tf_op jit(solution)/shard_map/ppermute | solution.py:80
  215.2 7.8 %collective-permute-done.29 = bf16[4,112,768]{2,1,0:T(8,128)(2,1)S(1)} collective-permute-done((bf16[4,112,768]{2,1,0:T(8,128)(2,1)S(1)}, bf16[4,112,768]{2,1,0:T(8,128)(2,1)S(1)}, u32[]{:S(2)}, u32[]{:S(2)}) %collective-permute-start.29) | collective-permute-done | bytes 688160 | tf_op jit(solution)/shard_map/ppermute | solution.py:80
  234.1 6.7 %collective-permute-done.37 = bf16[112,768]{1,0:T(8,128)(2,1)S(1)} collective-permute-done((bf16[112,768]{1,0:T(8,128)(2,1)S(1)}, bf16[112,768]{1,0:T(8,128)(2,1)S(1)}, u32[]{:S(2)}, u32[]{:S(2)}) %collective-permute-start.37) | collective-permute-done | bytes 172064 | tf_op jit(solution)/shard_map/ppermute | solution.py:70
  (182 shorter events, 86.3 us)
Async XLA Ops:
  2.0 24.6 %collective-permute-start = (bf16[2,128,768]{2,1,0:T(8,128)(2,1)S(1)}, bf16[2,128,768]{2,1,0:T(8,128)(2,1)S(1)}, u32[]{:S(2)}, u32[]{:S(2)}) collective-permute-start(bf16[2,128,768]{2,1,0:T(8,128)(2,1)S(1)} %pad_maximum_fusion.5), channel_id=1, source_target_pairs={{0,2},{2,0},{1,3},{3,1},{4,6},{6,4},{5,7},{7,5},{8,10},{10,8},{9,1... | collective-permute-start | bytes 1179656 | tf_op jit(solution)/shard_map/ppermute | solution.py:66
  11.1 14.5 %collective-permute-start.3 = (bf16[112,768]{1,0:T(8,128)(2,1)}, bf16[112,768]{1,0:T(8,128)(2,1)S(1)}, u32[]{:S(2)}, u32[]{:S(2)}) collective-permute-start(bf16[112,768]{1,0:T(8,128)(2,1)} %shard_map.169), channel_id=1, source_target_pairs={{0,16},{4,20},{8,24},{12,28},{16,0},{20,4},{24,8},{28,12},{1,17},{... | collective-permute-start | bytes 516104 | tf_op jit(solution)/shard_map/ppermute | solution.py:70
  26.7 16.8 %collective-permute-start.6 = (bf16[4,112,768]{2,1,0:T(8,128)(2,1)S(1)}, bf16[4,112,768]{2,1,0:T(8,128)(2,1)}, u32[]{:S(2)}, u32[]{:S(2)}) collective-permute-start(bf16[4,112,768]{2,1,0:T(8,128)(2,1)S(1)} %pad_maximum_fusion.1.own), channel_id=1, source_target_pairs={{0,4},{1,3},{2,6},{3,1},{4,0},{5,7},{6,2},{7,5},{8,12},{9,11},{10,... | collective-permute-start | bytes 2064392 | tf_op jit(solution)/shard_map/ppermute | solution.py:80
  28.2 15.3 %collective-permute-start.5 = (bf16[4,112,768]{2,1,0:T(8,128)(2,1)S(1)}, bf16[4,112,768]{2,1,0:T(8,128)(2,1)}, u32[]{:S(2)}, u32[]{:S(2)}) collective-permute-start(bf16[4,112,768]{2,1,0:T(8,128)(2,1)S(1)} %pad_maximum_fusion.1.own), channel_id=1, source_target_pairs={{0,2},{1,5},{2,0},{3,7},{4,6},{5,1},{6,4},{7,3},{8,10},{9,13},{10,... | collective-permute-start | bytes 2064392 | tf_op jit(solution)/shard_map/ppermute | solution.py:80
  28.9 33.2 %collective-permute-start.1 = (bf16[2,256,768]{2,1,0:T(8,128)(2,1)S(1)}, bf16[2,256,768]{2,1,0:T(8,128)(2,1)S(1)}, u32[]{:S(2)}, u32[]{:S(2)}) collective-permute-start(bf16[2,256,768]{2,1,0:T(8,128)(2,1)S(1)} %pad_maximum_fusion), channel_id=1, source_target_pairs={{0,1},{1,0},{2,3},{3,2},{4,5},{5,4},{6,7},{7,6},{8,9},{9,8},{10,11... | collective-permute-start | bytes 2359304 | tf_op jit(solution)/shard_map/ppermute | solution.py:63
  43.5 14.9 %collective-permute-start.7 = (bf16[4,112,768]{2,1,0:T(8,128)(2,1)}, bf16[4,112,768]{2,1,0:T(8,128)(2,1)S(1)}, u32[]{:S(2)}, u32[]{:S(2)}) collective-permute-start(bf16[4,112,768]{2,1,0:T(8,128)(2,1)} %collective-permute-done.5.first), channel_id=1, source_target_pairs={{0,4},{1,3},{2,6},{3,1},{4,0},{5,7},{6,2},{7,5},{8,12},{9,11},{10,... | collective-permute-start | bytes 2064392 | tf_op jit(solution)/shard_map/ppermute | solution.py:80
  59.4 17.6 %collective-permute-start.12 = (bf16[4,96,768]{2,1,0:T(8,128)(2,1)S(1)}, bf16[4,96,768]{2,1,0:T(8,128)(2,1)S(1)}, u32[]{:S(2)}, u32[]{:S(2)}) collective-permute-start(bf16[4,96,768]{2,1,0:T(8,128)(2,1)S(1)} %pad_maximum_fusion.2.own), channel_id=1, source_target_pairs={{0,4},{1,3},{2,6},{3,1},{4,0},{5,7},{6,2},{7,5},{8,12},{9,11},{10,... | collective-permute-start | bytes 1769480 | tf_op jit(solution)/shard_map/ppermute | solution.py:80
  60.7 16.2 %collective-permute-start.11 = (bf16[4,96,768]{2,1,0:T(8,128)(2,1)S(1)}, bf16[4,96,768]{2,1,0:T(8,128)(2,1)}, u32[]{:S(2)}, u32[]{:S(2)}) collective-permute-start(bf16[4,96,768]{2,1,0:T(8,128)(2,1)S(1)} %pad_maximum_fusion.2.own), channel_id=1, source_target_pairs={{0,2},{1,5},{2,0},{3,7},{4,6},{5,1},{6,4},{7,3},{8,10},{9,13},{10,... | collective-permute-start | bytes 1769480 | tf_op jit(solution)/shard_map/ppermute | solution.py:80
  77.1 19.6 %collective-permute-start.20 = (bf16[4,96,768]{2,1,0:T(8,128)(2,1)S(1)}, bf16[4,96,768]{2,1,0:T(8,128)(2,1)S(1)}, u32[]{:S(2)}, u32[]{:S(2)}) collective-permute-start(bf16[4,96,768]{2,1,0:T(8,128)(2,1)S(1)} %pad_maximum_fusion.3.own), channel_id=1, source_target_pairs={{0,4},{1,3},{2,6},{3,1},{4,0},{5,7},{6,2},{7,5},{8,12},{9,11},{10,... | collective-permute-start | bytes 1769480 | tf_op jit(solution)/shard_map/ppermute | solution.py:80
  78.6 18.0 %collective-permute-start.19 = (bf16[4,96,768]{2,1,0:T(8,128)(2,1)S(1)}, bf16[4,96,768]{2,1,0:T(8,128)(2,1)S(1)}, u32[]{:S(2)}, u32[]{:S(2)}) collective-permute-start(bf16[4,96,768]{2,1,0:T(8,128)(2,1)S(1)} %pad_maximum_fusion.3.own), channel_id=1, source_target_pairs={{0,2},{1,5},{2,0},{3,7},{4,6},{5,1},{6,4},{7,3},{8,10},{9,13},{10,... | collective-permute-start | bytes 1769480 | tf_op jit(solution)/shard_map/ppermute | solution.py:80
  96.7 23.3 %collective-permute-start.21 = (bf16[4,96,768]{2,1,0:T(8,128)(2,1)S(1)}, bf16[4,96,768]{2,1,0:T(8,128)(2,1)S(1)}, u32[]{:S(2)}, u32[]{:S(2)}) collective-permute-start(bf16[4,96,768]{2,1,0:T(8,128)(2,1)S(1)} %collective-permute-done.19.first), channel_id=1, source_target_pairs={{0,4},{1,3},{2,6},{3,1},{4,0},{5,7},{6,2},{7,5},{8,12},{9,11},{10,... | collective-permute-start | bytes 1769480 | tf_op jit(solution)/shard_map/ppermute | solution.py:80
  155.6 20.2 %collective-permute-start.25 = (bf16[4,96,768]{2,1,0:T(8,128)(2,1)}, bf16[4,96,768]{2,1,0:T(8,128)(2,1)S(1)}, u32[]{:S(2)}, u32[]{:S(2)}) collective-permute-start(bf16[4,96,768]{2,1,0:T(8,128)(2,1)} %get-tuple-element.123), channel_id=1, source_target_pairs={{0,2},{1,5},{2,0},{3,7},{4,6},{5,1},{6,4},{7,3},{8,10},{9,13},{10,... | collective-permute-start | bytes 1769480 | tf_op jit(solution)/shard_map/ppermute | solution.py:80
  157.0 18.9 %collective-permute-start.27 = (bf16[4,96,768]{2,1,0:T(8,128)(2,1)S(1)}, bf16[4,96,768]{2,1,0:T(8,128)(2,1)S(1)}, u32[]{:S(2)}, u32[]{:S(2)}) collective-permute-start(bf16[4,96,768]{2,1,0:T(8,128)(2,1)S(1)} %add_convert_fusion.2), channel_id=1, source_target_pairs={{0,4},{1,3},{2,6},{3,1},{4,0},{5,7},{6,2},{7,5},{8,12},{9,11},{10,... | collective-permute-start | bytes 1769480 | tf_op jit(solution)/shard_map/ppermute | solution.py:80
  157.6 20.3 %collective-permute-start.26 = (bf16[4,96,768]{2,1,0:T(8,128)(2,1)S(1)}, bf16[4,96,768]{2,1,0:T(8,128)(2,1)S(1)}, u32[]{:S(2)}, u32[]{:S(2)}) collective-permute-start(bf16[4,96,768]{2,1,0:T(8,128)(2,1)S(1)} %copy-done.27), channel_id=1, source_target_pairs={{0,2},{1,5},{2,0},{3,7},{4,6},{5,1},{6,4},{7,3},{8,10},{9,13},{10,... | collective-permute-start | bytes 1769480 | tf_op jit(solution)/shard_map/ppermute | solution.py:80
  184.5 19.4 %collective-permute-start.28 = (bf16[4,112,768]{2,1,0:T(8,128)(2,1)}, bf16[4,112,768]{2,1,0:T(8,128)(2,1)S(1)}, u32[]{:S(2)}, u32[]{:S(2)}) collective-permute-start(bf16[4,112,768]{2,1,0:T(8,128)(2,1)} %get-tuple-element.145), channel_id=1, source_target_pairs={{0,2},{1,5},{2,0},{3,7},{4,6},{5,1},{6,4},{7,3},{8,10},{9,13},{10,... | collective-permute-start | bytes 2064392 | tf_op jit(solution)/shard_map/ppermute | solution.py:80
  190.1 16.3 %collective-permute-start.31 = (bf16[4,96,768]{2,1,0:T(8,128)(2,1)S(1)}, bf16[4,96,768]{2,1,0:T(8,128)(2,1)S(1)}, u32[]{:S(2)}, u32[]{:S(2)}) collective-permute-start(bf16[4,96,768]{2,1,0:T(8,128)(2,1)S(1)} %add_convert_fusion.1), channel_id=1, source_target_pairs={{0,4},{1,3},{2,6},{3,1},{4,0},{5,7},{6,2},{7,5},{8,12},{9,11},{10,... | collective-permute-start | bytes 1769480 | tf_op jit(solution)/shard_map/ppermute | solution.py:80
  193.9 17.3 %collective-permute-start.30 = (bf16[4,96,768]{2,1,0:T(8,128)(2,1)}, bf16[4,96,768]{2,1,0:T(8,128)(2,1)S(1)}, u32[]{:S(2)}, u32[]{:S(2)}) collective-permute-start(bf16[4,96,768]{2,1,0:T(8,128)(2,1)} %get-tuple-element.151), channel_id=1, source_target_pairs={{0,2},{1,5},{2,0},{3,7},{4,6},{5,1},{6,4},{7,3},{8,10},{9,13},{10,... | collective-permute-start | bytes 1769480 | tf_op jit(solution)/shard_map/ppermute | solution.py:80
  198.0 15.2 %collective-permute-start.34 = (bf16[512,768]{1,0:T(8,128)(2,1)}, bf16[512,768]{1,0:T(8,128)(2,1)S(1)}, u32[]{:S(2)}, u32[]{:S(2)}) collective-permute-start(bf16[512,768]{1,0:T(8,128)(2,1)} %shard_map.183), channel_id=1, source_target_pairs={{0,1},{1,0},{2,3},{3,2},{4,5},{5,4},{6,7},{7,6},{8,9},{9,8},{10,11... | collective-permute-start | bytes 2359304 | tf_op jit(solution)/shard_map/ppermute | solution.py:63
  204.1 19.0 %collective-permute-start.32 = (bf16[4,112,768]{2,1,0:T(8,128)(2,1)S(1)}, bf16[4,112,768]{2,1,0:T(8,128)(2,1)S(1)}, u32[]{:S(2)}, u32[]{:S(2)}) collective-permute-start(bf16[4,112,768]{2,1,0:T(8,128)(2,1)S(1)} %add_convert_fusion), channel_id=1, source_target_pairs={{0,4},{1,3},{2,6},{3,1},{4,0},{5,7},{6,2},{7,5},{8,12},{9,11},{10,... | collective-permute-start | bytes 2064392 | tf_op jit(solution)/shard_map/ppermute | solution.py:80
  206.4 16.6 %collective-permute-start.29 = (bf16[4,112,768]{2,1,0:T(8,128)(2,1)S(1)}, bf16[4,112,768]{2,1,0:T(8,128)(2,1)S(1)}, u32[]{:S(2)}, u32[]{:S(2)}) collective-permute-start(bf16[4,112,768]{2,1,0:T(8,128)(2,1)S(1)} %copy-done.26), channel_id=1, source_target_pairs={{0,2},{1,5},{2,0},{3,7},{4,6},{5,1},{6,4},{7,3},{8,10},{9,13},{10,... | collective-permute-start | bytes 2064392 | tf_op jit(solution)/shard_map/ppermute | solution.py:80
  211.6 15.4 %collective-permute-start.41 = (bf16[96,768]{1,0:T(8,128)(2,1)S(1)}, bf16[96,768]{1,0:T(8,128)(2,1)S(1)}, u32[]{:S(2)}, u32[]{:S(2)}) collective-permute-start(bf16[96,768]{1,0:T(8,128)(2,1)S(1)} %get-tuple-element.183), channel_id=1, source_target_pairs={{0,24},{4,28},{8,16},{12,20},{16,8},{20,12},{24,0},{28,4},{1,25},{... | collective-permute-start | bytes 442376 | tf_op jit(solution)/shard_map/ppermute | solution.py:70
  225.3 15.5 %collective-permute-start.37 = (bf16[112,768]{1,0:T(8,128)(2,1)S(1)}, bf16[112,768]{1,0:T(8,128)(2,1)S(1)}, u32[]{:S(2)}, u32[]{:S(2)}) collective-permute-start(bf16[112,768]{1,0:T(8,128)(2,1)S(1)} %get-tuple-element.178), channel_id=1, source_target_pairs={{0,16},{4,20},{8,24},{12,28},{16,0},{20,4},{24,8},{28,12},{1,17},{... | collective-permute-start | bytes 516104 | tf_op jit(solution)/shard_map/ppermute | solution.py:70
  227.7 16.5 %collective-permute-start.33 = (bf16[128,768]{1,0:T(8,128)(2,1)S(1)}, bf16[128,768]{1,0:T(8,128)(2,1)S(1)}, u32[]{:S(2)}, u32[]{:S(2)}) collective-permute-start(bf16[128,768]{1,0:T(8,128)(2,1)S(1)} %get-tuple-element.154), channel_id=1, source_target_pairs={{0,2},{2,0},{1,3},{3,1},{4,6},{6,4},{5,7},{7,5},{8,10},{10,8},{9,1... | collective-permute-start | bytes 589832 | tf_op jit(solution)/shard_map/ppermute | solution.py:66
  229.0 16.0 %collective-permute-start.35 = (bf16[128,768]{1,0:T(8,128)(2,1)S(1)}, bf16[128,768]{1,0:T(8,128)(2,1)S(1)}, u32[]{:S(2)}, u32[]{:S(2)}) collective-permute-start(bf16[128,768]{1,0:T(8,128)(2,1)S(1)} %fusion.11), channel_id=1, source_target_pairs={{0,2},{2,0},{1,3},{3,1},{4,6},{6,4},{5,7},{7,5},{8,10},{10,8},{9,1... | collective-permute-start | bytes 589832 | tf_op jit(solution)/shard_map/ppermute | solution.py:66
  (49 other events, 504.1 us)

commit v4 on v3

--- a/solution.py
+++ b/solution.py
@@ -9,10 +9,11 @@
 
 HD = 64
 LANES = 128
+TILE = 256
 EXTRA = 16
 BF = jnp.bfloat16
 F32 = jnp.float32
-LIMIT = 56 * 1024 * 1024
+LIMIT = 28 * 1024 * 1024
 NN = ((1,), (0,))
 NT = ((1,), (1,))
 TN = ((0,), (0,))
@@ -43,7 +44,7 @@
         out_specs=[spec(shape, cut) for shape, _, cut in outs],
         scratch_shapes=list(scratch),
         compiler_params=pltpu.CompilerParams(vmem_limit_bytes=LIMIT),
-        cost_estimate=pl.CostEstimate(flops=0, bytes_accessed=0, transcendentals=0),
+        cost_estimate=pl.CostEstimate(flops=8000000000, bytes_accessed=10000000, transcendentals=0),
     )(*[arg for arg, _ in args])
 
 
@@ -108,19 +109,22 @@
     return [held[i] for i in range(n)]
 
 
-def scatter_line(place, terms):
+def scatter_parts(place, terms):
     n = place.line_size
     if n <= 4:
         low = terms.astype(BF)
-        total = terms[0]
-        for step in range(1, n):
-            total = total + place.line_swap(low[step], step).astype(F32)
-        return total
-    step = n // 2
+        return [place.line_swap(low[step], step) for step in range(1, n)]
+    first, step = terms[0], n // 2
     while step:
         got = place.line_swap(terms[step:].astype(BF), step)
         terms, step = terms[:step] + got.astype(F32), step // 2
-    return terms[0]
+    return [terms[0] - first]
+
+
+def total_of(start, parts):
+    for part in parts:
+        start = start + part.astype(F32)
+    return start
 
 
 def place_kernel(depth, n, where, own, first, second, far, whole, extras=None):
@@ -347,14 +351,16 @@
     for step in range(rows // chunk):
         at = slice(step * chunk, (step + 1) * chunk)
         queries = qkv[at, lanes(0)]
-        outs = []
+        heads = [
+            jnp.where(head_lanes(chunk, head), queries, jnp.zeros_like(queries)) for head in range(2)
+        ]
+        scores = [dot(one, keys, NT) + mask[at, :] for one in heads]
+        exponents = [jnp.exp(one - jnp.max(one, axis=1, keepdims=True)) for one in scores]
+        rates = [1.0 / jnp.sum(one, axis=1, keepdims=True) for one in exponents]
+        lows = [(one * rate).astype(BF) for one, rate in zip(exponents, rates)]
         for head in range(2):
-            one = jnp.where(head_lanes(chunk, head), queries, jnp.zeros_like(queries))
-            scores = dot(one, keys, NT) + mask[at, :]
-            exponent = jnp.exp(scores - jnp.max(scores, axis=1, keepdims=True))
-            low = (exponent * (1.0 / jnp.sum(exponent, axis=1, keepdims=True))).astype(BF)
-            probs[head, at, :] = low
-            outs.append(dot(low, values))
+            probs[head, at, :] = lows[head]
+        outs = [dot(one, values) for one in lows]
         ctx[at, lanes(0)] = jnp.where(head_lanes(chunk, 0), outs[0], outs[1]).astype(BF)
 
     @pl.when(pair == pl.num_programs(0) - 1)
@@ -377,14 +383,6 @@
     )
 
 
-def loop_rows(rows, chunk, step):
-    def one(index, carry):
-        step(pl.ds(pl.multiple_of(index * chunk, chunk), chunk))
-        return carry
-
-    lax.fori_loop(0, rows // chunk, one, 0)
-
-
 def start_sums(*refs):
     @pl.when(pl.program_id(0) == 0)
     def _():
@@ -392,30 +390,23 @@
             ref[...] = jnp.zeros_like(ref)
 
 
-def up_kernel(chunk, start, x, mine, other, norms, bias, weights, unit, rate, low, activated, slope, hidden):
-    rows, units = x.shape[0], weights.shape[2]
-
-    def first(at):
-        value = x[at, :].astype(F32) + mine[at, :].astype(F32) + other[at, :].astype(F32) + norms[2:3]
-        one, scale = norm_parts(value)
-        unit[at, :] = one
-        rate[at, :] = jnp.broadcast_to(scale, (chunk, LANES))
-        low[at, :] = (one * norms[0:1] + norms[3:4]).astype(BF)
-
-    loop_rows(rows, chunk, first)
+def up_kernel(start, x, mine, other, norms, bias, weights, unit, rate, low, activated, slope):
+    units = weights.shape[2]
+    first_in = x[...].astype(F32) + mine[...].astype(F32) + other[...].astype(F32) + norms[2:3]
+    one, scale = norm_parts(first_in)
+    unit[...] = one.astype(BF)
+    rate[...] = jnp.broadcast_to(scale, rate.shape)
+    normed = (one * norms[0:1] + norms[3:4]).astype(BF)
+    low[...] = normed
     up_bias = by_kind(bias, start, units)
     for half in range(2):
-        cut = slice(half * units, (half + 1) * units)
-        hidden[...] = dot(low[...], weights[half])
-
-        def act(at):
-            value = hidden[at, :] + up_bias[:, cut]
+        for part in range(units // TILE):
+            cut = slice(half * units + part * TILE, half * units + (part + 1) * TILE)
+            value = dot(normed, weights[half, :, part * TILE : (part + 1) * TILE]) + up_bias[:, cut]
             share = 0.5 + 0.5 * lax.erf(value * (0.5**0.5))
-            activated[at, cut] = (value * share).astype(BF)
+            activated[:, cut] = (value * share).astype(BF)
             bell = jnp.exp(-0.5 * value * value) * 0.3989422804014327
-            slope[at, cut] = (share + value * bell).astype(BF)
-
-        loop_rows(rows, chunk, act)
+            slope[:, cut] = (share + value * bell).astype(BF)
 
 
 def down_kernel(depth, n, where, activated, own, first, second, far, part, whole):
@@ -457,59 +448,44 @@
     totals[index : index + 1, :] = totals[index : index + 1, :] + jnp.sum(value, axis=0, keepdims=True)
 
 
-def second_kernel(chunk, unit, mine, other, grad, norms, result, d_second, d_mixed, totals):
+def second_kernel(unit, mine, other, grad, norms, result, d_mixed, totals):
     start_sums(totals)
-
-    def step(at):
-        normed = unit[at, :] * norms[0:1] + norms[3:4]
-        value = normed + mine[at, :].astype(F32) + other[at, :].astype(F32) + norms[4:5]
-        one, rate = norm_parts(value)
-        result[at, :] = (one * norms[1:2] + norms[5:6]).astype(BF)
-        dy = grad[at, :].astype(F32)
-        back = norm_back(dy, one, rate, norms[1:2])
-        d_second[at, :] = back
-        d_mixed[at, :] = back.astype(BF)
-        column_sums(totals, 0, dy * one)
-        column_sums(totals, 1, back)
-        column_sums(totals, 2, dy)
-
-    loop_rows(unit.shape[0], chunk, step)
-
-
-def hidden_back_kernel(chunk, d_mixed, down, up, slope, d_hidden, part, sums, d_act):
-    rows, units = d_mixed.shape[0], down.shape[2]
+    normed = unit[...].astype(F32) * norms[0:1] + norms[3:4]
+    one, rate = norm_parts(normed + mine[...].astype(F32) + other[...].astype(F32) + norms[4:5])
+    result[...] = (one * norms[1:2] + norms[5:6]).astype(BF)
+    dy = grad[...].astype(F32)
+    back = norm_back(dy, one, rate, norms[1:2])
+    d_mixed[...] = back.astype(BF)
+    column_sums(totals, 0, dy * one)
+    column_sums(totals, 1, back)
+    column_sums(totals, 2, dy)
+
+
+def hidden_back_kernel(d_mixed, down, up, slope, d_hidden, part, sums):
+    units = down.shape[2]
     start_sums(sums)
+    total = 0.0
     for half in range(2):
         cut = slice(half * units, (half + 1) * units)
-        d_act[...] = dot(d_mixed[...], down[half])
-
-        def step(at):
-            low = (d_act[at, :] * slope[at, cut].astype(F32)).astype(BF)
-            d_hidden[at, cut] = low
-            sums[0:1, cut] = sums[0:1, cut] + jnp.sum(low.astype(F32), axis=0, keepdims=True)
-
-        loop_rows(rows, chunk, step)
-    part[...] = (
-        dot(d_hidden[:, :units], up[0], NT) + dot(d_hidden[:, units:], up[1], NT)
-    ).astype(BF)
-
-
-def first_back_kernel(chunk, d_second, mine, other, unit, rate, norms, joined, d_first_in, d_att, d_ctx, totals):
-    rows, cols = d_second.shape[0], d_ctx.shape[1]
+        low = (dot(d_mixed[...], down[half]) * slope[:, cut].astype(F32)).astype(BF)
+        d_hidden[:, cut] = low
+        sums[0:1, cut] = sums[0:1, cut] + jnp.sum(low.astype(F32), axis=0, keepdims=True)
+        total += dot(low, up[half], NT)
+    part[...] = total.astype(BF)
+
+
+def first_back_kernel(d_second, mine, other, unit, rate, norms, joined, d_att, d_ctx, totals):
+    cols = d_ctx.shape[1]
     start_sums(totals)
-
-    def step(at):
-        d_first = d_second[at, :] + mine[at, :].astype(F32) + other[at, :].astype(F32)
-        one = unit[at, :]
-        back = norm_back(d_first, one, rate[at, 0:1], norms[0:1])
-        d_first_in[at, :] = back
-        d_att[at, :] = back.astype(BF)
-        column_sums(totals, 0, d_first * one)
-        column_sums(totals, 1, back)
-        column_sums(totals, 2, d_first)
-
-    loop_rows(rows, chunk, step)
-    d_ctx[...] = dot(d_att[...], joined[:, 3 * cols :]).astype(BF)
+    d_first = d_second[...].astype(F32) + mine[...].astype(F32) + other[...].astype(F32)
+    one = unit[...].astype(F32)
+    back = norm_back(d_first, one, rate[:, 0:1], norms[0:1])
+    low = back.astype(BF)
+    d_att[...] = low
+    column_sums(totals, 0, d_first * one)
+    column_sums(totals, 1, back)
+    column_sums(totals, 2, d_first)
+    d_ctx[...] = dot(low, joined[:, 3 * cols :]).astype(BF)
 
 
 def attend_back_kernel(chunk, d_ctx, qkv, probs, ctx, d_qkv, sums, d_scores):
@@ -525,15 +501,17 @@
         at = slice(step * chunk, (step + 1) * chunk)
         grads = d_ctx[at, lanes(0)]
         with_context = grads.astype(F32) * ctx[at, lanes(0)].astype(F32)
-        outs = []
+        inside = [head_lanes(chunk, head) for head in range(2)]
+        ones = [jnp.where(lane, grads, jnp.zeros_like(grads)) for lane in inside]
+        d_probs = [dot(one, values, NT) for one in ones]
+        inner = [jnp.sum(jnp.where(lane, with_context, 0.0), axis=1, keepdims=True) for lane in inside]
+        lows = [
+            (probs[head, at, :].astype(F32) * (d_probs[head] - inner[head])).astype(BF)
+            for head in range(2)
+        ]
         for head in range(2):
-            inside = head_lanes(chunk, head)
-            one = jnp.where(inside, grads, jnp.zeros_like(grads))
-            d_probs = dot(one, values, NT)
-            inner = jnp.sum(jnp.where(inside, with_context, 0.0), axis=1, keepdims=True)
-            low = (probs[head, at, :].astype(F32) * (d_probs - inner)).astype(BF)
-            d_scores[head, at, :] = low
-            outs.append(dot(low, keys))
+            d_scores[head, at, :] = lows[head]
+        outs = [dot(one, keys) for one in lows]
         d_queries = (jnp.where(head_lanes(chunk, 0), outs[0], outs[1]) * HD ** (-0.5)).astype(BF)
         d_qkv[at, lanes(0)] = d_queries
         sums[0:1, lanes(0)] = sums[0:1, lanes(0)] + jnp.sum(
@@ -580,7 +558,6 @@
     small = norm_gain.shape[1]
     cols = 2 * head_cols
     heads = cols // HD
-    chunk = 64
 
     if depth % 16 == 0:
         (attn_shard,) = call(
@@ -600,16 +577,13 @@
     incoming = place.row_swap(outgoing)
     attn_own = jnp.stack(line_parts(place, after(attn_shard, outgoing)))
     attn_own = after(attn_own, incoming)
-    attn_first = place.cross(attn_own, 0)
-    attn_second = place.cross(attn_own, 1)
-    up_parts = line_parts(place, after(w_up, attn_own))
-    attn_first = after(attn_first, attn_second)
+    attn_first, attn_second = place.cross(attn_own, 0), place.cross(attn_own, 1)
+    up_own = jnp.stack(line_parts(place, after(w_up, attn_own)))
+    attn_first = after(attn_first, attn_second, up_own)
     attn_far = place.cross(attn_first, 1)
-    up_own = jnp.stack([after(part, attn_first) for part in up_parts])
-    up_own = after(up_own, attn_far)
-    up_first = place.cross(up_own, 0)
-    up_second = place.cross(up_own, 1)
-    down_parts = line_parts(place, after(w_down.T, up_own))
+    up_own = after(up_own, attn_first)
+    up_first, up_second = place.cross(up_own, 0), place.cross(up_own, 1)
+    down_own = jnp.stack(line_parts(place, after(w_down.T, up_own)))
 
     mine = jnp.stack([keep(inputs, row), keep(cotangent, row)])
     low_rows = jnp.where(row == 0, mine, incoming)
@@ -644,15 +618,14 @@
         [((width, 4 * cols), BF), ((rows, 3 * cols), BF)],
         [x, attn_whole, unit_bias],
     )
-    up_first = after(up_first, up_second, qkv)
+    up_first = after(up_first, up_second, down_own, qkv)
     up_far = place.cross(up_first, 1)
-    down_own = jnp.stack([after(part, up_first) for part in down_parts])
-    down_first = place.cross(down_own, 0)
-    down_second = place.cross(down_own, 1)
+    down_own = after(down_own, up_first)
+    down_first, down_second = place.cross(down_own, 0), place.cross(down_own, 1)
     probs, ctx, part = call(
-        functools.partial(attend_kernel, block, 128),
+        functools.partial(attend_kernel, block, rows),
         [((heads, rows, rows), BF, True), ((rows, cols), BF), ((rows, width), BF)],
-        [bounds, after(qkv, down_own, norms), joined],
+        [bounds, after(qkv, up_first, norms), joined],
         scalars=1,
         scratch=[pltpu.VMEM((rows, rows), F32)],
         steps=cols // LANES,
@@ -662,49 +635,45 @@
     up_far = after(up_far, down_first)
     up_whole = place_group(place, (up_own, up_first, up_second, up_far), depth)[0]
     unit, rate, first_low, activated, slope = call(
-        functools.partial(up_kernel, chunk, 2 * head_cols),
+        functools.partial(up_kernel, 2 * head_cols),
         [
-            ((rows, width), F32, True),
+            ((rows, width), BF, True),
             ((rows, LANES), F32, True),
             ((rows, width), BF, True),
             ((rows, 2 * units), BF, True),
             ((rows, 2 * units), BF, True),
         ],
         [(x, True), (part, True), (place.core_swap(part), True), norms, unit_bias, up_whole],
-        scratch=[pltpu.VMEM((rows // 2, units), F32)],
         steps=2,
     )
     part, down_whole = down(place, activated, (down_own, down_first, down_second, down_far), depth)
-    result, d_second, d_mixed, totals_two = call(
-        functools.partial(second_kernel, chunk),
-        [((rows, width), BF, True), ((rows, width), F32, True), ((rows, width), BF, True), ((8, width), F32)],
+    result, d_mixed, totals_two = call(
+        second_kernel,
+        [((rows, width), BF, True), ((rows, width), BF, True), ((8, width), F32)],
         [(unit, True), (part, True), (place.core_swap(part), True), (grad_rows, True), norms],
-        steps=4,
+        steps=2,
     )
 
     down_own, down_first, down_second, down_far = outer(place, table, d_mixed, activated, depth)
     down_got_far = place.cross(down_far, 0)
     d_hidden, part, up_sums = call(
-        functools.partial(hidden_back_kernel, chunk),
+        hidden_back_kernel,
         [((rows, 2 * units), BF, True), ((rows, width), BF, True), ((8, 2 * units), F32)],
         [(after(d_mixed, down_far), True), down_whole, up_whole, (slope, True)],
-        scratch=[pltpu.VMEM((rows // 2, units), F32)],
         steps=2,
     )
     add = lambda one, other: (one.astype(F32) + other.astype(F32)).astype(BF)
     add_three = lambda one, two, three: one.astype(F32) + two.astype(F32) + three.astype(F32)
-    down_second = add(down_second, after(down_got_far, d_hidden))
+    up_own, up_first, up_second, up_far = outer(place, table, first_low, d_hidden, depth)
+    down_second = add(down_second, after(down_got_far, up_far))
     down_got_second = place.cross(down_second, 1)
-    down_got_first = place.cross(after(down_first, down_second), 0)
-    up_own, up_first, up_second, up_far = outer(
-        place, table, after(first_low, down_second), d_hidden, depth
-    )
-    up_got_far = place.cross(up_far, 0)
-    d_first_in, d_att, d_ctx, totals_one = call(
-        functools.partial(first_back_kernel, chunk),
-        [((rows, width), F32, True), ((rows, width), BF, True), ((rows, cols), BF, True), ((8, width), F32)],
+    down_got_first = place.cross(after(down_first, down_far), 0)
+    up_got_far = place.cross(after(up_far, down_second), 0)
+    d_att, d_ctx, totals_one = call(
+        first_back_kernel,
+        [((rows, width), BF, True), ((rows, cols), BF, True), ((8, width), F32)],
         [
-            (after(d_second, up_far), True),
+            (after(d_mixed, down_second), True),
             (part, True),
             (place.core_swap(part), True),
             (unit, True),
@@ -712,39 +681,41 @@
             norms,
             joined,
         ],
-        steps=4,
+        steps=2,
     )
     d_qkv, attn_sums = call(
-        functools.partial(attend_back_kernel, 128),
+        functools.partial(attend_back_kernel, rows),
         [((rows, 3 * cols), BF), ((8, 2 * cols), F32)],
         [d_ctx, qkv, (probs, True), ctx],
         scratch=[pltpu.VMEM((2, rows, rows), BF)],
         steps=cols // LANES,
     )
-    up_second = add(up_second, after(up_got_far, d_qkv))
+    attn_own, attn_first, attn_second, attn_far = outer_attn(
+        place, table, x, d_qkv, d_att, ctx,
+        (attn_sums, up_sums, totals_one, totals_two), depth,
+    )
+    attn_got_far = place.cross(attn_far, 0)
+    up_second = add(up_second, after(up_got_far, attn_far))
     up_got_second = place.cross(up_second, 1)
     up_got_first = place.cross(after(up_first, up_second), 0)
     down_sum = add_three(down_own, down_got_first, after(down_got_second, up_second))
-    grad_down = scatter_line(place, down_sum)
-    attn_own, attn_first, attn_second, attn_far = outer_attn(
-        place, table, x, after(d_qkv, up_second, down_sum), d_att, ctx,
-        (attn_sums, up_sums, totals_one, totals_two), depth,
-    )
-    attn_got_far = place.cross(attn_far, 0)
+    down_parts = scatter_parts(place, down_sum)
     (part,) = call(
         inputs_kernel,
         [((rows, width), BF, True)],
-        [(after(d_qkv, attn_far), True), joined],
+        [(after(d_qkv, down_sum), True), joined],
         steps=2,
     )
+    grad_in = d_att.astype(F32) + part.astype(F32) + place.core_swap(part).astype(F32)
     attn_second = add(attn_second, after(attn_got_far, part))
     attn_got_second = place.cross(attn_second, 1)
     attn_got_first = place.cross(after(attn_first, attn_second), 0)
+    grad_down = total_of(down_sum[0], down_parts)
     up_sum = add_three(up_own, up_got_first, after(up_got_second, attn_second))
-    grad_up = scatter_line(place, up_sum)
-    grad_in = d_first_in + part.astype(F32) + place.core_swap(part).astype(F32)
-    attn_sum = add_three(attn_own, after(attn_got_first, up_sum), attn_got_second)
-    attn_grad = scatter_line(place, attn_sum)
+    up_parts = scatter_parts(place, up_sum)
+    attn_sum = add_three(attn_own, after(attn_got_first, *down_parts, *up_parts), attn_got_second)
+    attn_grad = total_of(attn_sum[0], scatter_parts(place, attn_sum))
+    grad_up = total_of(up_sum[0], up_parts)
 
     def hand_back(full):
         mine = lax.dynamic_slice_in_dim(full, core * 2 * block, 2 * block, 0)

time: 247 us -> 201 us (0.81)
  Pallas kernels: 92 us -> 37.4 us
  starting transfers between devices: 48.1 us -> 55.3 us
  local copies, waits for them, and re-layouts: 14.6 us -> 18.1 us
    pallas_call x15, Pallas kernels: 92 us -> 37.4 us  [call(): pl.pallas_call(kernel, out_shape=[jax.ShapeDtypeStruct(shape, kind) for s...]
    unnamed x58 -> x80, local copies, waits for them, and re-layouts: 7.11 us -> 14.3 us
    ppermute x18, waiting for transfers between devices: 37.2 us -> 31.3 us  [cross(): return lax.ppermute(value, ('dp', 'mp'), pairs)]
    ppermute x18, starting transfers between devices: 23.7 us -> 29.6 us  [line_swap(): return lax.ppermute(value, 'dp', pairs)]
    ppermute x18, waiting for transfers between devices: 40.9 us -> 46.6 us  [line_swap(): return lax.ppermute(value, 'dp', pairs)]
  transfers between devices with their start and end apart: 45 -> 45, of which waited for: 17 -> 26; matrix products, arithmetic and copies ran while one was open for 7% -> 5% of each run, Pallas kernels for 28% -> 14%
where the time goes in v4:
time: 201 us
  waiting for transfers between devices  80.1 us (40%)
  starting transfers between devices  55.3 us (28%)
  Pallas kernels  37.4 us (19%)
  local copies, waits for them, and re-layouts  18.1 us (9%)
  other arithmetic  8.79 us (4%)
    ppermute x18, waiting for transfers between devices, line_swap(): return lax.ppermute(value, 'dp', pairs)  46.6 us
    pallas_call x15, Pallas kernels, call(): pl.pallas_call(kernel, out_shape=[jax.ShapeDtypeStruct(shape, kind) for s...  37.4 us
    ppermute x18, waiting for transfers between devices, cross(): return lax.ppermute(value, ('dp', 'mp'), pairs)  31.3 us
    ppermute x18, starting transfers between devices, line_swap(): return lax.ppermute(value, 'dp', pairs)  29.6 us
    ppermute x18, starting transfers between devices, cross(): return lax.ppermute(value, ('dp', 'mp'), pairs)  20.5 us
    unnamed x80, local copies, waits for them, and re-layouts  14.3 us
    ppermute x3, starting transfers between devices, row_swap(): return lax.ppermute(value, 'mp', [(0, 2), (2, 0), (1, 3), (3, 1)])  5.12 us
  transfers between devices with their start and end apart: 45, of which 26 were waited for; matrix products, arithmetic and copies ran while one was open for 5% of the time, Pallas kernels for 14%

profile of v4, /device:TPU:0, one launch (start us, length us, event | category | flops | bytes accessed | tf_op | source)
XLA Modules:
  0.0 201.1 jit_solution(17975223202907708785)
XLA Ops:
  2.1 3.0 %collective-permute-start = (bf16[2,128,768]{2,1,0:T(8,128)(2,1)S(1)}, bf16[2,128,768]{2,1,0:T(8,128)(2,1)S(1)}, u32[]{:S(2)}, u32[]{:S(2)}) collective-permute-start(bf16[2,128,768]{2,1,0:T(8,128)(2,1)S(1)} %pad_maximum_fusion.5), channel_id=1, source_target_pairs={{0,2},{2,0},{1,3},{3,1},{4,6},{6,4},{5,7},{7,5},{8,10},{10,8},{9,1... | collective-permute-start | bytes 1179656 | tf_op jit(solution)/shard_map/ppermute | solution.py:67
  5.4 3.7 %collective-permute-start.4 = (bf16[112,768]{1,0:T(8,128)(2,1)S(1)}, bf16[112,768]{1,0:T(8,128)(2,1)S(1)}, u32[]{:S(2)}, u32[]{:S(2)}) collective-permute-start(bf16[112,768]{1,0:T(8,128)(2,1)S(1)} %shard_map.169), channel_id=1, source_target_pairs={{0,24},{4,28},{8,16},{12,20},{16,8},{20,12},{24,0},{28,4},{1,25},{... | collective-permute-start | bytes 516104 | tf_op jit(solution)/shard_map/ppermute | solution.py:71
  9.8 4.8 %collective-permute-done.4 = bf16[112,768]{1,0:T(8,128)(2,1)S(1)} collective-permute-done((bf16[112,768]{1,0:T(8,128)(2,1)S(1)}, bf16[112,768]{1,0:T(8,128)(2,1)S(1)}, u32[]{:S(2)}, u32[]{:S(2)}) %collective-permute-start.4) | collective-permute-done | bytes 172064 | tf_op jit(solution)/shard_map/ppermute | solution.py:71
  14.6 8.8 %collective-permute-done.3 = bf16[112,768]{1,0:T(8,128)(2,1)S(1)} collective-permute-done((bf16[112,768]{1,0:T(8,128)(2,1)S(1)}, bf16[112,768]{1,0:T(8,128)(2,1)S(1)}, u32[]{:S(2)}, u32[]{:S(2)}) %collective-permute-start.3) | collective-permute-done | bytes 172064 | tf_op jit(solution)/shard_map/ppermute | solution.py:71
  29.0 6.1 %collective-permute-done.9 = bf16[96,768]{1,0:T(8,128)(2,1)S(1)} collective-permute-done((bf16[96,768]{1,0:T(8,128)(2,1)S(1)}, bf16[96,768]{1,0:T(8,128)(2,1)S(1)}, u32[]{:S(2)}, u32[]{:S(2)}) %collective-permute-start.9) | collective-permute-done | bytes 147488 | tf_op jit(solution)/shard_map/ppermute | solution.py:71
  35.1 4.0 %collective-permute-start.7 = (bf16[96,768]{1,0:T(8,128)(2,1)S(1)}, bf16[96,768]{1,0:T(8,128)(2,1)S(1)}, u32[]{:S(2)}, u32[]{:S(2)}) collective-permute-start(bf16[96,768]{1,0:T(8,128)(2,1)S(1)} %copy-done.35), channel_id=1, source_target_pairs={{0,8},{4,12},{8,0},{12,4},{16,24},{20,28},{24,16},{28,20},{1,9},{5... | collective-permute-start | bytes 442376 | tf_op jit(solution)/shard_map/ppermute | solution.py:71
  55.3 4.7 %collective-permute-done.14 = bf16[96,768]{1,0:T(8,128)(2,1)S(1)} collective-permute-done((bf16[96,768]{1,0:T(8,128)(2,1)S(1)}, bf16[96,768]{1,0:T(8,128)(2,1)S(1)}, u32[]{:S(2)}, u32[]{:S(2)}) %collective-permute-start.14) | collective-permute-done | bytes 147488 | tf_op jit(solution)/shard_map/ppermute | solution.py:71
  75.6 4.5 %shard_map.172 = (bf16[6,512,512]{2,1,0:T(8,128)(2,1)S(1)}, bf16[512,384]{1,0:T(8,128)(2,1)S(1)}, bf16[512,768]{1,0:T(8,128)(2,1)S(1)}) custom-call(s32[4]{0:T(128)S(1)} %bitcast.106, bf16[512,1152]{1,0:T(8,128)(2,1)S(1)} %copy-done.24, bf16[768,1536]{1,0:T(8,128)(2,1)S(1)} %copy-done.17), custom_call_target="tpu_custom_call" | custom-call | flops 8000000000 | bytes 10000000 | tf_op jit(solution)/shard_map/pallas_call | solution.py:38
  82.6 3.1 %collective-permute-done.19.first = bf16[4,96,768]{2,1,0:T(8,128)(2,1)} collective-permute-done((bf16[4,96,768]{2,1,0:T(8,128)(2,1)S(1)}, bf16[4,96,768]{2,1,0:T(8,128)(2,1)}, u32[]{:S(2)}, u32[]{:S(2)}) %collective-permute-start.19) | collective-permute-done | bytes 589856 | tf_op jit(solution)/shard_map/ppermute | solution.py:81
  90.4 3.1 %shard_map.174 = (bf16[512,768]{1,0:T(8,128)(2,1)S(1)}, f32[512,128]{1,0:T(8,128)S(1)}, bf16[512,768]{1,0:T(8,128)(2,1)S(1)}, bf16[512,1536]{1,0:T(8,128)(2,1)S(1)}, bf16[512,1536]{1,0:T(8,128)(2,1)S(1)}) custom-call(bf16[512,768]{1,0:T(8,128)(2,1)S(1)} %get-tuple-element.153.x, bf16[512,768]{1,0:T(8,128)(2,1)S(1)} %get-tuple-element.86.mine, ...), custom_call_target="tpu_custom_call" | custom-call | flops 8000000000 | bytes 10000000 | tf_op jit(solution)/shard_map/pallas_call | solution.py:38
  95.8 3.7 %shard_map.175 = (bf16[512,768]{1,0:T(8,128)(2,1)S(1)}, bf16[2,768,768]{2,1,0:T(8,128)(2,1)S(1)}) custom-call(s32[9]{0:T(128)S(1)} %stack.188.where, bf16[512,1536]{1,0:T(8,128)(2,1)S(1)} %get-tuple-element.92.activated.right, bf16[4,96,768]{2,1,0:T(8,128)(2,1)S(1)} %pad_maximum_fusion.3.own, bf16[4,96,768]{2,1,0:T(8,128)(2,1)} %collective-permute-done.19.first, ...), custom_call_target="tpu_custom_call" | custom-call | flops 8000000000 | bytes 10000000 | tf_op jit(solution)/shard_map/pallas_call | solution.py:38
  106.1 3.0 %shard_map.177 = (bf16[4,96,768]{2,1,0:T(8,128)(2,1)S(1)}, bf16[4,96,768]{2,1,0:T(8,128)(2,1)S(1)}, bf16[4,96,768]{2,1,0:T(8,128)(2,1)S(1)}, bf16[4,96,768]{2,1,0:T(8,128)(2,1)S(1)}) custom-call(s32[6]{0:T(128)S(1)} %stack.213.table, bf16[512,768]{1,0:T(8,128)(2,1)S(1)} %get-tuple-element.105.left.d_mixed.d_second, bf16[512,1536]{1,0:T(8,128)(2,1)S(1)} %copy-done.22), custom_call_target="tpu_custom_call" | custom-call | flops 8000000000 | bytes 10000000 | tf_op jit(solution)/shard_map/pallas_call | solution.py:38
  111.2 3.4 %shard_map.178 = (bf16[512,1536]{1,0:T(8,128)(2,1)S(1)}, bf16[512,768]{1,0:T(8,128)(2,1)S(1)}, f32[8,1536]{1,0:T(8,128)S(1)}) custom-call(bf16[512,768]{1,0:T(8,128)(2,1)S(1)} %get-tuple-element.105.left.d_mixed.d_second, bf16[2,768,768]{2,1,0:T(8,128)(2,1)S(1)} %copy-done.15, bf16[2,768,768]{2,1,0:T(8,128)(2,1)S(1)} %copy-done.13, ...), custom_call_target="tpu_custom_call" | custom-call | flops 8000000000 | bytes 10000000 | tf_op jit(solution)/shard_map/pallas_call | solution.py:38
  114.8 2.8 %shard_map.179 = (bf16[4,96,768]{2,1,0:T(8,128)(2,1)S(1)}, bf16[4,96,768]{2,1,0:T(8,128)(2,1)S(1)}, bf16[4,96,768]{2,1,0:T(8,128)(2,1)S(1)}, bf16[4,96,768]{2,1,0:T(8,128)(2,1)S(1)}) custom-call(s32[6]{0:T(128)S(1)} %stack.213.table, bf16[512,768]{1,0:T(8,128)(2,1)S(1)} %copy-done.30, bf16[512,1536]{1,0:T(8,128)(2,1)S(1)} %get-tuple-element.102.right), custom_call_target="tpu_custom_call" | custom-call | flops 8000000000 | bytes 10000000 | tf_op jit(solution)/shard_map/pallas_call | solution.py:38
  124.0 3.9 %shard_map.181 = (bf16[512,1152]{1,0:T(8,128)(2,1)S(1)}, f32[8,768]{1,0:T(8,128)S(1)}) custom-call(bf16[512,384]{1,0:T(8,128)(2,1)S(1)} %get-tuple-element.108.d_ctx, bf16[512,1152]{1,0:T(8,128)(2,1)S(1)} %copy-done.25, bf16[6,512,512]{2,1,0:T(8,128)(2,1)S(1)} %copy-done.11, bf16[512,384]{1,0:T(8,128)(2,1)S(1)} %copy-done.32), custom_call_target="tpu_custom_call" | custom-call | flops 8000000000 | bytes 10000000 | tf_op jit(solution)/shard_map/pallas_call | solution.py:38
  127.9 3.5 %shard_map.182 = (bf16[4,112,768]{2,1,0:T(8,128)(2,1)S(1)}, bf16[4,112,768]{2,1,0:T(8,128)(2,1)S(1)}, bf16[4,112,768]{2,1,0:T(8,128)(2,1)S(1)}, bf16[4,112,768]{2,1,0:T(8,128)(2,1)S(1)}) custom-call(s32[6]{0:T(128)S(1)} %stack.213.table, bf16[512,768]{1,0:T(8,128)(2,1)S(1)} %get-tuple-element.153.x, bf16[512,1152]{1,0:T(8,128)(2,1)S(1)} %get-tuple-element.127.d_qkv, ...), custom_call_target="tpu_custom_call" | custom-call | flops 8000000000 | bytes 10000000 | tf_op jit(solution)/shard_map/pallas_call | solution.py:38
  132.0 6.0 %collective-permute-done.28 = bf16[4,96,768]{2,1,0:T(8,128)(2,1)S(1)} collective-permute-done((bf16[4,96,768]{2,1,0:T(8,128)(2,1)S(1)}, bf16[4,96,768]{2,1,0:T(8,128)(2,1)S(1)}, u32[]{:S(2)}, u32[]{:S(2)}) %collective-permute-start.28) | collective-permute-done | bytes 589856 | tf_op jit(solution)/shard_map/ppermute | solution.py:81
  144.8 5.8 %collective-permute-done.25 = bf16[4,112,768]{2,1,0:T(8,128)(2,1)S(1)} collective-permute-done((bf16[4,112,768]{2,1,0:T(8,128)(2,1)S(1)}, bf16[4,112,768]{2,1,0:T(8,128)(2,1)S(1)}, u32[]{:S(2)}, u32[]{:S(2)}) %collective-permute-start.25) | collective-permute-done | bytes 688160 | tf_op jit(solution)/shard_map/ppermute | solution.py:81
  150.8 3.7 %collective-permute-done.34 = bf16[4,96,768]{2,1,0:T(8,128)(2,1)S(1)} collective-permute-done((bf16[4,96,768]{2,1,0:T(8,128)(2,1)S(1)}, bf16[4,96,768]{2,1,0:T(8,128)(2,1)S(1)}, u32[]{:S(2)}, u32[]{:S(2)}) %collective-permute-start.34) | collective-permute-done | bytes 589856 | tf_op jit(solution)/shard_map/ppermute | solution.py:81
  155.0 3.0 %collective-permute-done.33 = bf16[4,96,768]{2,1,0:T(8,128)(2,1)S(1)} collective-permute-done((bf16[4,96,768]{2,1,0:T(8,128)(2,1)S(1)}, bf16[4,96,768]{2,1,0:T(8,128)(2,1)S(1)}, u32[]{:S(2)}, u32[]{:S(2)}) %collective-permute-start.33) | collective-permute-done | bytes 589856 | tf_op jit(solution)/shard_map/ppermute | solution.py:81
  163.4 3.3 %collective-permute-done.37 = bf16[96,768]{1,0:T(8,128)(2,1)S(1)} collective-permute-done((bf16[96,768]{1,0:T(8,128)(2,1)S(1)}, bf16[96,768]{1,0:T(8,128)(2,1)S(1)}, u32[]{:S(2)}, u32[]{:S(2)}) %collective-permute-start.37) | collective-permute-done | bytes 147488 | tf_op jit(solution)/shard_map/ppermute | solution.py:71
  166.7 4.9 %collective-permute-start.35 = (bf16[96,768]{1,0:T(8,128)(2,1)S(1)}, bf16[96,768]{1,0:T(8,128)(2,1)S(1)}, u32[]{:S(2)}, u32[]{:S(2)}) collective-permute-start(bf16[96,768]{1,0:T(8,128)(2,1)S(1)} %get-tuple-element.161), channel_id=1, source_target_pairs={{0,8},{4,12},{8,0},{12,4},{16,24},{20,28},{24,16},{28,20},{1,9},{5... | collective-permute-start | bytes 442376 | tf_op jit(solution)/shard_map/ppermute | solution.py:71
  184.2 3.4 %collective-permute-done.42 = bf16[112,768]{1,0:T(8,128)(2,1)S(1)} collective-permute-done((bf16[112,768]{1,0:T(8,128)(2,1)S(1)}, bf16[112,768]{1,0:T(8,128)(2,1)S(1)}, u32[]{:S(2)}, u32[]{:S(2)}) %collective-permute-start.42) | collective-permute-done | bytes 172064 | tf_op jit(solution)/shard_map/ppermute | solution.py:71
  189.3 6.6 %collective-permute-done.43 = bf16[112,768]{1,0:T(8,128)(2,1)S(1)} collective-permute-done((bf16[112,768]{1,0:T(8,128)(2,1)S(1)}, bf16[112,768]{1,0:T(8,128)(2,1)S(1)}, u32[]{:S(2)}, u32[]{:S(2)}) %collective-permute-start.43) | collective-permute-done | bytes 172064 | tf_op jit(solution)/shard_map/ppermute | solution.py:71
  (204 shorter events, 96.9 us)
Async XLA Ops:
  2.1 21.3 %collective-permute-start = (bf16[2,128,768]{2,1,0:T(8,128)(2,1)S(1)}, bf16[2,128,768]{2,1,0:T(8,128)(2,1)S(1)}, u32[]{:S(2)}, u32[]{:S(2)}) collective-permute-start(bf16[2,128,768]{2,1,0:T(8,128)(2,1)S(1)} %pad_maximum_fusion.5), channel_id=1, source_target_pairs={{0,2},{2,0},{1,3},{3,1},{4,6},{6,4},{5,7},{7,5},{8,10},{10,8},{9,1... | collective-permute-start | bytes 1179656 | tf_op jit(solution)/shard_map/ppermute | solution.py:67
  9.1 14.3 %collective-permute-start.3 = (bf16[112,768]{1,0:T(8,128)(2,1)S(1)}, bf16[112,768]{1,0:T(8,128)(2,1)S(1)}, u32[]{:S(2)}, u32[]{:S(2)}) collective-permute-start(bf16[112,768]{1,0:T(8,128)(2,1)S(1)} %shard_map.169), channel_id=1, source_target_pairs={{0,16},{4,20},{8,24},{12,28},{16,0},{20,4},{24,8},{28,12},{1,17},{... | collective-permute-start | bytes 516104 | tf_op jit(solution)/shard_map/ppermute | solution.py:71
  23.5 19.9 %collective-permute-start.6 = (bf16[4,112,768]{2,1,0:T(8,128)(2,1)S(1)}, bf16[4,112,768]{2,1,0:T(8,128)(2,1)S(1)}, u32[]{:S(2)}, u32[]{:S(2)}) collective-permute-start(bf16[4,112,768]{2,1,0:T(8,128)(2,1)S(1)} %pad_maximum_fusion.1.own), channel_id=1, source_target_pairs={{0,4},{1,3},{2,6},{3,1},{4,0},{5,7},{6,2},{7,5},{8,12},{9,11},{10,... | collective-permute-start | bytes 2064392 | tf_op jit(solution)/shard_map/ppermute | solution.py:81
  25.0 19.2 %collective-permute-start.5 = (bf16[4,112,768]{2,1,0:T(8,128)(2,1)S(1)}, bf16[4,112,768]{2,1,0:T(8,128)(2,1)}, u32[]{:S(2)}, u32[]{:S(2)}) collective-permute-start(bf16[4,112,768]{2,1,0:T(8,128)(2,1)S(1)} %pad_maximum_fusion.1.own), channel_id=1, source_target_pairs={{0,2},{1,5},{2,0},{3,7},{4,6},{5,1},{6,4},{7,3},{8,10},{9,13},{10,... | collective-permute-start | bytes 2064392 | tf_op jit(solution)/shard_map/ppermute | solution.py:81
  26.5 23.0 %collective-permute-start.1 = (bf16[2,256,768]{2,1,0:T(8,128)(2,1)}, bf16[2,256,768]{2,1,0:T(8,128)(2,1)}, u32[]{:S(2)}, u32[]{:S(2)}) collective-permute-start(bf16[2,256,768]{2,1,0:T(8,128)(2,1)} %pad_maximum_fusion), channel_id=1, source_target_pairs={{0,1},{1,0},{2,3},{3,2},{4,5},{5,4},{6,7},{7,6},{8,9},{9,8},{10,11... | collective-permute-start | bytes 2359304 | tf_op jit(solution)/shard_map/ppermute | solution.py:64
  44.2 15.8 %collective-permute-start.10 = (bf16[4,112,768]{2,1,0:T(8,128)(2,1)}, bf16[4,112,768]{2,1,0:T(8,128)(2,1)}, u32[]{:S(2)}, u32[]{:S(2)}) collective-permute-start(bf16[4,112,768]{2,1,0:T(8,128)(2,1)} %collective-permute-done.5.first), channel_id=1, source_target_pairs={{0,4},{1,3},{2,6},{3,1},{4,0},{5,7},{6,2},{7,5},{8,12},{9,11},{10,... | collective-permute-start | bytes 2064392 | tf_op jit(solution)/shard_map/ppermute | solution.py:81
  49.5 18.5 %collective-permute-start.12 = (bf16[4,96,768]{2,1,0:T(8,128)(2,1)S(1)}, bf16[4,96,768]{2,1,0:T(8,128)(2,1)S(1)}, u32[]{:S(2)}, u32[]{:S(2)}) collective-permute-start(bf16[4,96,768]{2,1,0:T(8,128)(2,1)S(1)} %pad_maximum_fusion.2.own), channel_id=1, source_target_pairs={{0,4},{1,3},{2,6},{3,1},{4,0},{5,7},{6,2},{7,5},{8,12},{9,11},{10,... | collective-permute-start | bytes 1769480 | tf_op jit(solution)/shard_map/ppermute | solution.py:81
  53.8 15.1 %collective-permute-start.11 = (bf16[4,96,768]{2,1,0:T(8,128)(2,1)S(1)}, bf16[4,96,768]{2,1,0:T(8,128)(2,1)}, u32[]{:S(2)}, u32[]{:S(2)}) collective-permute-start(bf16[4,96,768]{2,1,0:T(8,128)(2,1)S(1)} %pad_maximum_fusion.2.own), channel_id=1, source_target_pairs={{0,2},{1,5},{2,0},{3,7},{4,6},{5,1},{6,4},{7,3},{8,10},{9,13},{10,... | collective-permute-start | bytes 1769480 | tf_op jit(solution)/shard_map/ppermute | solution.py:81
  69.4 16.4 %collective-permute-start.19 = (bf16[4,96,768]{2,1,0:T(8,128)(2,1)S(1)}, bf16[4,96,768]{2,1,0:T(8,128)(2,1)}, u32[]{:S(2)}, u32[]{:S(2)}) collective-permute-start(bf16[4,96,768]{2,1,0:T(8,128)(2,1)S(1)} %pad_maximum_fusion.3.own), channel_id=1, source_target_pairs={{0,2},{1,5},{2,0},{3,7},{4,6},{5,1},{6,4},{7,3},{8,10},{9,13},{10,... | collective-permute-start | bytes 1769480 | tf_op jit(solution)/shard_map/ppermute | solution.py:81
  70.9 18.0 %collective-permute-start.18 = (bf16[4,96,768]{2,1,0:T(8,128)(2,1)}, bf16[4,96,768]{2,1,0:T(8,128)(2,1)}, u32[]{:S(2)}, u32[]{:S(2)}) collective-permute-start(bf16[4,96,768]{2,1,0:T(8,128)(2,1)} %collective-permute-done.11.first), channel_id=1, source_target_pairs={{0,4},{1,3},{2,6},{3,1},{4,0},{5,7},{6,2},{7,5},{8,12},{9,11},{10,... | collective-permute-start | bytes 1769480 | tf_op jit(solution)/shard_map/ppermute | solution.py:81
  110.7 28.4 %collective-permute-start.26 = (bf16[4,96,768]{2,1,0:T(8,128)(2,1)S(1)}, bf16[4,96,768]{2,1,0:T(8,128)(2,1)S(1)}, u32[]{:S(2)}, u32[]{:S(2)}) collective-permute-start(bf16[4,96,768]{2,1,0:T(8,128)(2,1)S(1)} %get-tuple-element.122), channel_id=1, source_target_pairs={{0,2},{1,5},{2,0},{3,7},{4,6},{5,1},{6,4},{7,3},{8,10},{9,13},{10,... | collective-permute-start | bytes 1769480 | tf_op jit(solution)/shard_map/ppermute | solution.py:81
  119.2 19.9 %collective-permute-start.27 = (bf16[4,96,768]{2,1,0:T(8,128)(2,1)S(1)}, bf16[4,96,768]{2,1,0:T(8,128)(2,1)S(1)}, u32[]{:S(2)}, u32[]{:S(2)}) collective-permute-start(bf16[4,96,768]{2,1,0:T(8,128)(2,1)S(1)} %add_convert_fusion.2), channel_id=1, source_target_pairs={{0,4},{1,3},{2,6},{3,1},{4,0},{5,7},{6,2},{7,5},{8,12},{9,11},{10,... | collective-permute-start | bytes 1769480 | tf_op jit(solution)/shard_map/ppermute | solution.py:81
  120.1 17.9 %collective-permute-start.28 = (bf16[4,96,768]{2,1,0:T(8,128)(2,1)S(1)}, bf16[4,96,768]{2,1,0:T(8,128)(2,1)S(1)}, u32[]{:S(2)}, u32[]{:S(2)}) collective-permute-start(bf16[4,96,768]{2,1,0:T(8,128)(2,1)S(1)} %get-tuple-element.124), channel_id=1, source_target_pairs={{0,2},{1,5},{2,0},{3,7},{4,6},{5,1},{6,4},{7,3},{8,10},{9,13},{10,... | collective-permute-start | bytes 1769480 | tf_op jit(solution)/shard_map/ppermute | solution.py:81
  131.4 19.2 %collective-permute-start.25 = (bf16[4,112,768]{2,1,0:T(8,128)(2,1)S(1)}, bf16[4,112,768]{2,1,0:T(8,128)(2,1)S(1)}, u32[]{:S(2)}, u32[]{:S(2)}) collective-permute-start(bf16[4,112,768]{2,1,0:T(8,128)(2,1)S(1)} %get-tuple-element.119), channel_id=1, source_target_pairs={{0,2},{1,5},{2,0},{3,7},{4,6},{5,1},{6,4},{7,3},{8,10},{9,13},{10,... | collective-permute-start | bytes 2064392 | tf_op jit(solution)/shard_map/ppermute | solution.py:81
  138.2 16.3 %collective-permute-start.34 = (bf16[4,96,768]{2,1,0:T(8,128)(2,1)S(1)}, bf16[4,96,768]{2,1,0:T(8,128)(2,1)S(1)}, u32[]{:S(2)}, u32[]{:S(2)}) collective-permute-start(bf16[4,96,768]{2,1,0:T(8,128)(2,1)S(1)} %add_convert_fusion.1), channel_id=1, source_target_pairs={{0,4},{1,3},{2,6},{3,1},{4,0},{5,7},{6,2},{7,5},{8,12},{9,11},{10,... | collective-permute-start | bytes 1769480 | tf_op jit(solution)/shard_map/ppermute | solution.py:81
  139.3 18.7 %collective-permute-start.33 = (bf16[4,96,768]{2,1,0:T(8,128)(2,1)S(1)}, bf16[4,96,768]{2,1,0:T(8,128)(2,1)S(1)}, u32[]{:S(2)}, u32[]{:S(2)}) collective-permute-start(bf16[4,96,768]{2,1,0:T(8,128)(2,1)S(1)} %get-tuple-element.132), channel_id=1, source_target_pairs={{0,2},{1,5},{2,0},{3,7},{4,6},{5,1},{6,4},{7,3},{8,10},{9,13},{10,... | collective-permute-start | bytes 1769480 | tf_op jit(solution)/shard_map/ppermute | solution.py:81
  142.4 18.6 %collective-permute-start.32 = (bf16[96,768]{1,0:T(8,128)(2,1)S(1)}, bf16[96,768]{1,0:T(8,128)(2,1)S(1)}, u32[]{:S(2)}, u32[]{:S(2)}) collective-permute-start(bf16[96,768]{1,0:T(8,128)(2,1)S(1)} %get-tuple-element.162), channel_id=1, source_target_pairs={{0,24},{4,28},{8,16},{12,20},{16,8},{20,12},{24,0},{28,4},{1,25},{... | collective-permute-start | bytes 442376 | tf_op jit(solution)/shard_map/ppermute | solution.py:71
  144.8 16.9 %collective-permute-start.31 = (bf16[96,768]{1,0:T(8,128)(2,1)S(1)}, bf16[96,768]{1,0:T(8,128)(2,1)S(1)}, u32[]{:S(2)}, u32[]{:S(2)}) collective-permute-start(bf16[96,768]{1,0:T(8,128)(2,1)S(1)} %get-tuple-element.163), channel_id=1, source_target_pairs={{0,16},{4,20},{8,24},{12,28},{16,0},{20,4},{24,8},{28,12},{1,17},{... | collective-permute-start | bytes 442376 | tf_op jit(solution)/shard_map/ppermute | solution.py:71
  150.6 24.9 %collective-permute-start.40 = (bf16[512,768]{1,0:T(8,128)(2,1)S(1)}, bf16[512,768]{1,0:T(8,128)(2,1)S(1)}, u32[]{:S(2)}, u32[]{:S(2)}) collective-permute-start(bf16[512,768]{1,0:T(8,128)(2,1)S(1)} %shard_map.183), channel_id=1, source_target_pairs={{0,1},{1,0},{2,3},{3,2},{4,5},{5,4},{6,7},{7,6},{8,9},{9,8},{10,11... | collective-permute-start | bytes 2359304 | tf_op jit(solution)/shard_map/ppermute | solution.py:64
  161.0 17.1 %collective-permute-start.38 = (bf16[4,112,768]{2,1,0:T(8,128)(2,1)S(1)}, bf16[4,112,768]{2,1,0:T(8,128)(2,1)S(1)}, u32[]{:S(2)}, u32[]{:S(2)}) collective-permute-start(bf16[4,112,768]{2,1,0:T(8,128)(2,1)S(1)} %add_convert_fusion), channel_id=1, source_target_pairs={{0,4},{1,3},{2,6},{3,1},{4,0},{5,7},{6,2},{7,5},{8,12},{9,11},{10,... | collective-permute-start | bytes 2064392 | tf_op jit(solution)/shard_map/ppermute | solution.py:81
  161.7 15.7 %collective-permute-start.29 = (bf16[4,112,768]{2,1,0:T(8,128)(2,1)S(1)}, bf16[4,112,768]{2,1,0:T(8,128)(2,1)S(1)}, u32[]{:S(2)}, u32[]{:S(2)}) collective-permute-start(bf16[4,112,768]{2,1,0:T(8,128)(2,1)S(1)} %get-tuple-element.129), channel_id=1, source_target_pairs={{0,2},{1,5},{2,0},{3,7},{4,6},{5,1},{6,4},{7,3},{8,10},{9,13},{10,... | collective-permute-start | bytes 2064392 | tf_op jit(solution)/shard_map/ppermute | solution.py:81
  180.3 15.5 %collective-permute-start.43 = (bf16[112,768]{1,0:T(8,128)(2,1)S(1)}, bf16[112,768]{1,0:T(8,128)(2,1)S(1)}, u32[]{:S(2)}, u32[]{:S(2)}) collective-permute-start(bf16[112,768]{1,0:T(8,128)(2,1)S(1)} %get-tuple-element.158), channel_id=1, source_target_pairs={{0,16},{4,20},{8,24},{12,28},{16,0},{20,4},{24,8},{28,12},{1,17},{... | collective-permute-start | bytes 516104 | tf_op jit(solution)/shard_map/ppermute | solution.py:71
  182.1 17.2 %collective-permute-start.39 = (bf16[128,768]{1,0:T(8,128)(2,1)S(1)}, bf16[128,768]{1,0:T(8,128)(2,1)S(1)}, u32[]{:S(2)}, u32[]{:S(2)}) collective-permute-start(bf16[128,768]{1,0:T(8,128)(2,1)S(1)} %get-tuple-element.135), channel_id=1, source_target_pairs={{0,2},{2,0},{1,3},{3,1},{4,6},{6,4},{5,7},{7,5},{8,10},{10,8},{9,1... | collective-permute-start | bytes 589832 | tf_op jit(solution)/shard_map/ppermute | solution.py:67
  183.2 16.9 %collective-permute-start.41 = (bf16[128,768]{1,0:T(8,128)(2,1)S(1)}, bf16[128,768]{1,0:T(8,128)(2,1)S(1)}, u32[]{:S(2)}, u32[]{:S(2)}) collective-permute-start(bf16[128,768]{1,0:T(8,128)(2,1)S(1)} %fusion.10), channel_id=1, source_target_pairs={{0,2},{2,0},{1,3},{3,1},{4,6},{6,4},{5,7},{7,5},{8,10},{10,8},{9,1... | collective-permute-start | bytes 589832 | tf_op jit(solution)/shard_map/ppermute | solution.py:67
  (60 other events, 401.0 us)

commit v5 on v4

--- a/solution.py
+++ b/solution.py
@@ -544,6 +544,41 @@
     attn[depth:, :] = jnp.concatenate(small, axis=0).astype(BF)
 
 
+def unpack_kernel(count, own, *refs):
+    parts, (qkv, out, unit, gain, bias) = refs[:count], refs[count:]
+    total = own[...]
+    for part in parts:
+        total = total + part[...].astype(F32)
+    depth, cols = qkv.shape[1], qkv.shape[2]
+    for kind in range(3):
+        qkv[kind] = total[:depth, kind * cols : (kind + 1) * cols]
+    out[...] = total[:depth, 3 * cols :].T
+    extra = total[depth:]
+    unit[...] = extra[0:1, : unit.shape[1]]
+    gain[...] = extra[1:3, : gain.shape[1]]
+    bias[...] = extra[3:7, : bias.shape[1]]
+
+
+def unpack(own, parts, depth, cols, share, small):
+    outs = [
+        ((3, depth, cols), F32),
+        ((cols, depth), F32),
+        ((1, share), F32),
+        ((2, small), F32),
+        ((4, small), F32),
+    ]
+    if depth % 16 == 0:
+        return call(functools.partial(unpack_kernel, len(parts)), outs, [own] + list(parts))
+    total = total_of(own, parts)
+    return (
+        jnp.stack([total[:depth, t * cols : (t + 1) * cols] for t in range(3)]),
+        total[:depth, 3 * cols :].T,
+        total[depth : depth + 1, :share],
+        total[depth + 1 : depth + 3, :small],
+        total[depth + 3 : depth + 7, :small],
+    )
+
+
 def body(
     inputs, w_qkv, w_out, w_up, w_down, unit_bias, norm_gain, norm_bias, seq_lengths, cotangent
 ):
@@ -714,7 +749,7 @@
     up_sum = add_three(up_own, up_got_first, after(up_got_second, attn_second))
     up_parts = scatter_parts(place, up_sum)
     attn_sum = add_three(attn_own, after(attn_got_first, *down_parts, *up_parts), attn_got_second)
-    attn_grad = total_of(attn_sum[0], scatter_parts(place, attn_sum))
+    attn_start, attn_parts = attn_sum[0], scatter_parts(place, attn_sum)
     grad_up = total_of(up_sum[0], up_parts)
 
     def hand_back(full):
@@ -724,22 +759,23 @@
         got = place.row_swap(after(keep(mine, 1 - row).astype(BF), attn_sum)).astype(full.dtype)
         return jnp.where(row == 0, jnp.stack([kept, got]), jnp.stack([got, kept]))
 
-    grad_qkv = jnp.stack(
-        [attn_grad[:depth, t * head_cols : (t + 1) * head_cols] for t in range(3)]
-    )
-    grad_out = jnp.transpose(attn_grad[:depth, 3 * head_cols :])
-    norm_grad = attn_grad[depth + 1 : depth + 7, :small]
+    outputs, grad_inputs = hand_back(result), hand_back(grad_in)
+    attn_parts = [after(part, outputs, grad_inputs) for part in attn_parts]
+    grad_qkv, grad_out, grad_unit, grad_gain, grad_bias = unpack(
+        attn_start, attn_parts, depth, head_cols, share, small
+    )
     return (
-        hand_back(result),
-        hand_back(grad_in),
+        outputs,
+        grad_inputs,
         grad_qkv,
         grad_out,
         grad_up,
         jnp.transpose(grad_down),
-        attn_grad[depth : depth + 1, :share],
-        norm_grad[:2],
-        norm_grad[2:],
-    )
+        grad_unit,
+        grad_gain,
+        grad_bias,
+    )
+
 
 def solution(mesh):
     placed = (

time: 201 us -> 195 us (0.970)
  waiting for transfers between devices: 80.1 us -> 75.6 us
  local copies, waits for them, and re-layouts: 18.1 us -> 15.6 us
    ppermute x18, waiting for transfers between devices: 46.6 us -> 35.2 us  [line_swap(): return lax.ppermute(value, 'dp', pairs)]
    ppermute x3, waiting for transfers between devices: 0.01 us -> 6.96 us  [row_swap(): return lax.ppermute(value, 'mp', [(0, 2), (2, 0), (1, 3), (3, 1)])]
    pallas_call x15 -> x16, Pallas kernels: 37.4 us -> 38.3 us  [call(): pl.pallas_call(kernel, out_shape=[jax.ShapeDtypeStruct(shape, kind) for s...]
    unnamed x80 -> x79, local copies, waits for them, and re-layouts: 14.3 us -> 13.5 us
  transfers between devices with their start and end apart: 45 -> 45, of which waited for: 26 -> 25; matrix products, arithmetic and copies ran while one was open for 5% -> 4% of each run, Pallas kernels for 14% -> 15%
where the time goes in v5:
time: 195 us
  waiting for transfers between devices  75.6 us (39%)
  starting transfers between devices  56.1 us (29%)
  Pallas kernels  38.3 us (20%)
  local copies, waits for them, and re-layouts  15.6 us (8%)
  other arithmetic  7.96 us (4%)
    pallas_call x16, Pallas kernels, call(): pl.pallas_call(kernel, out_shape=[jax.ShapeDtypeStruct(shape, kind) for s...  38.3 us
    ppermute x18, waiting for transfers between devices, line_swap(): return lax.ppermute(value, 'dp', pairs)  35.2 us
    ppermute x18, waiting for transfers between devices, cross(): return lax.ppermute(value, ('dp', 'mp'), pairs)  31.2 us
    ppermute x18, starting transfers between devices, line_swap(): return lax.ppermute(value, 'dp', pairs)  30.4 us
    ppermute x18, starting transfers between devices, cross(): return lax.ppermute(value, ('dp', 'mp'), pairs)  20.5 us
    unnamed x79, local copies, waits for them, and re-layouts  13.5 us
    ppermute x3, waiting for transfers between devices, row_swap(): return lax.ppermute(value, 'mp', [(0, 2), (2, 0), (1, 3), (3, 1)])  6.96 us
    ppermute x3, starting transfers between devices, row_swap(): return lax.ppermute(value, 'mp', [(0, 2), (2, 0), (1, 3), (3, 1)])  5.06 us
  transfers between devices with their start and end apart: 45, of which 25 were waited for; matrix products, arithmetic and copies ran while one was open for 4% of the time, Pallas kernels for 15%

profile of v5, /device:TPU:0, one launch (start us, length us, event | category | flops | bytes accessed | tf_op | source)
XLA Modules:
  0.0 194.9 jit_solution(14651631863821581813)
XLA Ops:
  2.1 3.0 %collective-permute-start = (bf16[2,128,768]{2,1,0:T(8,128)(2,1)S(1)}, bf16[2,128,768]{2,1,0:T(8,128)(2,1)S(1)}, u32[]{:S(2)}, u32[]{:S(2)}) collective-permute-start(bf16[2,128,768]{2,1,0:T(8,128)(2,1)S(1)} %pad_maximum_fusion.5), channel_id=1, source_target_pairs={{0,2},{2,0},{1,3},{3,1},{4,6},{6,4},{5,7},{7,5},{8,10},{10,8},{9,1... | collective-permute-start | bytes 1179656 | tf_op jit(solution)/shard_map/ppermute | solution.py:67
  5.4 3.7 %collective-permute-start.4 = (bf16[112,768]{1,0:T(8,128)(2,1)S(1)}, bf16[112,768]{1,0:T(8,128)(2,1)S(1)}, u32[]{:S(2)}, u32[]{:S(2)}) collective-permute-start(bf16[112,768]{1,0:T(8,128)(2,1)S(1)} %shard_map.169), channel_id=1, source_target_pairs={{0,24},{4,28},{8,16},{12,20},{16,8},{20,12},{24,0},{28,4},{1,25},{... | collective-permute-start | bytes 516104 | tf_op jit(solution)/shard_map/ppermute | solution.py:71
  9.8 4.8 %collective-permute-done.4 = bf16[112,768]{1,0:T(8,128)(2,1)S(1)} collective-permute-done((bf16[112,768]{1,0:T(8,128)(2,1)S(1)}, bf16[112,768]{1,0:T(8,128)(2,1)S(1)}, u32[]{:S(2)}, u32[]{:S(2)}) %collective-permute-start.4) | collective-permute-done | bytes 172064 | tf_op jit(solution)/shard_map/ppermute | solution.py:71
  14.6 8.8 %collective-permute-done.3 = bf16[112,768]{1,0:T(8,128)(2,1)S(1)} collective-permute-done((bf16[112,768]{1,0:T(8,128)(2,1)S(1)}, bf16[112,768]{1,0:T(8,128)(2,1)S(1)}, u32[]{:S(2)}, u32[]{:S(2)}) %collective-permute-start.3) | collective-permute-done | bytes 172064 | tf_op jit(solution)/shard_map/ppermute | solution.py:71
  29.0 6.1 %collective-permute-done.9 = bf16[96,768]{1,0:T(8,128)(2,1)S(1)} collective-permute-done((bf16[96,768]{1,0:T(8,128)(2,1)S(1)}, bf16[96,768]{1,0:T(8,128)(2,1)S(1)}, u32[]{:S(2)}, u32[]{:S(2)}) %collective-permute-start.9) | collective-permute-done | bytes 147488 | tf_op jit(solution)/shard_map/ppermute | solution.py:71
  35.1 4.0 %collective-permute-start.7 = (bf16[96,768]{1,0:T(8,128)(2,1)S(1)}, bf16[96,768]{1,0:T(8,128)(2,1)S(1)}, u32[]{:S(2)}, u32[]{:S(2)}) collective-permute-start(bf16[96,768]{1,0:T(8,128)(2,1)S(1)} %copy-done.35), channel_id=1, source_target_pairs={{0,8},{4,12},{8,0},{12,4},{16,24},{20,28},{24,16},{28,20},{1,9},{5... | collective-permute-start | bytes 442376 | tf_op jit(solution)/shard_map/ppermute | solution.py:71
  55.3 4.7 %collective-permute-done.14 = bf16[96,768]{1,0:T(8,128)(2,1)S(1)} collective-permute-done((bf16[96,768]{1,0:T(8,128)(2,1)S(1)}, bf16[96,768]{1,0:T(8,128)(2,1)S(1)}, u32[]{:S(2)}, u32[]{:S(2)}) %collective-permute-start.14) | collective-permute-done | bytes 147488 | tf_op jit(solution)/shard_map/ppermute | solution.py:71
  75.6 4.5 %shard_map.172 = (bf16[6,512,512]{2,1,0:T(8,128)(2,1)S(1)}, bf16[512,384]{1,0:T(8,128)(2,1)S(1)}, bf16[512,768]{1,0:T(8,128)(2,1)S(1)}) custom-call(s32[4]{0:T(128)S(1)} %bitcast.92, bf16[512,1152]{1,0:T(8,128)(2,1)S(1)} %copy-done.24, bf16[768,1536]{1,0:T(8,128)(2,1)S(1)} %copy-done.17), custom_call_target="tpu_custom_call" | custom-call | flops 8000000000 | bytes 10000000 | tf_op jit(solution)/shard_map/pallas_call | solution.py:38
  82.6 3.1 %collective-permute-done.19.first = bf16[4,96,768]{2,1,0:T(8,128)(2,1)} collective-permute-done((bf16[4,96,768]{2,1,0:T(8,128)(2,1)S(1)}, bf16[4,96,768]{2,1,0:T(8,128)(2,1)}, u32[]{:S(2)}, u32[]{:S(2)}) %collective-permute-start.19) | collective-permute-done | bytes 589856 | tf_op jit(solution)/shard_map/ppermute | solution.py:81
  90.4 3.1 %shard_map.174 = (bf16[512,768]{1,0:T(8,128)(2,1)S(1)}, f32[512,128]{1,0:T(8,128)S(1)}, bf16[512,768]{1,0:T(8,128)(2,1)S(1)}, bf16[512,1536]{1,0:T(8,128)(2,1)S(1)}, bf16[512,1536]{1,0:T(8,128)(2,1)S(1)}) custom-call(bf16[512,768]{1,0:T(8,128)(2,1)S(1)} %get-tuple-element.160.x, bf16[512,768]{1,0:T(8,128)(2,1)S(1)} %get-tuple-element.94.mine, ...), custom_call_target="tpu_custom_call" | custom-call | flops 8000000000 | bytes 10000000 | tf_op jit(solution)/shard_map/pallas_call | solution.py:38
  95.8 3.7 %shard_map.175 = (bf16[512,768]{1,0:T(8,128)(2,1)S(1)}, bf16[2,768,768]{2,1,0:T(8,128)(2,1)S(1)}) custom-call(s32[9]{0:T(128)S(1)} %stack.176.where, bf16[512,1536]{1,0:T(8,128)(2,1)S(1)} %get-tuple-element.100.activated.right, bf16[4,96,768]{2,1,0:T(8,128)(2,1)S(1)} %pad_maximum_fusion.3.own, bf16[4,96,768]{2,1,0:T(8,128)(2,1)} %collective-permute-done.19.first, ...), custom_call_target="tpu_custom_call" | custom-call | flops 8000000000 | bytes 10000000 | tf_op jit(solution)/shard_map/pallas_call | solution.py:38
  106.1 3.0 %shard_map.177 = (bf16[4,96,768]{2,1,0:T(8,128)(2,1)S(1)}, bf16[4,96,768]{2,1,0:T(8,128)(2,1)S(1)}, bf16[4,96,768]{2,1,0:T(8,128)(2,1)S(1)}, bf16[4,96,768]{2,1,0:T(8,128)(2,1)S(1)}) custom-call(s32[6]{0:T(128)S(1)} %stack.201.table, bf16[512,768]{1,0:T(8,128)(2,1)S(1)} %get-tuple-element.113.left.d_mixed.d_second, bf16[512,1536]{1,0:T(8,128)(2,1)S(1)} %copy-done.22), custom_call_target="tpu_custom_call" | custom-call | flops 8000000000 | bytes 10000000 | tf_op jit(solution)/shard_map/pallas_call | solution.py:38
  111.2 3.4 %shard_map.178 = (bf16[512,1536]{1,0:T(8,128)(2,1)S(1)}, bf16[512,768]{1,0:T(8,128)(2,1)S(1)}, f32[8,1536]{1,0:T(8,128)S(1)}) custom-call(bf16[512,768]{1,0:T(8,128)(2,1)S(1)} %get-tuple-element.113.left.d_mixed.d_second, bf16[2,768,768]{2,1,0:T(8,128)(2,1)S(1)} %copy-done.15, bf16[2,768,768]{2,1,0:T(8,128)(2,1)S(1)} %copy-done.13, ...), custom_call_target="tpu_custom_call" | custom-call | flops 8000000000 | bytes 10000000 | tf_op jit(solution)/shard_map/pallas_call | solution.py:38
  114.8 2.8 %shard_map.179 = (bf16[4,96,768]{2,1,0:T(8,128)(2,1)S(1)}, bf16[4,96,768]{2,1,0:T(8,128)(2,1)S(1)}, bf16[4,96,768]{2,1,0:T(8,128)(2,1)S(1)}, bf16[4,96,768]{2,1,0:T(8,128)(2,1)S(1)}) custom-call(s32[6]{0:T(128)S(1)} %stack.201.table, bf16[512,768]{1,0:T(8,128)(2,1)S(1)} %copy-done.30, bf16[512,1536]{1,0:T(8,128)(2,1)S(1)} %get-tuple-element.110.right), custom_call_target="tpu_custom_call" | custom-call | flops 8000000000 | bytes 10000000 | tf_op jit(solution)/shard_map/pallas_call | solution.py:38
  124.0 3.9 %shard_map.181 = (bf16[512,1152]{1,0:T(8,128)(2,1)S(1)}, f32[8,768]{1,0:T(8,128)S(1)}) custom-call(bf16[512,384]{1,0:T(8,128)(2,1)S(1)} %get-tuple-element.116.d_ctx, bf16[512,1152]{1,0:T(8,128)(2,1)S(1)} %copy-done.25, bf16[6,512,512]{2,1,0:T(8,128)(2,1)S(1)} %copy-done.11, bf16[512,384]{1,0:T(8,128)(2,1)S(1)} %copy-done.32), custom_call_target="tpu_custom_call" | custom-call | flops 8000000000 | bytes 10000000 | tf_op jit(solution)/shard_map/pallas_call | solution.py:38
  127.9 3.5 %shard_map.182 = (bf16[4,112,768]{2,1,0:T(8,128)(2,1)S(1)}, bf16[4,112,768]{2,1,0:T(8,128)(2,1)S(1)}, bf16[4,112,768]{2,1,0:T(8,128)(2,1)S(1)}, bf16[4,112,768]{2,1,0:T(8,128)(2,1)S(1)}) custom-call(s32[6]{0:T(128)S(1)} %stack.201.table, bf16[512,768]{1,0:T(8,128)(2,1)S(1)} %get-tuple-element.160.x, bf16[512,1152]{1,0:T(8,128)(2,1)S(1)} %get-tuple-element.135.d_qkv, ...), custom_call_target="tpu_custom_call" | custom-call | flops 8000000000 | bytes 10000000 | tf_op jit(solution)/shard_map/pallas_call | solution.py:38
  132.0 6.0 %collective-permute-done.28 = bf16[4,96,768]{2,1,0:T(8,128)(2,1)S(1)} collective-permute-done((bf16[4,96,768]{2,1,0:T(8,128)(2,1)S(1)}, bf16[4,96,768]{2,1,0:T(8,128)(2,1)S(1)}, u32[]{:S(2)}, u32[]{:S(2)}) %collective-permute-start.28) | collective-permute-done | bytes 589856 | tf_op jit(solution)/shard_map/ppermute | solution.py:81
  144.8 5.8 %collective-permute-done.25 = bf16[4,112,768]{2,1,0:T(8,128)(2,1)S(1)} collective-permute-done((bf16[4,112,768]{2,1,0:T(8,128)(2,1)S(1)}, bf16[4,112,768]{2,1,0:T(8,128)(2,1)S(1)}, u32[]{:S(2)}, u32[]{:S(2)}) %collective-permute-start.25) | collective-permute-done | bytes 688160 | tf_op jit(solution)/shard_map/ppermute | solution.py:81
  150.8 3.7 %collective-permute-done.34 = bf16[4,96,768]{2,1,0:T(8,128)(2,1)S(1)} collective-permute-done((bf16[4,96,768]{2,1,0:T(8,128)(2,1)S(1)}, bf16[4,96,768]{2,1,0:T(8,128)(2,1)S(1)}, u32[]{:S(2)}, u32[]{:S(2)}) %collective-permute-start.34) | collective-permute-done | bytes 589856 | tf_op jit(solution)/shard_map/ppermute | solution.py:81
  155.0 3.0 %collective-permute-done.33 = bf16[4,96,768]{2,1,0:T(8,128)(2,1)S(1)} collective-permute-done((bf16[4,96,768]{2,1,0:T(8,128)(2,1)S(1)}, bf16[4,96,768]{2,1,0:T(8,128)(2,1)S(1)}, u32[]{:S(2)}, u32[]{:S(2)}) %collective-permute-start.33) | collective-permute-done | bytes 589856 | tf_op jit(solution)/shard_map/ppermute | solution.py:81
  158.3 2.7 %collective-permute-start.37 = (bf16[96,768]{1,0:T(8,128)(2,1)S(1)}, bf16[96,768]{1,0:T(8,128)(2,1)S(1)}, u32[]{:S(2)}, u32[]{:S(2)}) collective-permute-start(bf16[96,768]{1,0:T(8,128)(2,1)S(1)} %get-tuple-element.166), channel_id=1, source_target_pairs={{0,24},{4,28},{8,16},{12,20},{16,8},{20,12},{24,0},{28,4},{1,25},{... | collective-permute-start | bytes 442376 | tf_op jit(solution)/shard_map/ppermute | solution.py:71
  163.3 3.3 %collective-permute-done.37 = bf16[96,768]{1,0:T(8,128)(2,1)S(1)} collective-permute-done((bf16[96,768]{1,0:T(8,128)(2,1)S(1)}, bf16[96,768]{1,0:T(8,128)(2,1)S(1)}, u32[]{:S(2)}, u32[]{:S(2)}) %collective-permute-start.37) | collective-permute-done | bytes 147488 | tf_op jit(solution)/shard_map/ppermute | solution.py:71
  166.6 4.9 %collective-permute-start.35 = (bf16[96,768]{1,0:T(8,128)(2,1)S(1)}, bf16[96,768]{1,0:T(8,128)(2,1)S(1)}, u32[]{:S(2)}, u32[]{:S(2)}) collective-permute-start(bf16[96,768]{1,0:T(8,128)(2,1)S(1)} %get-tuple-element.168), channel_id=1, source_target_pairs={{0,8},{4,12},{8,0},{12,4},{16,24},{20,28},{24,16},{28,20},{1,9},{5... | collective-permute-start | bytes 442376 | tf_op jit(solution)/shard_map/ppermute | solution.py:71
  185.0 7.0 %collective-permute-done.41 = bf16[128,768]{1,0:T(8,128)(2,1)S(1)} collective-permute-done((bf16[128,768]{1,0:T(8,128)(2,1)S(1)}, bf16[128,768]{1,0:T(8,128)(2,1)S(1)}, u32[]{:S(2)}, u32[]{:S(2)}) %collective-permute-start.41) | collective-permute-done | bytes 196640 | tf_op jit(solution)/shard_map/ppermute | solution.py:67
  (199 shorter events, 91.0 us)
Async XLA Ops:
  2.1 21.3 %collective-permute-start = (bf16[2,128,768]{2,1,0:T(8,128)(2,1)S(1)}, bf16[2,128,768]{2,1,0:T(8,128)(2,1)S(1)}, u32[]{:S(2)}, u32[]{:S(2)}) collective-permute-start(bf16[2,128,768]{2,1,0:T(8,128)(2,1)S(1)} %pad_maximum_fusion.5), channel_id=1, source_target_pairs={{0,2},{2,0},{1,3},{3,1},{4,6},{6,4},{5,7},{7,5},{8,10},{10,8},{9,1... | collective-permute-start | bytes 1179656 | tf_op jit(solution)/shard_map/ppermute | solution.py:67
  9.1 14.3 %collective-permute-start.3 = (bf16[112,768]{1,0:T(8,128)(2,1)S(1)}, bf16[112,768]{1,0:T(8,128)(2,1)S(1)}, u32[]{:S(2)}, u32[]{:S(2)}) collective-permute-start(bf16[112,768]{1,0:T(8,128)(2,1)S(1)} %shard_map.169), channel_id=1, source_target_pairs={{0,16},{4,20},{8,24},{12,28},{16,0},{20,4},{24,8},{28,12},{1,17},{... | collective-permute-start | bytes 516104 | tf_op jit(solution)/shard_map/ppermute | solution.py:71
  9.1 14.3 %collective-permute-start.2 = (bf16[112,768]{1,0:T(8,128)(2,1)S(1)}, bf16[112,768]{1,0:T(8,128)(2,1)S(1)}, u32[]{:S(2)}, u32[]{:S(2)}) collective-permute-start(bf16[112,768]{1,0:T(8,128)(2,1)S(1)} %shard_map.169), channel_id=1, source_target_pairs={{0,8},{4,12},{8,0},{12,4},{16,24},{20,28},{24,16},{28,20},{1,9},{5... | collective-permute-start | bytes 516104 | tf_op jit(solution)/shard_map/ppermute | solution.py:71
  23.5 19.9 %collective-permute-start.6 = (bf16[4,112,768]{2,1,0:T(8,128)(2,1)S(1)}, bf16[4,112,768]{2,1,0:T(8,128)(2,1)S(1)}, u32[]{:S(2)}, u32[]{:S(2)}) collective-permute-start(bf16[4,112,768]{2,1,0:T(8,128)(2,1)S(1)} %pad_maximum_fusion.1.own), channel_id=1, source_target_pairs={{0,4},{1,3},{2,6},{3,1},{4,0},{5,7},{6,2},{7,5},{8,12},{9,11},{10,... | collective-permute-start | bytes 2064392 | tf_op jit(solution)/shard_map/ppermute | solution.py:81
  25.0 19.2 %collective-permute-start.5 = (bf16[4,112,768]{2,1,0:T(8,128)(2,1)S(1)}, bf16[4,112,768]{2,1,0:T(8,128)(2,1)}, u32[]{:S(2)}, u32[]{:S(2)}) collective-permute-start(bf16[4,112,768]{2,1,0:T(8,128)(2,1)S(1)} %pad_maximum_fusion.1.own), channel_id=1, source_target_pairs={{0,2},{1,5},{2,0},{3,7},{4,6},{5,1},{6,4},{7,3},{8,10},{9,13},{10,... | collective-permute-start | bytes 2064392 | tf_op jit(solution)/shard_map/ppermute | solution.py:81
  26.5 23.0 %collective-permute-start.1 = (bf16[2,256,768]{2,1,0:T(8,128)(2,1)}, bf16[2,256,768]{2,1,0:T(8,128)(2,1)}, u32[]{:S(2)}, u32[]{:S(2)}) collective-permute-start(bf16[2,256,768]{2,1,0:T(8,128)(2,1)} %pad_maximum_fusion), channel_id=1, source_target_pairs={{0,1},{1,0},{2,3},{3,2},{4,5},{5,4},{6,7},{7,6},{8,9},{9,8},{10,11... | collective-permute-start | bytes 2359304 | tf_op jit(solution)/shard_map/ppermute | solution.py:64
  44.2 15.8 %collective-permute-start.10 = (bf16[4,112,768]{2,1,0:T(8,128)(2,1)}, bf16[4,112,768]{2,1,0:T(8,128)(2,1)}, u32[]{:S(2)}, u32[]{:S(2)}) collective-permute-start(bf16[4,112,768]{2,1,0:T(8,128)(2,1)} %collective-permute-done.5.first), channel_id=1, source_target_pairs={{0,4},{1,3},{2,6},{3,1},{4,0},{5,7},{6,2},{7,5},{8,12},{9,11},{10,... | collective-permute-start | bytes 2064392 | tf_op jit(solution)/shard_map/ppermute | solution.py:81
  49.5 18.5 %collective-permute-start.12 = (bf16[4,96,768]{2,1,0:T(8,128)(2,1)S(1)}, bf16[4,96,768]{2,1,0:T(8,128)(2,1)S(1)}, u32[]{:S(2)}, u32[]{:S(2)}) collective-permute-start(bf16[4,96,768]{2,1,0:T(8,128)(2,1)S(1)} %pad_maximum_fusion.2.own), channel_id=1, source_target_pairs={{0,4},{1,3},{2,6},{3,1},{4,0},{5,7},{6,2},{7,5},{8,12},{9,11},{10,... | collective-permute-start | bytes 1769480 | tf_op jit(solution)/shard_map/ppermute | solution.py:81
  53.8 15.1 %collective-permute-start.11 = (bf16[4,96,768]{2,1,0:T(8,128)(2,1)S(1)}, bf16[4,96,768]{2,1,0:T(8,128)(2,1)}, u32[]{:S(2)}, u32[]{:S(2)}) collective-permute-start(bf16[4,96,768]{2,1,0:T(8,128)(2,1)S(1)} %pad_maximum_fusion.2.own), channel_id=1, source_target_pairs={{0,2},{1,5},{2,0},{3,7},{4,6},{5,1},{6,4},{7,3},{8,10},{9,13},{10,... | collective-permute-start | bytes 1769480 | tf_op jit(solution)/shard_map/ppermute | solution.py:81
  68.8 13.8 %collective-permute-start.20 = (bf16[4,96,768]{2,1,0:T(8,128)(2,1)S(1)}, bf16[4,96,768]{2,1,0:T(8,128)(2,1)}, u32[]{:S(2)}, u32[]{:S(2)}) collective-permute-start(bf16[4,96,768]{2,1,0:T(8,128)(2,1)S(1)} %pad_maximum_fusion.3.own), channel_id=1, source_target_pairs={{0,4},{1,3},{2,6},{3,1},{4,0},{5,7},{6,2},{7,5},{8,12},{9,11},{10,... | collective-permute-start | bytes 1769480 | tf_op jit(solution)/shard_map/ppermute | solution.py:81
  69.4 16.4 %collective-permute-start.19 = (bf16[4,96,768]{2,1,0:T(8,128)(2,1)S(1)}, bf16[4,96,768]{2,1,0:T(8,128)(2,1)}, u32[]{:S(2)}, u32[]{:S(2)}) collective-permute-start(bf16[4,96,768]{2,1,0:T(8,128)(2,1)S(1)} %pad_maximum_fusion.3.own), channel_id=1, source_target_pairs={{0,2},{1,5},{2,0},{3,7},{4,6},{5,1},{6,4},{7,3},{8,10},{9,13},{10,... | collective-permute-start | bytes 1769480 | tf_op jit(solution)/shard_map/ppermute | solution.py:81
  70.9 18.0 %collective-permute-start.18 = (bf16[4,96,768]{2,1,0:T(8,128)(2,1)}, bf16[4,96,768]{2,1,0:T(8,128)(2,1)}, u32[]{:S(2)}, u32[]{:S(2)}) collective-permute-start(bf16[4,96,768]{2,1,0:T(8,128)(2,1)} %collective-permute-done.11.first), channel_id=1, source_target_pairs={{0,4},{1,3},{2,6},{3,1},{4,0},{5,7},{6,2},{7,5},{8,12},{9,11},{10,... | collective-permute-start | bytes 1769480 | tf_op jit(solution)/shard_map/ppermute | solution.py:81
  110.7 28.4 %collective-permute-start.26 = (bf16[4,96,768]{2,1,0:T(8,128)(2,1)S(1)}, bf16[4,96,768]{2,1,0:T(8,128)(2,1)S(1)}, u32[]{:S(2)}, u32[]{:S(2)}) collective-permute-start(bf16[4,96,768]{2,1,0:T(8,128)(2,1)S(1)} %get-tuple-element.130), channel_id=1, source_target_pairs={{0,2},{1,5},{2,0},{3,7},{4,6},{5,1},{6,4},{7,3},{8,10},{9,13},{10,... | collective-permute-start | bytes 1769480 | tf_op jit(solution)/shard_map/ppermute | solution.py:81
  119.2 19.9 %collective-permute-start.27 = (bf16[4,96,768]{2,1,0:T(8,128)(2,1)S(1)}, bf16[4,96,768]{2,1,0:T(8,128)(2,1)S(1)}, u32[]{:S(2)}, u32[]{:S(2)}) collective-permute-start(bf16[4,96,768]{2,1,0:T(8,128)(2,1)S(1)} %add_convert_fusion.2), channel_id=1, source_target_pairs={{0,4},{1,3},{2,6},{3,1},{4,0},{5,7},{6,2},{7,5},{8,12},{9,11},{10,... | collective-permute-start | bytes 1769480 | tf_op jit(solution)/shard_map/ppermute | solution.py:81
  120.1 17.9 %collective-permute-start.28 = (bf16[4,96,768]{2,1,0:T(8,128)(2,1)S(1)}, bf16[4,96,768]{2,1,0:T(8,128)(2,1)S(1)}, u32[]{:S(2)}, u32[]{:S(2)}) collective-permute-start(bf16[4,96,768]{2,1,0:T(8,128)(2,1)S(1)} %get-tuple-element.132), channel_id=1, source_target_pairs={{0,2},{1,5},{2,0},{3,7},{4,6},{5,1},{6,4},{7,3},{8,10},{9,13},{10,... | collective-permute-start | bytes 1769480 | tf_op jit(solution)/shard_map/ppermute | solution.py:81
  131.4 19.2 %collective-permute-start.25 = (bf16[4,112,768]{2,1,0:T(8,128)(2,1)S(1)}, bf16[4,112,768]{2,1,0:T(8,128)(2,1)S(1)}, u32[]{:S(2)}, u32[]{:S(2)}) collective-permute-start(bf16[4,112,768]{2,1,0:T(8,128)(2,1)S(1)} %get-tuple-element.127), channel_id=1, source_target_pairs={{0,2},{1,5},{2,0},{3,7},{4,6},{5,1},{6,4},{7,3},{8,10},{9,13},{10,... | collective-permute-start | bytes 2064392 | tf_op jit(solution)/shard_map/ppermute | solution.py:81
  138.2 16.3 %collective-permute-start.34 = (bf16[4,96,768]{2,1,0:T(8,128)(2,1)S(1)}, bf16[4,96,768]{2,1,0:T(8,128)(2,1)S(1)}, u32[]{:S(2)}, u32[]{:S(2)}) collective-permute-start(bf16[4,96,768]{2,1,0:T(8,128)(2,1)S(1)} %add_convert_fusion.1), channel_id=1, source_target_pairs={{0,4},{1,3},{2,6},{3,1},{4,0},{5,7},{6,2},{7,5},{8,12},{9,11},{10,... | collective-permute-start | bytes 1769480 | tf_op jit(solution)/shard_map/ppermute | solution.py:81
  139.3 18.7 %collective-permute-start.33 = (bf16[4,96,768]{2,1,0:T(8,128)(2,1)S(1)}, bf16[4,96,768]{2,1,0:T(8,128)(2,1)S(1)}, u32[]{:S(2)}, u32[]{:S(2)}) collective-permute-start(bf16[4,96,768]{2,1,0:T(8,128)(2,1)S(1)} %get-tuple-element.140), channel_id=1, source_target_pairs={{0,2},{1,5},{2,0},{3,7},{4,6},{5,1},{6,4},{7,3},{8,10},{9,13},{10,... | collective-permute-start | bytes 1769480 | tf_op jit(solution)/shard_map/ppermute | solution.py:81
  142.4 18.7 %collective-permute-start.32 = (bf16[96,768]{1,0:T(8,128)(2,1)S(1)}, bf16[96,768]{1,0:T(8,128)(2,1)S(1)}, u32[]{:S(2)}, u32[]{:S(2)}) collective-permute-start(bf16[96,768]{1,0:T(8,128)(2,1)S(1)} %get-tuple-element.169), channel_id=1, source_target_pairs={{0,24},{4,28},{8,16},{12,20},{16,8},{20,12},{24,0},{28,4},{1,25},{... | collective-permute-start | bytes 442376 | tf_op jit(solution)/shard_map/ppermute | solution.py:71
  144.8 16.9 %collective-permute-start.31 = (bf16[96,768]{1,0:T(8,128)(2,1)S(1)}, bf16[96,768]{1,0:T(8,128)(2,1)S(1)}, u32[]{:S(2)}, u32[]{:S(2)}) collective-permute-start(bf16[96,768]{1,0:T(8,128)(2,1)S(1)} %get-tuple-element.170), channel_id=1, source_target_pairs={{0,16},{4,20},{8,24},{12,28},{16,0},{20,4},{24,8},{28,12},{1,17},{... | collective-permute-start | bytes 442376 | tf_op jit(solution)/shard_map/ppermute | solution.py:71
  150.6 24.9 %collective-permute-start.40 = (bf16[512,768]{1,0:T(8,128)(2,1)S(1)}, bf16[512,768]{1,0:T(8,128)(2,1)S(1)}, u32[]{:S(2)}, u32[]{:S(2)}) collective-permute-start(bf16[512,768]{1,0:T(8,128)(2,1)S(1)} %shard_map.183), channel_id=1, source_target_pairs={{0,1},{1,0},{2,3},{3,2},{4,5},{5,4},{6,7},{7,6},{8,9},{9,8},{10,11... | collective-permute-start | bytes 2359304 | tf_op jit(solution)/shard_map/ppermute | solution.py:64
  161.1 17.1 %collective-permute-start.38 = (bf16[4,112,768]{2,1,0:T(8,128)(2,1)S(1)}, bf16[4,112,768]{2,1,0:T(8,128)(2,1)S(1)}, u32[]{:S(2)}, u32[]{:S(2)}) collective-permute-start(bf16[4,112,768]{2,1,0:T(8,128)(2,1)S(1)} %add_convert_fusion), channel_id=1, source_target_pairs={{0,4},{1,3},{2,6},{3,1},{4,0},{5,7},{6,2},{7,5},{8,12},{9,11},{10,... | collective-permute-start | bytes 2064392 | tf_op jit(solution)/shard_map/ppermute | solution.py:81
  161.8 15.7 %collective-permute-start.29 = (bf16[4,112,768]{2,1,0:T(8,128)(2,1)S(1)}, bf16[4,112,768]{2,1,0:T(8,128)(2,1)S(1)}, u32[]{:S(2)}, u32[]{:S(2)}) collective-permute-start(bf16[4,112,768]{2,1,0:T(8,128)(2,1)S(1)} %get-tuple-element.137), channel_id=1, source_target_pairs={{0,2},{1,5},{2,0},{3,7},{4,6},{5,1},{6,4},{7,3},{8,10},{9,13},{10,... | collective-permute-start | bytes 2064392 | tf_op jit(solution)/shard_map/ppermute | solution.py:81
  178.5 15.2 %collective-permute-start.44 = (bf16[112,768]{1,0:T(8,128)(2,1)S(1)}, bf16[112,768]{1,0:T(8,128)(2,1)S(1)}, u32[]{:S(2)}, u32[]{:S(2)}) collective-permute-start(bf16[112,768]{1,0:T(8,128)(2,1)S(1)} %get-tuple-element.163), channel_id=1, source_target_pairs={{0,24},{4,28},{8,16},{12,20},{16,8},{20,12},{24,0},{28,4},{1,25},{... | collective-permute-start | bytes 516104 | tf_op jit(solution)/shard_map/ppermute | solution.py:71
  (60 other events, 395.9 us)

commit v6 on v5

--- a/solution.py
+++ b/solution.py
@@ -448,10 +448,9 @@
     totals[index : index + 1, :] = totals[index : index + 1, :] + jnp.sum(value, axis=0, keepdims=True)
 
 
-def second_kernel(unit, mine, other, grad, norms, result, d_mixed, totals):
+def second_kernel(low, mine, other, grad, norms, result, d_mixed, totals):
     start_sums(totals)
-    normed = unit[...].astype(F32) * norms[0:1] + norms[3:4]
-    one, rate = norm_parts(normed + mine[...].astype(F32) + other[...].astype(F32) + norms[4:5])
+    one, rate = norm_parts(low[...].astype(F32) + mine[...].astype(F32) + other[...].astype(F32) + norms[4:5])
     result[...] = (one * norms[1:2] + norms[5:6]).astype(BF)
     dy = grad[...].astype(F32)
     back = norm_back(dy, one, rate, norms[1:2])
@@ -685,7 +684,7 @@
     result, d_mixed, totals_two = call(
         second_kernel,
         [((rows, width), BF, True), ((rows, width), BF, True), ((8, width), F32)],
-        [(unit, True), (part, True), (place.core_swap(part), True), (grad_rows, True), norms],
+        [(first_low, True), (part, True), (place.core_swap(part), True), (grad_rows, True), norms],
         steps=2,
     )
 

time: 195 us -> 195 us (level)
  no operation moved by 1% of the time
where the time goes in v6:
time: 195 us
  waiting for transfers between devices  75.7 us (39%)
  starting transfers between devices  56 us (29%)
  Pallas kernels  38.2 us (20%)
  local copies, waits for them, and re-layouts  15.6 us (8%)
  other arithmetic  7.96 us (4%)
    pallas_call x16, Pallas kernels, call(): pl.pallas_call(kernel, out_shape=[jax.ShapeDtypeStruct(shape, kind) for s...  38.2 us
    ppermute x18, waiting for transfers between devices, line_swap(): return lax.ppermute(value, 'dp', pairs)  35.2 us
    ppermute x18, waiting for transfers between devices, cross(): return lax.ppermute(value, ('dp', 'mp'), pairs)  31.3 us
    ppermute x18, starting transfers between devices, line_swap(): return lax.ppermute(value, 'dp', pairs)  30.4 us
    ppermute x18, starting transfers between devices, cross(): return lax.ppermute(value, ('dp', 'mp'), pairs)  20.4 us
    unnamed x79, local copies, waits for them, and re-layouts  13.6 us
    ppermute x3, waiting for transfers between devices, row_swap(): return lax.ppermute(value, 'mp', [(0, 2), (2, 0), (1, 3), (3, 1)])  6.97 us
    ppermute x3, starting transfers between devices, row_swap(): return lax.ppermute(value, 'mp', [(0, 2), (2, 0), (1, 3), (3, 1)])  5.06 us
  transfers between devices with their start and end apart: 45, of which 25 were waited for; matrix products, arithmetic and copies ran while one was open for 4% of the time, Pallas kernels for 15%

profile of v6, /device:TPU:0, one launch (start us, length us, event | category | flops | bytes accessed | tf_op | source)
XLA Modules:
  0.0 194.8 jit_solution(14452476822573209581)
XLA Ops:
  2.1 3.0 %collective-permute-start = (bf16[2,128,768]{2,1,0:T(8,128)(2,1)S(1)}, bf16[2,128,768]{2,1,0:T(8,128)(2,1)S(1)}, u32[]{:S(2)}, u32[]{:S(2)}) collective-permute-start(bf16[2,128,768]{2,1,0:T(8,128)(2,1)S(1)} %pad_maximum_fusion.5), channel_id=1, source_target_pairs={{0,2},{2,0},{1,3},{3,1},{4,6},{6,4},{5,7},{7,5},{8,10},{10,8},{9,1... | collective-permute-start | bytes 1179656 | tf_op jit(solution)/shard_map/ppermute | solution.py:67
  5.4 3.7 %collective-permute-start.4 = (bf16[112,768]{1,0:T(8,128)(2,1)S(1)}, bf16[112,768]{1,0:T(8,128)(2,1)S(1)}, u32[]{:S(2)}, u32[]{:S(2)}) collective-permute-start(bf16[112,768]{1,0:T(8,128)(2,1)S(1)} %shard_map.169), channel_id=1, source_target_pairs={{0,24},{4,28},{8,16},{12,20},{16,8},{20,12},{24,0},{28,4},{1,25},{... | collective-permute-start | bytes 516104 | tf_op jit(solution)/shard_map/ppermute | solution.py:71
  9.8 4.8 %collective-permute-done.4 = bf16[112,768]{1,0:T(8,128)(2,1)S(1)} collective-permute-done((bf16[112,768]{1,0:T(8,128)(2,1)S(1)}, bf16[112,768]{1,0:T(8,128)(2,1)S(1)}, u32[]{:S(2)}, u32[]{:S(2)}) %collective-permute-start.4) | collective-permute-done | bytes 172064 | tf_op jit(solution)/shard_map/ppermute | solution.py:71
  14.6 8.8 %collective-permute-done.3 = bf16[112,768]{1,0:T(8,128)(2,1)S(1)} collective-permute-done((bf16[112,768]{1,0:T(8,128)(2,1)S(1)}, bf16[112,768]{1,0:T(8,128)(2,1)S(1)}, u32[]{:S(2)}, u32[]{:S(2)}) %collective-permute-start.3) | collective-permute-done | bytes 172064 | tf_op jit(solution)/shard_map/ppermute | solution.py:71
  29.0 6.1 %collective-permute-done.9 = bf16[96,768]{1,0:T(8,128)(2,1)S(1)} collective-permute-done((bf16[96,768]{1,0:T(8,128)(2,1)S(1)}, bf16[96,768]{1,0:T(8,128)(2,1)S(1)}, u32[]{:S(2)}, u32[]{:S(2)}) %collective-permute-start.9) | collective-permute-done | bytes 147488 | tf_op jit(solution)/shard_map/ppermute | solution.py:71
  35.1 4.0 %collective-permute-start.7 = (bf16[96,768]{1,0:T(8,128)(2,1)S(1)}, bf16[96,768]{1,0:T(8,128)(2,1)S(1)}, u32[]{:S(2)}, u32[]{:S(2)}) collective-permute-start(bf16[96,768]{1,0:T(8,128)(2,1)S(1)} %copy-done.35), channel_id=1, source_target_pairs={{0,8},{4,12},{8,0},{12,4},{16,24},{20,28},{24,16},{28,20},{1,9},{5... | collective-permute-start | bytes 442376 | tf_op jit(solution)/shard_map/ppermute | solution.py:71
  55.3 4.7 %collective-permute-done.14 = bf16[96,768]{1,0:T(8,128)(2,1)S(1)} collective-permute-done((bf16[96,768]{1,0:T(8,128)(2,1)S(1)}, bf16[96,768]{1,0:T(8,128)(2,1)S(1)}, u32[]{:S(2)}, u32[]{:S(2)}) %collective-permute-start.14) | collective-permute-done | bytes 147488 | tf_op jit(solution)/shard_map/ppermute | solution.py:71
  75.6 4.5 %shard_map.172 = (bf16[6,512,512]{2,1,0:T(8,128)(2,1)S(1)}, bf16[512,384]{1,0:T(8,128)(2,1)S(1)}, bf16[512,768]{1,0:T(8,128)(2,1)S(1)}) custom-call(s32[4]{0:T(128)S(1)} %bitcast.92, bf16[512,1152]{1,0:T(8,128)(2,1)S(1)} %copy-done.24, bf16[768,1536]{1,0:T(8,128)(2,1)S(1)} %copy-done.17), custom_call_target="tpu_custom_call" | custom-call | flops 8000000000 | bytes 10000000 | tf_op jit(solution)/shard_map/pallas_call | solution.py:38
  82.6 3.1 %collective-permute-done.19.first = bf16[4,96,768]{2,1,0:T(8,128)(2,1)} collective-permute-done((bf16[4,96,768]{2,1,0:T(8,128)(2,1)S(1)}, bf16[4,96,768]{2,1,0:T(8,128)(2,1)}, u32[]{:S(2)}, u32[]{:S(2)}) %collective-permute-start.19) | collective-permute-done | bytes 589856 | tf_op jit(solution)/shard_map/ppermute | solution.py:81
  90.4 3.1 %shard_map.174 = (bf16[512,768]{1,0:T(8,128)(2,1)S(1)}, f32[512,128]{1,0:T(8,128)S(1)}, bf16[512,768]{1,0:T(8,128)(2,1)S(1)}, bf16[512,1536]{1,0:T(8,128)(2,1)S(1)}, bf16[512,1536]{1,0:T(8,128)(2,1)S(1)}) custom-call(bf16[512,768]{1,0:T(8,128)(2,1)S(1)} %get-tuple-element.160.x, bf16[512,768]{1,0:T(8,128)(2,1)S(1)} %get-tuple-element.94.mine, ...), custom_call_target="tpu_custom_call" | custom-call | flops 8000000000 | bytes 10000000 | tf_op jit(solution)/shard_map/pallas_call | solution.py:38
  95.8 3.7 %shard_map.175 = (bf16[512,768]{1,0:T(8,128)(2,1)S(1)}, bf16[2,768,768]{2,1,0:T(8,128)(2,1)S(1)}) custom-call(s32[9]{0:T(128)S(1)} %stack.176.where, bf16[512,1536]{1,0:T(8,128)(2,1)S(1)} %get-tuple-element.100.activated.right, bf16[4,96,768]{2,1,0:T(8,128)(2,1)S(1)} %pad_maximum_fusion.3.own, bf16[4,96,768]{2,1,0:T(8,128)(2,1)} %collective-permute-done.19.first, ...), custom_call_target="tpu_custom_call" | custom-call | flops 8000000000 | bytes 10000000 | tf_op jit(solution)/shard_map/pallas_call | solution.py:38
  106.1 3.0 %shard_map.177 = (bf16[4,96,768]{2,1,0:T(8,128)(2,1)S(1)}, bf16[4,96,768]{2,1,0:T(8,128)(2,1)S(1)}, bf16[4,96,768]{2,1,0:T(8,128)(2,1)S(1)}, bf16[4,96,768]{2,1,0:T(8,128)(2,1)S(1)}) custom-call(s32[6]{0:T(128)S(1)} %stack.201.table, bf16[512,768]{1,0:T(8,128)(2,1)S(1)} %get-tuple-element.112.left.d_mixed.d_second, bf16[512,1536]{1,0:T(8,128)(2,1)S(1)} %copy-done.22), custom_call_target="tpu_custom_call" | custom-call | flops 8000000000 | bytes 10000000 | tf_op jit(solution)/shard_map/pallas_call | solution.py:38
  111.2 3.4 %shard_map.178 = (bf16[512,1536]{1,0:T(8,128)(2,1)S(1)}, bf16[512,768]{1,0:T(8,128)(2,1)S(1)}, f32[8,1536]{1,0:T(8,128)S(1)}) custom-call(bf16[512,768]{1,0:T(8,128)(2,1)S(1)} %get-tuple-element.112.left.d_mixed.d_second, bf16[2,768,768]{2,1,0:T(8,128)(2,1)S(1)} %copy-done.15, bf16[2,768,768]{2,1,0:T(8,128)(2,1)S(1)} %copy-done.13, ...), custom_call_target="tpu_custom_call" | custom-call | flops 8000000000 | bytes 10000000 | tf_op jit(solution)/shard_map/pallas_call | solution.py:38
  114.7 2.8 %shard_map.179 = (bf16[4,96,768]{2,1,0:T(8,128)(2,1)S(1)}, bf16[4,96,768]{2,1,0:T(8,128)(2,1)S(1)}, bf16[4,96,768]{2,1,0:T(8,128)(2,1)S(1)}, bf16[4,96,768]{2,1,0:T(8,128)(2,1)S(1)}) custom-call(s32[6]{0:T(128)S(1)} %stack.201.table, bf16[512,768]{1,0:T(8,128)(2,1)S(1)} %copy-done.30, bf16[512,1536]{1,0:T(8,128)(2,1)S(1)} %get-tuple-element.109.right), custom_call_target="tpu_custom_call" | custom-call | flops 8000000000 | bytes 10000000 | tf_op jit(solution)/shard_map/pallas_call | solution.py:38
  123.9 3.9 %shard_map.181 = (bf16[512,1152]{1,0:T(8,128)(2,1)S(1)}, f32[8,768]{1,0:T(8,128)S(1)}) custom-call(bf16[512,384]{1,0:T(8,128)(2,1)S(1)} %get-tuple-element.116.d_ctx, bf16[512,1152]{1,0:T(8,128)(2,1)S(1)} %copy-done.25, bf16[6,512,512]{2,1,0:T(8,128)(2,1)S(1)} %copy-done.11, bf16[512,384]{1,0:T(8,128)(2,1)S(1)} %copy-done.32), custom_call_target="tpu_custom_call" | custom-call | flops 8000000000 | bytes 10000000 | tf_op jit(solution)/shard_map/pallas_call | solution.py:38
  127.8 3.5 %shard_map.182 = (bf16[4,112,768]{2,1,0:T(8,128)(2,1)S(1)}, bf16[4,112,768]{2,1,0:T(8,128)(2,1)S(1)}, bf16[4,112,768]{2,1,0:T(8,128)(2,1)S(1)}, bf16[4,112,768]{2,1,0:T(8,128)(2,1)S(1)}) custom-call(s32[6]{0:T(128)S(1)} %stack.201.table, bf16[512,768]{1,0:T(8,128)(2,1)S(1)} %get-tuple-element.160.x, bf16[512,1152]{1,0:T(8,128)(2,1)S(1)} %get-tuple-element.135.d_qkv, ...), custom_call_target="tpu_custom_call" | custom-call | flops 8000000000 | bytes 10000000 | tf_op jit(solution)/shard_map/pallas_call | solution.py:38
  131.9 6.1 %collective-permute-done.28 = bf16[4,96,768]{2,1,0:T(8,128)(2,1)S(1)} collective-permute-done((bf16[4,96,768]{2,1,0:T(8,128)(2,1)S(1)}, bf16[4,96,768]{2,1,0:T(8,128)(2,1)S(1)}, u32[]{:S(2)}, u32[]{:S(2)}) %collective-permute-start.28) | collective-permute-done | bytes 589856 | tf_op jit(solution)/shard_map/ppermute | solution.py:81
  144.7 5.8 %collective-permute-done.25 = bf16[4,112,768]{2,1,0:T(8,128)(2,1)S(1)} collective-permute-done((bf16[4,112,768]{2,1,0:T(8,128)(2,1)S(1)}, bf16[4,112,768]{2,1,0:T(8,128)(2,1)S(1)}, u32[]{:S(2)}, u32[]{:S(2)}) %collective-permute-start.25) | collective-permute-done | bytes 688160 | tf_op jit(solution)/shard_map/ppermute | solution.py:81
  150.7 3.7 %collective-permute-done.34 = bf16[4,96,768]{2,1,0:T(8,128)(2,1)S(1)} collective-permute-done((bf16[4,96,768]{2,1,0:T(8,128)(2,1)S(1)}, bf16[4,96,768]{2,1,0:T(8,128)(2,1)S(1)}, u32[]{:S(2)}, u32[]{:S(2)}) %collective-permute-start.34) | collective-permute-done | bytes 589856 | tf_op jit(solution)/shard_map/ppermute | solution.py:81
  154.9 3.0 %collective-permute-done.33 = bf16[4,96,768]{2,1,0:T(8,128)(2,1)S(1)} collective-permute-done((bf16[4,96,768]{2,1,0:T(8,128)(2,1)S(1)}, bf16[4,96,768]{2,1,0:T(8,128)(2,1)S(1)}, u32[]{:S(2)}, u32[]{:S(2)}) %collective-permute-start.33) | collective-permute-done | bytes 589856 | tf_op jit(solution)/shard_map/ppermute | solution.py:81
  158.2 2.7 %collective-permute-start.37 = (bf16[96,768]{1,0:T(8,128)(2,1)S(1)}, bf16[96,768]{1,0:T(8,128)(2,1)S(1)}, u32[]{:S(2)}, u32[]{:S(2)}) collective-permute-start(bf16[96,768]{1,0:T(8,128)(2,1)S(1)} %get-tuple-element.166), channel_id=1, source_target_pairs={{0,24},{4,28},{8,16},{12,20},{16,8},{20,12},{24,0},{28,4},{1,25},{... | collective-permute-start | bytes 442376 | tf_op jit(solution)/shard_map/ppermute | solution.py:71
  163.2 3.4 %collective-permute-done.37 = bf16[96,768]{1,0:T(8,128)(2,1)S(1)} collective-permute-done((bf16[96,768]{1,0:T(8,128)(2,1)S(1)}, bf16[96,768]{1,0:T(8,128)(2,1)S(1)}, u32[]{:S(2)}, u32[]{:S(2)}) %collective-permute-start.37) | collective-permute-done | bytes 147488 | tf_op jit(solution)/shard_map/ppermute | solution.py:71
  166.6 4.9 %collective-permute-start.35 = (bf16[96,768]{1,0:T(8,128)(2,1)S(1)}, bf16[96,768]{1,0:T(8,128)(2,1)S(1)}, u32[]{:S(2)}, u32[]{:S(2)}) collective-permute-start(bf16[96,768]{1,0:T(8,128)(2,1)S(1)} %get-tuple-element.168), channel_id=1, source_target_pairs={{0,8},{4,12},{8,0},{12,4},{16,24},{20,28},{24,16},{28,20},{1,9},{5... | collective-permute-start | bytes 442376 | tf_op jit(solution)/shard_map/ppermute | solution.py:71
  184.9 7.0 %collective-permute-done.41 = bf16[128,768]{1,0:T(8,128)(2,1)S(1)} collective-permute-done((bf16[128,768]{1,0:T(8,128)(2,1)S(1)}, bf16[128,768]{1,0:T(8,128)(2,1)S(1)}, u32[]{:S(2)}, u32[]{:S(2)}) %collective-permute-start.41) | collective-permute-done | bytes 196640 | tf_op jit(solution)/shard_map/ppermute | solution.py:67
  (199 shorter events, 90.8 us)
Async XLA Ops:
  2.1 21.3 %collective-permute-start = (bf16[2,128,768]{2,1,0:T(8,128)(2,1)S(1)}, bf16[2,128,768]{2,1,0:T(8,128)(2,1)S(1)}, u32[]{:S(2)}, u32[]{:S(2)}) collective-permute-start(bf16[2,128,768]{2,1,0:T(8,128)(2,1)S(1)} %pad_maximum_fusion.5), channel_id=1, source_target_pairs={{0,2},{2,0},{1,3},{3,1},{4,6},{6,4},{5,7},{7,5},{8,10},{10,8},{9,1... | collective-permute-start | bytes 1179656 | tf_op jit(solution)/shard_map/ppermute | solution.py:67
  9.1 14.3 %collective-permute-start.3 = (bf16[112,768]{1,0:T(8,128)(2,1)S(1)}, bf16[112,768]{1,0:T(8,128)(2,1)S(1)}, u32[]{:S(2)}, u32[]{:S(2)}) collective-permute-start(bf16[112,768]{1,0:T(8,128)(2,1)S(1)} %shard_map.169), channel_id=1, source_target_pairs={{0,16},{4,20},{8,24},{12,28},{16,0},{20,4},{24,8},{28,12},{1,17},{... | collective-permute-start | bytes 516104 | tf_op jit(solution)/shard_map/ppermute | solution.py:71
  9.1 14.3 %collective-permute-start.2 = (bf16[112,768]{1,0:T(8,128)(2,1)S(1)}, bf16[112,768]{1,0:T(8,128)(2,1)S(1)}, u32[]{:S(2)}, u32[]{:S(2)}) collective-permute-start(bf16[112,768]{1,0:T(8,128)(2,1)S(1)} %shard_map.169), channel_id=1, source_target_pairs={{0,8},{4,12},{8,0},{12,4},{16,24},{20,28},{24,16},{28,20},{1,9},{5... | collective-permute-start | bytes 516104 | tf_op jit(solution)/shard_map/ppermute | solution.py:71
  23.5 19.9 %collective-permute-start.6 = (bf16[4,112,768]{2,1,0:T(8,128)(2,1)S(1)}, bf16[4,112,768]{2,1,0:T(8,128)(2,1)S(1)}, u32[]{:S(2)}, u32[]{:S(2)}) collective-permute-start(bf16[4,112,768]{2,1,0:T(8,128)(2,1)S(1)} %pad_maximum_fusion.1.own), channel_id=1, source_target_pairs={{0,4},{1,3},{2,6},{3,1},{4,0},{5,7},{6,2},{7,5},{8,12},{9,11},{10,... | collective-permute-start | bytes 2064392 | tf_op jit(solution)/shard_map/ppermute | solution.py:81
  25.0 19.2 %collective-permute-start.5 = (bf16[4,112,768]{2,1,0:T(8,128)(2,1)S(1)}, bf16[4,112,768]{2,1,0:T(8,128)(2,1)}, u32[]{:S(2)}, u32[]{:S(2)}) collective-permute-start(bf16[4,112,768]{2,1,0:T(8,128)(2,1)S(1)} %pad_maximum_fusion.1.own), channel_id=1, source_target_pairs={{0,2},{1,5},{2,0},{3,7},{4,6},{5,1},{6,4},{7,3},{8,10},{9,13},{10,... | collective-permute-start | bytes 2064392 | tf_op jit(solution)/shard_map/ppermute | solution.py:81
  26.5 23.0 %collective-permute-start.1 = (bf16[2,256,768]{2,1,0:T(8,128)(2,1)}, bf16[2,256,768]{2,1,0:T(8,128)(2,1)}, u32[]{:S(2)}, u32[]{:S(2)}) collective-permute-start(bf16[2,256,768]{2,1,0:T(8,128)(2,1)} %pad_maximum_fusion), channel_id=1, source_target_pairs={{0,1},{1,0},{2,3},{3,2},{4,5},{5,4},{6,7},{7,6},{8,9},{9,8},{10,11... | collective-permute-start | bytes 2359304 | tf_op jit(solution)/shard_map/ppermute | solution.py:64
  44.2 15.8 %collective-permute-start.10 = (bf16[4,112,768]{2,1,0:T(8,128)(2,1)}, bf16[4,112,768]{2,1,0:T(8,128)(2,1)}, u32[]{:S(2)}, u32[]{:S(2)}) collective-permute-start(bf16[4,112,768]{2,1,0:T(8,128)(2,1)} %collective-permute-done.5.first), channel_id=1, source_target_pairs={{0,4},{1,3},{2,6},{3,1},{4,0},{5,7},{6,2},{7,5},{8,12},{9,11},{10,... | collective-permute-start | bytes 2064392 | tf_op jit(solution)/shard_map/ppermute | solution.py:81
  49.5 18.5 %collective-permute-start.12 = (bf16[4,96,768]{2,1,0:T(8,128)(2,1)S(1)}, bf16[4,96,768]{2,1,0:T(8,128)(2,1)S(1)}, u32[]{:S(2)}, u32[]{:S(2)}) collective-permute-start(bf16[4,96,768]{2,1,0:T(8,128)(2,1)S(1)} %pad_maximum_fusion.2.own), channel_id=1, source_target_pairs={{0,4},{1,3},{2,6},{3,1},{4,0},{5,7},{6,2},{7,5},{8,12},{9,11},{10,... | collective-permute-start | bytes 1769480 | tf_op jit(solution)/shard_map/ppermute | solution.py:81
  53.8 15.1 %collective-permute-start.11 = (bf16[4,96,768]{2,1,0:T(8,128)(2,1)S(1)}, bf16[4,96,768]{2,1,0:T(8,128)(2,1)}, u32[]{:S(2)}, u32[]{:S(2)}) collective-permute-start(bf16[4,96,768]{2,1,0:T(8,128)(2,1)S(1)} %pad_maximum_fusion.2.own), channel_id=1, source_target_pairs={{0,2},{1,5},{2,0},{3,7},{4,6},{5,1},{6,4},{7,3},{8,10},{9,13},{10,... | collective-permute-start | bytes 1769480 | tf_op jit(solution)/shard_map/ppermute | solution.py:81
  68.8 13.8 %collective-permute-start.20 = (bf16[4,96,768]{2,1,0:T(8,128)(2,1)S(1)}, bf16[4,96,768]{2,1,0:T(8,128)(2,1)}, u32[]{:S(2)}, u32[]{:S(2)}) collective-permute-start(bf16[4,96,768]{2,1,0:T(8,128)(2,1)S(1)} %pad_maximum_fusion.3.own), channel_id=1, source_target_pairs={{0,4},{1,3},{2,6},{3,1},{4,0},{5,7},{6,2},{7,5},{8,12},{9,11},{10,... | collective-permute-start | bytes 1769480 | tf_op jit(solution)/shard_map/ppermute | solution.py:81
  69.4 16.4 %collective-permute-start.19 = (bf16[4,96,768]{2,1,0:T(8,128)(2,1)S(1)}, bf16[4,96,768]{2,1,0:T(8,128)(2,1)}, u32[]{:S(2)}, u32[]{:S(2)}) collective-permute-start(bf16[4,96,768]{2,1,0:T(8,128)(2,1)S(1)} %pad_maximum_fusion.3.own), channel_id=1, source_target_pairs={{0,2},{1,5},{2,0},{3,7},{4,6},{5,1},{6,4},{7,3},{8,10},{9,13},{10,... | collective-permute-start | bytes 1769480 | tf_op jit(solution)/shard_map/ppermute | solution.py:81
  70.9 18.0 %collective-permute-start.18 = (bf16[4,96,768]{2,1,0:T(8,128)(2,1)}, bf16[4,96,768]{2,1,0:T(8,128)(2,1)}, u32[]{:S(2)}, u32[]{:S(2)}) collective-permute-start(bf16[4,96,768]{2,1,0:T(8,128)(2,1)} %collective-permute-done.11.first), channel_id=1, source_target_pairs={{0,4},{1,3},{2,6},{3,1},{4,0},{5,7},{6,2},{7,5},{8,12},{9,11},{10,... | collective-permute-start | bytes 1769480 | tf_op jit(solution)/shard_map/ppermute | solution.py:81
  110.6 28.4 %collective-permute-start.26 = (bf16[4,96,768]{2,1,0:T(8,128)(2,1)S(1)}, bf16[4,96,768]{2,1,0:T(8,128)(2,1)S(1)}, u32[]{:S(2)}, u32[]{:S(2)}) collective-permute-start(bf16[4,96,768]{2,1,0:T(8,128)(2,1)S(1)} %get-tuple-element.130), channel_id=1, source_target_pairs={{0,2},{1,5},{2,0},{3,7},{4,6},{5,1},{6,4},{7,3},{8,10},{9,13},{10,... | collective-permute-start | bytes 1769480 | tf_op jit(solution)/shard_map/ppermute | solution.py:81
  119.1 19.9 %collective-permute-start.27 = (bf16[4,96,768]{2,1,0:T(8,128)(2,1)S(1)}, bf16[4,96,768]{2,1,0:T(8,128)(2,1)S(1)}, u32[]{:S(2)}, u32[]{:S(2)}) collective-permute-start(bf16[4,96,768]{2,1,0:T(8,128)(2,1)S(1)} %add_convert_fusion.2), channel_id=1, source_target_pairs={{0,4},{1,3},{2,6},{3,1},{4,0},{5,7},{6,2},{7,5},{8,12},{9,11},{10,... | collective-permute-start | bytes 1769480 | tf_op jit(solution)/shard_map/ppermute | solution.py:81
  120.0 17.9 %collective-permute-start.28 = (bf16[4,96,768]{2,1,0:T(8,128)(2,1)S(1)}, bf16[4,96,768]{2,1,0:T(8,128)(2,1)S(1)}, u32[]{:S(2)}, u32[]{:S(2)}) collective-permute-start(bf16[4,96,768]{2,1,0:T(8,128)(2,1)S(1)} %get-tuple-element.132), channel_id=1, source_target_pairs={{0,2},{1,5},{2,0},{3,7},{4,6},{5,1},{6,4},{7,3},{8,10},{9,13},{10,... | collective-permute-start | bytes 1769480 | tf_op jit(solution)/shard_map/ppermute | solution.py:81
  131.3 19.2 %collective-permute-start.25 = (bf16[4,112,768]{2,1,0:T(8,128)(2,1)S(1)}, bf16[4,112,768]{2,1,0:T(8,128)(2,1)S(1)}, u32[]{:S(2)}, u32[]{:S(2)}) collective-permute-start(bf16[4,112,768]{2,1,0:T(8,128)(2,1)S(1)} %get-tuple-element.127), channel_id=1, source_target_pairs={{0,2},{1,5},{2,0},{3,7},{4,6},{5,1},{6,4},{7,3},{8,10},{9,13},{10,... | collective-permute-start | bytes 2064392 | tf_op jit(solution)/shard_map/ppermute | solution.py:81
  138.1 16.3 %collective-permute-start.34 = (bf16[4,96,768]{2,1,0:T(8,128)(2,1)S(1)}, bf16[4,96,768]{2,1,0:T(8,128)(2,1)S(1)}, u32[]{:S(2)}, u32[]{:S(2)}) collective-permute-start(bf16[4,96,768]{2,1,0:T(8,128)(2,1)S(1)} %add_convert_fusion.1), channel_id=1, source_target_pairs={{0,4},{1,3},{2,6},{3,1},{4,0},{5,7},{6,2},{7,5},{8,12},{9,11},{10,... | collective-permute-start | bytes 1769480 | tf_op jit(solution)/shard_map/ppermute | solution.py:81
  139.2 18.7 %collective-permute-start.33 = (bf16[4,96,768]{2,1,0:T(8,128)(2,1)S(1)}, bf16[4,96,768]{2,1,0:T(8,128)(2,1)S(1)}, u32[]{:S(2)}, u32[]{:S(2)}) collective-permute-start(bf16[4,96,768]{2,1,0:T(8,128)(2,1)S(1)} %get-tuple-element.140), channel_id=1, source_target_pairs={{0,2},{1,5},{2,0},{3,7},{4,6},{5,1},{6,4},{7,3},{8,10},{9,13},{10,... | collective-permute-start | bytes 1769480 | tf_op jit(solution)/shard_map/ppermute | solution.py:81
  142.3 18.7 %collective-permute-start.32 = (bf16[96,768]{1,0:T(8,128)(2,1)S(1)}, bf16[96,768]{1,0:T(8,128)(2,1)S(1)}, u32[]{:S(2)}, u32[]{:S(2)}) collective-permute-start(bf16[96,768]{1,0:T(8,128)(2,1)S(1)} %get-tuple-element.169), channel_id=1, source_target_pairs={{0,24},{4,28},{8,16},{12,20},{16,8},{20,12},{24,0},{28,4},{1,25},{... | collective-permute-start | bytes 442376 | tf_op jit(solution)/shard_map/ppermute | solution.py:71
  144.7 16.9 %collective-permute-start.31 = (bf16[96,768]{1,0:T(8,128)(2,1)S(1)}, bf16[96,768]{1,0:T(8,128)(2,1)S(1)}, u32[]{:S(2)}, u32[]{:S(2)}) collective-permute-start(bf16[96,768]{1,0:T(8,128)(2,1)S(1)} %get-tuple-element.170), channel_id=1, source_target_pairs={{0,16},{4,20},{8,24},{12,28},{16,0},{20,4},{24,8},{28,12},{1,17},{... | collective-permute-start | bytes 442376 | tf_op jit(solution)/shard_map/ppermute | solution.py:71
  150.6 24.8 %collective-permute-start.40 = (bf16[512,768]{1,0:T(8,128)(2,1)S(1)}, bf16[512,768]{1,0:T(8,128)(2,1)S(1)}, u32[]{:S(2)}, u32[]{:S(2)}) collective-permute-start(bf16[512,768]{1,0:T(8,128)(2,1)S(1)} %shard_map.183), channel_id=1, source_target_pairs={{0,1},{1,0},{2,3},{3,2},{4,5},{5,4},{6,7},{7,6},{8,9},{9,8},{10,11... | collective-permute-start | bytes 2359304 | tf_op jit(solution)/shard_map/ppermute | solution.py:64
  161.0 17.1 %collective-permute-start.38 = (bf16[4,112,768]{2,1,0:T(8,128)(2,1)S(1)}, bf16[4,112,768]{2,1,0:T(8,128)(2,1)S(1)}, u32[]{:S(2)}, u32[]{:S(2)}) collective-permute-start(bf16[4,112,768]{2,1,0:T(8,128)(2,1)S(1)} %add_convert_fusion), channel_id=1, source_target_pairs={{0,4},{1,3},{2,6},{3,1},{4,0},{5,7},{6,2},{7,5},{8,12},{9,11},{10,... | collective-permute-start | bytes 2064392 | tf_op jit(solution)/shard_map/ppermute | solution.py:81
  161.7 15.7 %collective-permute-start.29 = (bf16[4,112,768]{2,1,0:T(8,128)(2,1)S(1)}, bf16[4,112,768]{2,1,0:T(8,128)(2,1)S(1)}, u32[]{:S(2)}, u32[]{:S(2)}) collective-permute-start(bf16[4,112,768]{2,1,0:T(8,128)(2,1)S(1)} %get-tuple-element.137), channel_id=1, source_target_pairs={{0,2},{1,5},{2,0},{3,7},{4,6},{5,1},{6,4},{7,3},{8,10},{9,13},{10,... | collective-permute-start | bytes 2064392 | tf_op jit(solution)/shard_map/ppermute | solution.py:81
  178.4 15.3 %collective-permute-start.44 = (bf16[112,768]{1,0:T(8,128)(2,1)S(1)}, bf16[112,768]{1,0:T(8,128)(2,1)S(1)}, u32[]{:S(2)}, u32[]{:S(2)}) collective-permute-start(bf16[112,768]{1,0:T(8,128)(2,1)S(1)} %get-tuple-element.163), channel_id=1, source_target_pairs={{0,24},{4,28},{8,16},{12,20},{16,8},{20,12},{24,0},{28,4},{1,25},{... | collective-permute-start | bytes 516104 | tf_op jit(solution)/shard_map/ppermute | solution.py:71
  (60 other events, 395.7 us)
